TPU v7x, 32 devices: a whole 2x2x4 slice. The times are simulated.
32 devices in a mesh: seq: 4 (over y, core), fsdp: 8 (over z, x).
Axes of the slice: x: 2, y: 2, z: 4, core: 2. Of those that a mesh axis runs over, the one named last changes fastest.
Arguments:
- tokens: bfloat16 [8, 1024, 2048], P('fsdp', 'seq'), may hold values from -6 to 6
- gain_attn: bfloat16 [2048], P('fsdp'), may hold values from 0.5 to 1.5
- w_qkv: bfloat16 [2048, 2560], P('fsdp'), may hold values from -0.125 to 0.125
- w_out: bfloat16 [2048, 2048], P('fsdp'), may hold values from -3 to 3
- gain_mlp: bfloat16 [2048], P('fsdp'), may hold values from 0.5 to 1.5
- w_gate_up: bfloat16 [2048, 11264], P('fsdp'), may hold values from -0.125 to 0.125
- w_down: bfloat16 [2048, 5632], P('fsdp'), may hold values from -0.078125 to 0.078125
- cotangent: bfloat16 [8, 1024, 2048], P('fsdp', 'seq'), may hold values from -6 to 6
Outputs:
- output: bfloat16 [8, 1024, 2048], P('fsdp', 'seq')
- grad_tokens: float32 [8, 1024, 2048], P('fsdp', 'seq')
- grad_w_qkv: float32 [2048, 2560], P('fsdp')
- grad_w_out: float32 [2048, 2048], P('fsdp')
- grad_w_gate_up: float32 [2048, 11264], P('fsdp')
- grad_w_down: float32 [2048, 5632], P('fsdp')
- grad_gain_attn: float32 [2048], P('fsdp')
- grad_gain_mlp: float32 [2048], P('fsdp')
All inputs are finite; a program needn't handle non-finite values.
Results may differ from a plain program's by a relative error of at most 0.02.
Values may be sent and summed in bfloat16 or wider, within the bound.
No kernel may reach another device: no remote copies, remote signals or barrier semaphores. Data moves between devices by JAX's collectives and lax.ppermute only.
A program may use at most 576 MiB of HBM per device.

v0:
```python
import jax
import jax.numpy as jnp
from jax import lax
from jax.sharding import PartitionSpec as P

H = 32
KVH = 4
HDIM = 64
FF = 5632
SEQ_LEN = 8192


epsilon = 1e-05


def from_behind(value, axis, by):
    length = lax.axis_size(axis)
    pairs = [(i, i + by) for i in range(length) if 0 <= i + by < length]
    return lax.ppermute(value, axis, pairs)


def rotate(vector, cosine_table, sine_table):
    half_width = vector.shape[-1] // 2
    turned = jnp.concatenate([-vector[..., half_width:], vector[..., :half_width]], axis=-1)
    return vector * cosine_table + turned * sine_table


def angle_table(offset, length, width):
    half_width = width // 2
    frequency = 1.0 / 10000.0 ** (jnp.arange(half_width, dtype=jnp.float32) * (2.0 / width))
    places = (offset + jnp.arange(length, dtype=jnp.int32)).astype(jnp.float32)
    angles = places[:, None] * frequency[None, :]
    angles = jnp.concatenate([angles, angles], axis=1)
    return (jnp.cos(angles)[:, None, :], jnp.sin(angles)[:, None, :])


def contract_rows(left_side, right_side):
    return lax.dot_general(
        left_side, right_side, (((0,), (0,)), ((), ())), preferred_element_type=jnp.float32
    )


def times_transposed(left_side, right_side):
    return lax.dot_general(
        left_side, right_side, (((1,), (1,)), ((), ())), preferred_element_type=jnp.float32
    )


def norm_back(grad_hat, normal, inverse):
    return inverse * (grad_hat - normal * jnp.mean(grad_hat * normal, axis=-1, keepdims=True))


def heads_to_rows(heads, length, kv_local, group_size):
    return heads.reshape(length, kv_local, group_size, HDIM).transpose(1, 2, 0, 3).reshape(-1, HDIM)


def rows_to_heads(stacked, length, kv_local, group_size):
    return (
        stacked.reshape(kv_local, group_size, length, HDIM)
        .transpose(2, 0, 1, 3)
        .reshape(length, -1)
    )


def add_columns(running, distance, column, piece):
    start = (distance, jnp.int32(0), column)
    current = lax.dynamic_slice(running, start, (1, piece.shape[0], piece.shape[1]))
    return lax.dynamic_update_slice(running, current + piece[None], start)


def local(tokens, gain_attn, w_qkv, w_out, gain_mlp, w_gate_up, w_down, cotangent):
    width_model = tokens.shape[-1]
    inputs = tokens.reshape(-1, width_model).astype(jnp.float32)
    tok_rows = inputs.shape[0]
    seq_parts = lax.axis_size("seq")
    slab = tok_rows * seq_parts
    span = SEQ_LEN // slab
    position = lax.axis_index("fsdp") % span
    width_q = H * HDIM
    width_kv = KVH * HDIM
    kv_local = KVH // seq_parts
    kv_width = kv_local * HDIM
    group_size = H // KVH
    factor = HDIM ** (-0.5)
    block_rows = min(512, slab)
    per_kv = group_size * slab // block_rows
    block_count = kv_local * per_kv
    qkv_full, out_full, gain_first, gain_second = (
        lax.all_gather(w_qkv, "fsdp", axis=0, tiled=True),
        lax.all_gather(w_out, "fsdp", axis=0, tiled=True),
        lax.all_gather(gain_attn, "fsdp", axis=0, tiled=True),
        lax.all_gather(gain_mlp, "fsdp", axis=0, tiled=True),
    )
    gain_one = gain_first.astype(jnp.float32)
    gain_two = gain_second.astype(jnp.float32)
    cosine_table, sine_table = angle_table(
        position * slab + lax.axis_index("seq") * tok_rows, tok_rows, HDIM
    )
    inverse_one = lax.rsqrt(jnp.mean(inputs * inputs, axis=-1, keepdims=True) + epsilon)
    hat_one = inputs * inverse_one
    normed_one = (hat_one * gain_one).astype(jnp.bfloat16)
    projected = jnp.dot(normed_one, qkv_full, preferred_element_type=jnp.float32)
    queries = rotate(projected[:, :width_q].reshape(tok_rows, H, HDIM), cosine_table, sine_table)
    keys = rotate(
        projected[:, width_q : width_q + width_kv].reshape(tok_rows, KVH, HDIM),
        cosine_table,
        sine_table,
    )
    queries = queries.reshape(tok_rows, width_q).astype(jnp.bfloat16)
    keys = keys.reshape(tok_rows, width_kv).astype(jnp.bfloat16)
    values = projected[:, width_q + width_kv :].astype(jnp.bfloat16)
    query_heads, key_heads, value_heads = (
        lax.all_to_all(queries, "seq", split_axis=1, concat_axis=0, tiled=True),
        lax.all_to_all(keys, "seq", split_axis=1, concat_axis=0, tiled=True),
        lax.all_to_all(values, "seq", split_axis=1, concat_axis=0, tiled=True),
    )
    query_rows = heads_to_rows(query_heads, slab, kv_local, group_size)
    kv_own = jnp.concatenate([key_heads, value_heads], axis=1)

    def pass_along(carried, unused):
        moved = from_behind(carried, "fsdp", 1)
        return (moved, moved)

    _, earlier = lax.scan(pass_along, kv_own, None, length=span - 1)
    kv_blocks = jnp.concatenate([kv_own[None], earlier], axis=0)
    local_places = jnp.arange(slab, dtype=jnp.int32)
    reach = position + 1

    def block_setup(block_index):
        kv_index = block_index // per_kv
        row_start = block_index * block_rows
        query_block = lax.dynamic_slice_in_dim(query_rows, row_start, block_rows, 0)
        query_places = position * slab + row_start % slab + jnp.arange(block_rows, dtype=jnp.int32)
        return (kv_index, row_start, query_block, query_places)

    def key_value(distance, kv_index):
        held = lax.dynamic_index_in_dim(kv_blocks, distance, 0, keepdims=False)
        key_block = lax.dynamic_slice_in_dim(held, kv_index * HDIM, HDIM, 1)
        value_block = lax.dynamic_slice_in_dim(held, kv_width + kv_index * HDIM, HDIM, 1)
        return (key_block, value_block)

    def masked_scores(query_block, query_places, key_block, distance):
        key_places = (position - distance) * slab + local_places
        scores = times_transposed(query_block, key_block) * factor
        return jnp.where(key_places[None, :] <= query_places[:, None], scores, -1e30)

    def forward_block(block_index):
        kv_index, row_start, query_block, query_places = block_setup(block_index)

        def gather_stats(distance, stats):
            row_max, row_sum = stats
            key_block, value_block = key_value(distance, kv_index)
            scores = masked_scores(query_block, query_places, key_block, distance)
            new_max = jnp.maximum(row_max, jnp.max(scores, axis=-1))
            row_sum = row_sum * jnp.exp(row_max - new_max) + jnp.sum(
                jnp.exp(scores - new_max[:, None]), axis=-1
            )
            return (new_max, row_sum)

        start_stats = (
            jnp.full((block_rows,), -1e30, jnp.float32),
            jnp.zeros((block_rows,), jnp.float32),
        )
        row_max, row_sum = lax.fori_loop(0, reach, gather_stats, start_stats)
        log_total = row_max + jnp.log(row_sum)

        def add_values(distance, total):
            key_block, value_block = key_value(distance, kv_index)
            scores = masked_scores(query_block, query_places, key_block, distance)
            probs = jnp.exp(scores - log_total[:, None]).astype(jnp.bfloat16)
            return total + jnp.dot(probs, value_block, preferred_element_type=jnp.float32)

        mixed = lax.fori_loop(0, reach, add_values, jnp.zeros((block_rows, HDIM), jnp.float32))
        return (mixed.astype(jnp.bfloat16), log_total)

    mixed_blocks, log_totals = lax.map(forward_block, jnp.arange(block_count, dtype=jnp.int32))
    mixed_heads = rows_to_heads(mixed_blocks, slab, kv_local, group_size)
    mixed_tokens = lax.all_to_all(mixed_heads, "seq", split_axis=0, concat_axis=1, tiled=True)
    middle = inputs + jnp.dot(mixed_tokens, out_full, preferred_element_type=jnp.float32)
    inverse_two = lax.rsqrt(jnp.mean(middle * middle, axis=-1, keepdims=True) + epsilon)
    hat_two = middle * inverse_two
    normed_two = (hat_two * gain_two).astype(jnp.bfloat16)
    columns = normed_two
    gate_up = jnp.dot(
        columns,
        lax.all_gather(w_gate_up, "fsdp", axis=0, tiled=True),
        preferred_element_type=jnp.float32,
    )
    gate_part = gate_up[:, :FF]
    up_part = gate_up[:, FF:]
    sigmoid_gate = jax.nn.sigmoid(gate_part)
    silu_gate = gate_part * sigmoid_gate
    hidden = (silu_gate * up_part).astype(jnp.bfloat16)
    feed = times_transposed(hidden, lax.all_gather(w_down, "fsdp", axis=0, tiled=True))
    layer_out = (middle + feed).astype(jnp.bfloat16)
    grad_feed = cotangent.reshape(-1, width_model)
    columns = grad_feed
    grad_hidden = jnp.dot(
        columns,
        lax.all_gather(w_down, "fsdp", axis=0, tiled=True),
        preferred_element_type=jnp.float32,
    )
    grad_gate = grad_hidden * up_part * sigmoid_gate * (1.0 + gate_part * (1.0 - sigmoid_gate))
    grad_up = grad_hidden * silu_gate
    grad_pre = jnp.concatenate([grad_gate, grad_up], axis=1).astype(jnp.bfloat16)
    grad_normed_two = times_transposed(
        grad_pre, lax.all_gather(w_gate_up, "fsdp", axis=0, tiled=True)
    )
    grad_middle = grad_feed.astype(jnp.float32) + norm_back(
        grad_normed_two * gain_two, hat_two, inverse_two
    )
    grad_branch = grad_middle.astype(jnp.bfloat16)
    grad_mixed = times_transposed(grad_branch, out_full).astype(jnp.bfloat16)
    grad_heads = lax.all_to_all(grad_mixed, "seq", split_axis=1, concat_axis=0, tiled=True)
    grad_rows = heads_to_rows(grad_heads, slab, kv_local, group_size)

    def backward_block(kv_running, block_index):
        kv_index, row_start, query_block, query_places = block_setup(block_index)
        grad_block = lax.dynamic_slice_in_dim(grad_rows, row_start, block_rows, 0)
        log_total = lax.dynamic_index_in_dim(log_totals, block_index, 0, keepdims=False)

        def probs_at(distance):
            key_block, value_block = key_value(distance, kv_index)
            scores = masked_scores(query_block, query_places, key_block, distance)
            probs = jnp.exp(scores - log_total[:, None])
            return (probs, key_block, value_block, times_transposed(grad_block, value_block))

        def add_inner(distance, inner):
            probs, key_block, value_block, grad_probs = probs_at(distance)
            return inner + jnp.sum(probs * grad_probs, axis=-1)

        inner = lax.fori_loop(0, reach, add_inner, jnp.zeros((block_rows,), jnp.float32))

        def add_grads(distance, carried):
            query_total, running = carried
            probs, key_block, value_block, grad_probs = probs_at(distance)
            grad_scores = (probs * (grad_probs - inner[:, None])).astype(jnp.bfloat16)
            query_total = (
                query_total
                + jnp.dot(grad_scores, key_block, preferred_element_type=jnp.float32) * factor
            )
            running = add_columns(
                running, distance, kv_index * HDIM, contract_rows(grad_scores, query_block) * factor
            )
            running = add_columns(
                running,
                distance,
                kv_width + kv_index * HDIM,
                contract_rows(probs.astype(jnp.bfloat16), grad_block),
            )
            return (query_total, running)

        query_total, kv_running = lax.fori_loop(
            0, reach, add_grads, (jnp.zeros((block_rows, HDIM), jnp.float32), kv_running)
        )
        return (kv_running, query_total.astype(jnp.bfloat16))

    kv_start = jnp.zeros((span, slab, 2 * kv_width), jnp.float32)
    kv_running, grad_query_blocks = lax.scan(
        backward_block, kv_start, jnp.arange(block_count, dtype=jnp.int32)
    )

    def bring_home(carried, distance):
        moved = from_behind(carried.astype(jnp.bfloat16), "fsdp", -1).astype(carried.dtype)
        return (moved + lax.dynamic_index_in_dim(kv_running, distance, 0, keepdims=False), None)

    home, _ = lax.scan(
        bring_home, kv_running[span - 1], jnp.arange(span - 2, -1, -1, dtype=jnp.int32)
    )
    grad_query_heads = rows_to_heads(grad_query_blocks, slab, kv_local, group_size)
    grad_key_heads = home[:, :kv_width].astype(jnp.bfloat16)
    grad_value_heads = home[:, kv_width:].astype(jnp.bfloat16)
    grad_q_tok, grad_k_tok, grad_v_tok = (
        lax.all_to_all(grad_query_heads, "seq", split_axis=0, concat_axis=1, tiled=True),
        lax.all_to_all(grad_key_heads, "seq", split_axis=0, concat_axis=1, tiled=True),
        lax.all_to_all(grad_value_heads, "seq", split_axis=0, concat_axis=1, tiled=True),
    )
    grad_q_lin = rotate(
        grad_q_tok.astype(jnp.float32).reshape(tok_rows, H, HDIM), cosine_table, -sine_table
    ).reshape(tok_rows, width_q)
    grad_k_lin = rotate(
        grad_k_tok.astype(jnp.float32).reshape(tok_rows, KVH, HDIM), cosine_table, -sine_table
    ).reshape(tok_rows, width_kv)
    grad_proj = jnp.concatenate(
        [grad_q_lin, grad_k_lin, grad_v_tok.astype(jnp.float32)], axis=1
    ).astype(jnp.bfloat16)
    grad_normed_one = times_transposed(grad_proj, qkv_full)
    grad_inputs = grad_middle + norm_back(grad_normed_one * gain_one, hat_one, inverse_one)
    owned_grads = lax.psum_scatter(
        jnp.concatenate(
            [
                contract_rows(normed_one, grad_proj),
                jnp.concatenate(
                    [
                        contract_rows(mixed_tokens, grad_branch),
                        contract_rows(normed_two, grad_pre),
                        contract_rows(grad_feed, hidden),
                    ],
                    axis=1,
                ),
            ],
            axis=1,
        ).astype(jnp.bfloat16),
        "fsdp",
        scatter_dimension=0,
        tiled=True,
    )
    summed = lax.psum(owned_grads, "seq").astype(jnp.float32)
    cols_qkv = width_q + 2 * width_kv
    weight_grad_qkv = summed[:, :cols_qkv]
    weight_grad_out = summed[:, cols_qkv : cols_qkv + width_q]
    weight_grad_gate_up = summed[:, cols_qkv + width_q : cols_qkv + width_q + 2 * FF]
    weight_grad_down = summed[:, cols_qkv + width_q + 2 * FF :]
    grad_gain_one = jnp.sum(w_qkv.astype(jnp.float32) * weight_grad_qkv, axis=1) / gain_attn.astype(
        jnp.float32
    )
    grad_gain_two = jnp.sum(
        w_gate_up.astype(jnp.float32) * weight_grad_gate_up, axis=1
    ) / gain_mlp.astype(jnp.float32)
    return (
        layer_out.reshape(tokens.shape),
        grad_inputs.reshape(tokens.shape),
        weight_grad_qkv,
        weight_grad_out,
        weight_grad_gate_up,
        weight_grad_down,
        grad_gain_one,
        grad_gain_two,
    )


def solution(mesh):
    return jax.shard_map(
        local,
        mesh=mesh,
        in_specs=(
            P("fsdp", "seq", None),
            P("fsdp"),
            P("fsdp", None),
            P("fsdp", None),
            P("fsdp"),
            P("fsdp", None),
            P("fsdp", None),
            P("fsdp", "seq", None),
        ),
        out_specs=(
            P("fsdp", "seq", None),
            P("fsdp", "seq", None),
            P("fsdp", None),
            P("fsdp", None),
            P("fsdp", None),
            P("fsdp", None),
            P("fsdp"),
            P("fsdp"),
        ),
        check_vma=False,
    )
```

profile of v0, /device:TPU:0, one launch (start us, length us, event | category | flops | bytes accessed | tf_op | source)
XLA Modules:
  0.0 4547.8 jit_solution(1803676677994864681)
XLA Ops:
  10.9 22.5 all-gather
  37.9 125.8 %all-gather.7.cloned.1.call-done = bf16[2048,2560]{1,0:T(8,128)(2,1)} async-done(((bf16[256,2560]{1,0:T(8,128)(2,1)}), bf16[2048,2560]{1,0:T(8,128)(2,1)}) %all-gather.7.cloned.1.call-update) | async-done | bytes 10485776 | tf_op jit(solution)/shard_map/all_gather | solution.py:89
  209.2 112.2 %while.158 = (s32[]{:T(128)}, bf16[1024,128]{1,0:T(8,128)(2,1)S(1)}, bf16[7,1024,128]{2,1,0:T(8,128)(2,1)}, s32[]{:T(128)}) while((s32[]{:T(128)}, bf16[1024,128]{1,0:T(8,128)(2,1)S(1)}, bf16[7,1024,128]{2,1,0:T(8,128)(2,1)}, s32[]{:T(128)}) %tuple.274), condition=%wide.region_2.3_spmd, body=%wide.region_1.2_spmd.sunk | while | flops 2 | bytes 2097257 | solution.py:124
  211.7 9.1 collective-permute-done
  225.9 11.6 collective-permute-done
  242.6 11.3 collective-permute-done
  259.1 11.1 collective-permute-done
  271.0 9.8 collective-permute-start
  286.0 9.9 collective-permute-start
  300.6 16.3 collective-permute-start
  332.6 144.0 %while.162 = (s32[]{:T(128)}, bf16[16,512,64]{1,2,0:T(8,128)(2,1)}, f32[16,512]{1,0:T(8,128)}, s32[16]{0:T(128)S(1)}, bf16[8192,64]{1,0:T(8,128)(2,1)}, /*index=...) while((s32[]{:T(128)}, bf16[16,512,64]{1,2,0:T(8,128)(2,1)}, ...), condition=%wide.region_10.11_spmd.clone.clone, body=%wide.region_3.10_spmd.clone.clone.sunk | while | flops 208736816 | bytes 6052327 | solution.py:176
  493.6 343.0 %all-gather.1 = bf16[8,1,256]{2,1,0:T(2,128)(2,1)S(1)} all-gather(bf16[1,1,256]{2,1,0:T(2,128)(2,1)S(1)} %reshape.278), channel_id=1, replica_groups=mesh['seq'=4,'fsdp'=8] {'fsdp'}, dimensions={0}, use_global_device_ids=true | all-gather | bytes 4608 | tf_op jit(solution)/shard_map/all_gather | solution.py:92
  837.2 7.6 multiply_reduce_fusion.3
  844.8 348.0 %all-gather.11.cloned.1.call-done = bf16[2048,11264]{1,0:T(8,128)(2,1)} async-done(((bf16[256,11264]{1,0:T(8,128)(2,1)}), bf16[2048,11264]{1,0:T(8,128)(2,1)}) %all-gather.11.cloned.1.call-update) | async-done | bytes 46137360 | tf_op jit(solution)/shard_map/all_gather | solution.py:186
  1192.8 25.0 fusion.100
  1217.8 420.3 %all-gather.13.cloned.1.call-done = bf16[2048,5632]{1,0:T(8,128)(2,1)} async-done(((bf16[256,5632]{1,0:T(8,128)(2,1)}), bf16[2048,5632]{1,0:T(8,128)(2,1)}) %all-gather.13.cloned.1.call-update) | async-done | bytes 23068688 | tf_op jit(solution)/shard_map/all_gather | solution.py:194
  1638.1 19.7 multiply_convert_fusion.1
  1657.8 30.3 multiply_reduce_fusion.2
  1702.6 21.4 convolution_convert_fusion
  1732.5 241.8 %while.165 = (s32[]{:T(128)}, f32[8,1024,128]{1,2,0:T(8,128)}, bf16[16,512,64]{1,2,0:T(8,128)(2,1)S(1)}, s32[16]{0:T(128)}, bf16[8192,64]{1,0:T(8,128)(2,1)}, /*...) while((s32[]{:T(128)}, f32[8,1024,128]{1,2,0:T(8,128)}, ...), condition=%wide.region_19.20_spmd.clone.clone, body=%wide.region_13.19_spmd.clone.clone.sunk | while | flops 477400128 | bytes 17558172 | solution.py:259
  1756.8 5.9 while.169
  1771.9 5.9 while.169
  1802.1 5.9 while.169
  1832.4 5.9 while.169
  1847.5 5.9 while.169
  1862.6 5.9 while.169
  1877.7 5.9 while.169
  1892.8 5.9 while.169
  1908.0 5.9 while.169
  1923.1 5.9 while.169
  1975.6 864.1 %while.159 = (s32[]{:T(128)}, bf16[1024,128]{1,0:T(8,128)(2,1)S(1)}, s32[7]{0:T(128)S(1)}, f32[8,1024,128]{1,2,0:T(8,128)}, s32[]{:T(128)}, /*index=5*/s32[]{:T(128)}, s32[]{:T(128)}) while((s32[]{:T(128)}, bf16[1024,128]{1,0:T(8,128)(2,1)S(1)}, s32[7]{0:T(128)S(1)}, f32[8,1024,128]{1,2,0:T(8,128)}, s32[]{:T(128)}, /*index=5*/s32[]{:T(128)}, ...), condition=%wide.region_21.22_spmd, body=%wide.region_20.21_spmd.sunk | while | flops 393221 | bytes 4194479 | solution.py:267
  1980.7 119.0 %collective-permute-done.1 = bf16[1024,128]{1,0:T(8,128)(2,1)S(1)} collective-permute-done((bf16[1024,128]{1,0:T(8,128)(2,1)S(1)}, bf16[1024,128]{1,0:T(8,128)(2,1)S(1)}, u32[]{:S(2)}, u32[]{:S(2)}) %collective-permute-start.1) | collective-permute-done | bytes 262176 | tf_op jit(solution)/shard_map/while/body/eval_jaxpr/ppermute | solution.py:19
  2104.9 120.4 %collective-permute-done.1 = bf16[1024,128]{1,0:T(8,128)(2,1)S(1)} collective-permute-done((bf16[1024,128]{1,0:T(8,128)(2,1)S(1)}, bf16[1024,128]{1,0:T(8,128)(2,1)S(1)}, u32[]{:S(2)}, u32[]{:S(2)}) %collective-permute-start.1) | collective-permute-done | bytes 262176 | tf_op jit(solution)/shard_map/while/body/eval_jaxpr/ppermute | solution.py:19
  2230.5 118.3 %collective-permute-done.1 = bf16[1024,128]{1,0:T(8,128)(2,1)S(1)} collective-permute-done((bf16[1024,128]{1,0:T(8,128)(2,1)S(1)}, bf16[1024,128]{1,0:T(8,128)(2,1)S(1)}, u32[]{:S(2)}, u32[]{:S(2)}) %collective-permute-start.1) | collective-permute-done | bytes 262176 | tf_op jit(solution)/shard_map/while/body/eval_jaxpr/ppermute | solution.py:19
  2354.0 119.1 %collective-permute-done.1 = bf16[1024,128]{1,0:T(8,128)(2,1)S(1)} collective-permute-done((bf16[1024,128]{1,0:T(8,128)(2,1)S(1)}, bf16[1024,128]{1,0:T(8,128)(2,1)S(1)}, u32[]{:S(2)}, u32[]{:S(2)}) %collective-permute-start.1) | collective-permute-done | bytes 262176 | tf_op jit(solution)/shard_map/while/body/eval_jaxpr/ppermute | solution.py:19
  2478.2 116.9 %collective-permute-done.1 = bf16[1024,128]{1,0:T(8,128)(2,1)S(1)} collective-permute-done((bf16[1024,128]{1,0:T(8,128)(2,1)S(1)}, bf16[1024,128]{1,0:T(8,128)(2,1)S(1)}, u32[]{:S(2)}, u32[]{:S(2)}) %collective-permute-start.1) | collective-permute-done | bytes 262176 | tf_op jit(solution)/shard_map/while/body/eval_jaxpr/ppermute | solution.py:19
  2600.3 118.2 %collective-permute-done.1 = bf16[1024,128]{1,0:T(8,128)(2,1)S(1)} collective-permute-done((bf16[1024,128]{1,0:T(8,128)(2,1)S(1)}, bf16[1024,128]{1,0:T(8,128)(2,1)S(1)}, u32[]{:S(2)}, u32[]{:S(2)}) %collective-permute-start.1) | collective-permute-done | bytes 262176 | tf_op jit(solution)/shard_map/while/body/eval_jaxpr/ppermute | solution.py:19
  2723.7 116.0 %collective-permute-done.1 = bf16[1024,128]{1,0:T(8,128)(2,1)S(1)} collective-permute-done((bf16[1024,128]{1,0:T(8,128)(2,1)S(1)}, bf16[1024,128]{1,0:T(8,128)(2,1)S(1)}, u32[]{:S(2)}, u32[]{:S(2)}) %collective-permute-start.1) | collective-permute-done | bytes 262176 | tf_op jit(solution)/shard_map/while/body/eval_jaxpr/ppermute | solution.py:19
  2845.6 12.7 convert_bitcast_fusion
  2865.3 7.0 convolution_convert_fusion.2
  2872.3 12.4 copy.113
  2895.3 6.7 convolution_convert_fusion.1
  2902.0 58.2 %pad_maximum_fusion = bf16[2048,21504]{1,0:T(8,128)(2,1)} fusion(bf16[2048,5632]{1,0:T(8,128)(2,1)} %convert_bitcast_fusion, bf16[2048,11264]{1,0:T(8,128)(2,1)} %convolution_convert_fusion, bf16[2048,2048]{1,0:T(8,128)(2,1)} %copy.113, bf16[2048,2560]{1,0:T(8,128)(2,1)} %convolution_convert_fusion.1), kind=kLoop, calls=%fused_computation.86 | loop fusion | flops 352321536 | bytes 176160768 | tf_op jit(solution)/shard_map/concatenate | solution.py:290
  2960.3 1361.4 %reduce-scatter.4.cloned.1.call-done = bf16[256,21504]{1,0:T(8,128)(2,1)} async-done(((bf16[2048,21504]{1,0:T(8,128)(2,1)}), bf16[256,21504]{1,0:T(8,128)(2,1)}) %reduce-scatter.4.cloned.1.call-update) | async-done | bytes 11010064
  4323.2 13.8 fusion.73
  4337.0 6.3 fusion.75
  4345.2 173.4 %all-reduce.3.cloned.1.call-done = bf16[256,21504]{1,0:T(8,128)(2,1)} async-done(((bf16[256,21504]{1,0:T(8,128)(2,1)}), bf16[256,21504]{1,0:T(8,128)(2,1)}) %all-reduce.3.cloned.1.call-update) | async-done | bytes 11010064 | tf_op jit(solution)/shard_map/psum | solution.py:308
  4521.7 10.4 multiply_reduce_fusion
  (882 shorter events, 543.0 us)
Async XLA Ops:
  7.2 156.6 %all-gather.7.cloned.1.call-start = ((), (), s32[]{:S(2)}) async-start(), calls=%async_computation.9 | async-start | bytes 11796480 | tf_op jit(solution)/shard_map/all_gather | solution.py:89
  7.9 829.3 %all-gather.9.cloned.1.call-start = ((), (), s32[]{:S(2)}) async-start(), calls=%async_computation.10 | async-start | bytes 9437184 | tf_op jit(solution)/shard_map/all_gather | solution.py:90
  8.6 1184.1 %all-gather.11.cloned.1.call-start = ((), (), s32[]{:S(2)}) async-start(), calls=%async_computation.11 | async-start | bytes 51904512 | tf_op jit(solution)/shard_map/all_gather | solution.py:186
  9.4 1628.7 %all-gather.13.cloned.1.call-start = ((), (), s32[]{:S(2)}) async-start(), calls=%async_computation.12 | async-start | bytes 25952256 | tf_op jit(solution)/shard_map/all_gather | solution.py:194
  10.9 152.8 %copy-start.18 = (f32[256]{0:T(256)}, f32[256]{0:T(256)S(1)}, u32[]{:S(2)}) copy-start(f32[256]{0:T(256)S(1)} %add_rsqrt_fusion.1) | copy-start | bytes 3076
  33.4 130.3 %copy-start.16 = (f32[8,1,256]{2,1,0:T(1,128)}, f32[8,1,256]{2,1,0:T(1,128)S(1)}, u32[]{:S(2)}) copy-start(f32[8,1,256]{2,1,0:T(1,128)S(1)} %convert_element_type.172) | copy-start | bytes 24580
  34.2 1.7 copy-start.11
  169.4 1.6 copy-start.6
  174.2 20.2 all-to-all-start.2
  194.4 10.2 all-to-all-start.1
  204.5 118.6 %all-to-all-start = ((bf16[256,4,512]{0,2,1:T(8,128)(2,1)}), bf16[256,4,512]{0,2,1:T(8,128)(2,1)}, u32[]{:S(2)}, u32[]{:S(2)}) async-start(bf16[256,4,512]{0,2,1:T(8,128)(2,1)} %bitcast.9), calls=%async_computation | async-start | bytes 2097152 | tf_op jit(solution)/shard_map/all_to_all | solution.py:113
  209.2 11.5 collective-permute-start
  221.5 16.0 collective-permute-start
  238.2 15.7 collective-permute-start
  254.7 15.5 collective-permute-start
  271.0 14.3 collective-permute-start
  286.0 13.8 collective-permute-start
  300.6 20.1 collective-permute-start
  487.0 6.6 copy-start.22
  489.4 347.8 %all-to-all-start.3 = ((bf16[4,256,512]{1,2,0:T(8,128)(2,1)}), bf16[4,256,512]{1,2,0:T(8,128)(2,1)}, u32[]{:S(2)}, u32[]{:S(2)}) async-start(bf16[4,256,512]{1,2,0:T(8,128)(2,1)} %copy.97), calls=%async_computation.3 | async-start | bytes 2097152 | tf_op jit(solution)/shard_map/all_to_all | solution.py:178
  1192.8 445.3 %copy-start.9 = (bf16[1,256,2048]{2,1,0:T(8,128)(2,1)S(1)}, bf16[1,256,2048]{2,1,0:T(8,128)(2,1)}, u32[]{:S(2)}) copy-start(bf16[1,256,2048]{2,1,0:T(8,128)(2,1)} %param.31) | copy-start | bytes 3145732
  1699.1 24.9 all-to-all-start.4
  1732.5 243.1 %copy-start.24 = (s32[7]{0:T(128)S(1)}, s32[7]{0:T(128)}, u32[]{:S(2)}) copy-start(s32[7]{0:T(128)} %multiply_add_fusion.2) | copy-start | bytes 88
  1975.6 124.1 %collective-permute-start.1 = (bf16[1024,128]{1,0:T(8,128)(2,1)S(1)}, bf16[1024,128]{1,0:T(8,128)(2,1)S(1)}, u32[]{:S(2)}, u32[]{:S(2)}) collective-permute-start(bf16[1024,128]{1,0:T(8,128)(2,1)S(1)} %get-tuple-element.2707), channel_id=1, source_target_pairs={{1,0},{2,1},{3,2},{4,3},{5,4},{6,5},{7,6},{9,8},{10,9},{11,10},{12... | collective-permute-start | bytes 786440 | tf_op jit(solution)/shard_map/while/body/eval_jaxpr/ppermute | solution.py:19
  2099.8 125.5 %collective-permute-start.1 = (bf16[1024,128]{1,0:T(8,128)(2,1)S(1)}, bf16[1024,128]{1,0:T(8,128)(2,1)S(1)}, u32[]{:S(2)}, u32[]{:S(2)}) collective-permute-start(bf16[1024,128]{1,0:T(8,128)(2,1)S(1)} %get-tuple-element.2707), channel_id=1, source_target_pairs={{1,0},{2,1},{3,2},{4,3},{5,4},{6,5},{7,6},{9,8},{10,9},{11,10},{12... | collective-permute-start | bytes 786440 | tf_op jit(solution)/shard_map/while/body/eval_jaxpr/ppermute | solution.py:19
  2225.4 123.4 %collective-permute-start.1 = (bf16[1024,128]{1,0:T(8,128)(2,1)S(1)}, bf16[1024,128]{1,0:T(8,128)(2,1)S(1)}, u32[]{:S(2)}, u32[]{:S(2)}) collective-permute-start(bf16[1024,128]{1,0:T(8,128)(2,1)S(1)} %get-tuple-element.2707), channel_id=1, source_target_pairs={{1,0},{2,1},{3,2},{4,3},{5,4},{6,5},{7,6},{9,8},{10,9},{11,10},{12... | collective-permute-start | bytes 786440 | tf_op jit(solution)/shard_map/while/body/eval_jaxpr/ppermute | solution.py:19
  2348.9 124.2 %collective-permute-start.1 = (bf16[1024,128]{1,0:T(8,128)(2,1)S(1)}, bf16[1024,128]{1,0:T(8,128)(2,1)S(1)}, u32[]{:S(2)}, u32[]{:S(2)}) collective-permute-start(bf16[1024,128]{1,0:T(8,128)(2,1)S(1)} %get-tuple-element.2707), channel_id=1, source_target_pairs={{1,0},{2,1},{3,2},{4,3},{5,4},{6,5},{7,6},{9,8},{10,9},{11,10},{12... | collective-permute-start | bytes 786440 | tf_op jit(solution)/shard_map/while/body/eval_jaxpr/ppermute | solution.py:19
  2473.1 122.1 %collective-permute-start.1 = (bf16[1024,128]{1,0:T(8,128)(2,1)S(1)}, bf16[1024,128]{1,0:T(8,128)(2,1)S(1)}, u32[]{:S(2)}, u32[]{:S(2)}) collective-permute-start(bf16[1024,128]{1,0:T(8,128)(2,1)S(1)} %get-tuple-element.2707), channel_id=1, source_target_pairs={{1,0},{2,1},{3,2},{4,3},{5,4},{6,5},{7,6},{9,8},{10,9},{11,10},{12... | collective-permute-start | bytes 786440 | tf_op jit(solution)/shard_map/while/body/eval_jaxpr/ppermute | solution.py:19
  2595.2 123.3 %collective-permute-start.1 = (bf16[1024,128]{1,0:T(8,128)(2,1)S(1)}, bf16[1024,128]{1,0:T(8,128)(2,1)S(1)}, u32[]{:S(2)}, u32[]{:S(2)}) collective-permute-start(bf16[1024,128]{1,0:T(8,128)(2,1)S(1)} %get-tuple-element.2707), channel_id=1, source_target_pairs={{1,0},{2,1},{3,2},{4,3},{5,4},{6,5},{7,6},{9,8},{10,9},{11,10},{12... | collective-permute-start | bytes 786440 | tf_op jit(solution)/shard_map/while/body/eval_jaxpr/ppermute | solution.py:19
  2718.6 121.1 %collective-permute-start.1 = (bf16[1024,128]{1,0:T(8,128)(2,1)S(1)}, bf16[1024,128]{1,0:T(8,128)(2,1)S(1)}, u32[]{:S(2)}, u32[]{:S(2)}) collective-permute-start(bf16[1024,128]{1,0:T(8,128)(2,1)S(1)} %get-tuple-element.2707), channel_id=1, source_target_pairs={{1,0},{2,1},{3,2},{4,3},{5,4},{6,5},{7,6},{9,8},{10,9},{11,10},{12... | collective-permute-start | bytes 786440 | tf_op jit(solution)/shard_map/while/body/eval_jaxpr/ppermute | solution.py:19
  2839.8 5.8 copy-start.10
  2841.4 20.3 all-to-all-start.6
  2860.6 4.7 copy-start.4
  2861.7 25.6 all-to-all-start.5
  2872.3 12.4 copy-start.14
  2872.3 14.1 copy-start.12
  2872.3 14.1 copy-start.15
  2887.4 7.9 all-to-all-start.7
  2890.7 1430.9 %reduce-scatter.4.cloned.1.call-start = ((), (), s32[]{:S(2)}) async-start(), calls=%async_computation.14 | async-start | bytes 99090432
  2891.3 4.0 copy-start.1
  2891.4 4.0 copy-start.17
  2891.4 3.9 copy-start.19
  2891.7 10.3 copy-start.8
  2960.2 1558.4 %all-reduce.3.cloned.1.call-start = ((), (), s32[]{:S(2)}) async-start(), calls=%async_computation.13 | async-start | bytes 22020096 | tf_op jit(solution)/shard_map/psum | solution.py:308
  4337.0 6.4 copy-start.5
  4343.4 175.2 %copy-start.7 = (bf16[256,2560]{1,0:T(8,128)(2,1)S(1)}, bf16[256,2560]{1,0:T(8,128)(2,1)}, u32[]{:S(2)}) copy-start(bf16[256,2560]{1,0:T(8,128)(2,1)} %param.26) | copy-start | bytes 3932164
  4521.7 10.4 copy-start.21
  4521.7 10.4 copy-start.23
  (5 other events, 6.4 us)
Sparse Core Ops, SparseCore 0:
  10.2 153.5 all-gather.6
  165.9 139.4 all-gather.8
  306.9 885.7 all-gather.10
  1194.2 443.8 all-gather.12
  2960.3 1361.2 reduce-scatter.3
  4324.1 194.4 all-reduce.2
where the time goes:
time: 4570 us; the launch traced here: 4550 us
  waiting for transfers between devices  3320 us (73%)
  blocking collectives  365 us (8%)
  matrix products  298 us (7%)
  local copies, waits for them, and re-layouts  197 us (4%)
  loops' own time  149 us (3%)
  other arithmetic  113 us (2%)
  starting transfers between devices  91.2 us (2%)
    unnamed x7, waiting for transfers between devices  1360 us
    ppermute x14, waiting for transfers between devices, from_behind(): return lax.ppermute(value, axis, pairs)  883 us
    all_gather x1, waiting for transfers between devices, local(): lax.all_gather(w_down, 'fsdp', axis=0, tiled=True)  420 us
    all_gather x1, waiting for transfers between devices, local(): lax.all_gather(w_gate_up, 'fsdp', axis=0, tiled=True)  348 us
    all_gather x1, blocking collectives, local(): lax.all_gather(gain_mlp, 'fsdp', axis=0, tiled=True)  343 us
    psum x1, waiting for transfers between devices, local(): summed = lax.psum(owned_grads, 'seq').astype(jnp.float32)  173 us
    all_gather x1, waiting for transfers between devices, local(): lax.all_gather(w_qkv, 'fsdp', axis=0, tiled=True)  126 us
    dot_general x36, matrix products, contract_rows(): lax.dot_general(left_side, right_side, (((0,), (0,)), ((), ())), preferre...  115 us
  transfers between devices with their start and end apart: 28, of which 20 were waited for; matrix products, arithmetic and copies ran while one was open for 6% of the time, Pallas kernels for 0%

commit v1 on v0

v1 whole, which is shorter than its diff:
```python
import functools

import jax
import jax.numpy as jnp
from jax import lax
from jax.experimental import pallas as pl
from jax.experimental.pallas import tpu as pltpu
from jax.sharding import PartitionSpec as P

H = 32
KVH = 4
HDIM = 64
FF = 5632
SEQ_LEN = 8192
GROUP = H // KVH

epsilon = 1e-05
low = jnp.bfloat16
wide = jnp.float32


def dot(left, right, left_dim, right_dim):
    return lax.dot_general(
        left, right, (((left_dim,), (right_dim,)), ((), ())), preferred_element_type=wide
    )


def head_columns(ref, chunk, per_chunk):
    return jnp.concatenate(
        [ref[h * HDIM : (h + 1) * HDIM, :] for h in range(chunk * per_chunk, (chunk + 1) * per_chunk)],
        axis=1,
    )


def causal(offset, first, key_block, tile, copies):
    key_places = offset + lax.broadcasted_iota(jnp.int32, (key_block, tile), 0)
    query_places = first + lax.broadcasted_iota(jnp.int32, (key_block, tile), 1)
    return jnp.concatenate([key_places <= query_places] * copies, axis=1)


def attend_kernel(places, q_ref, k_ref, v_ref, mixed_ref, lse_ref, max_s, sum_s, *, key_block, per_chunk):
    tile = q_ref.shape[1]
    chunks = GROUP // per_chunk
    first = places[pl.program_id(0)]
    queries = [head_columns(q_ref, c, per_chunk) for c in range(chunks)]
    max_s[...] = jnp.full(max_s.shape, -1e30, wide)
    sum_s[...] = jnp.zeros(sum_s.shape, wide)

    def step(index, masked):
        offset = pl.multiple_of(index * key_block, key_block)
        keys = k_ref[pl.ds(offset, key_block), :]
        values = v_ref[:, pl.ds(offset, key_block)]
        if masked:
            keep = causal(offset, first, key_block, tile, per_chunk)
        for c in range(chunks):
            scores = jnp.dot(keys, queries[c], preferred_element_type=wide)
            if masked:
                scores = jnp.where(keep, scores, -1e30)
            old = max_s[c]
            new = jnp.maximum(old, jnp.max(scores, axis=0, keepdims=True))
            probs = jnp.exp(scores - new).astype(low)
            max_s[c] = new
            sum_s[c] = sum_s[c] * jnp.exp(old - new) + jnp.dot(
                values, probs, preferred_element_type=wide
            )

    full = first // key_block
    lax.fori_loop(0, full, lambda i, _: (step(i, False), 0)[1], 0)
    step(full, True)
    for c in range(chunks):
        sums = sum_s[c]
        total = sums[HDIM : HDIM + 1, :]
        mixed = sums[:HDIM, :] * (1.0 / total)
        lse = max_s[c] + jnp.log(total)
        for i in range(per_chunk):
            h = c * per_chunk + i
            mixed_ref[h * HDIM : (h + 1) * HDIM, :] = mixed[:, i * tile : (i + 1) * tile]
            lse_ref[0, h : h + 1, :] = lse[:, i * tile : (i + 1) * tile]


def attend(places, queries, keys, values_ones, tile, key_block=512, per_chunk=4):
    features, tokens = queries.shape
    tiles = tokens // tile
    chunks = GROUP // per_chunk
    pairs = GROUP * tokens * keys.shape[0] // 2
    return pl.pallas_call(
        functools.partial(attend_kernel, key_block=key_block, per_chunk=per_chunk),
        grid_spec=pltpu.PrefetchScalarGridSpec(
            num_scalar_prefetch=1,
            grid=(tiles,),
            in_specs=[
                pl.BlockSpec((features, tile), lambda i, p: (0, i)),
                pl.BlockSpec(keys.shape, lambda i, p: (0, 0)),
                pl.BlockSpec(values_ones.shape, lambda i, p: (0, 0)),
            ],
            out_specs=[
                pl.BlockSpec((features, tile), lambda i, p: (0, i)),
                pl.BlockSpec((1, GROUP, tile), lambda i, p: (i, 0, 0)),
            ],
            scratch_shapes=[
                pltpu.VMEM((chunks, 1, per_chunk * tile), wide),
                pltpu.VMEM((chunks, values_ones.shape[0], per_chunk * tile), wide),
            ],
        ),
        out_shape=[
            jax.ShapeDtypeStruct((features, tokens), wide),
            jax.ShapeDtypeStruct((tiles, GROUP, tile), wide),
        ],
        compiler_params=pltpu.CompilerParams(vmem_limit_bytes=40 << 20),
        cost_estimate=pl.CostEstimate(
            flops=pairs * HDIM * 16, bytes_accessed=16 << 20, transcendentals=pairs
        ),
        name="attend",
    )(places, queries, keys, values_ones)


def attend_back_kernel(
    places, qt_ref, q_ref, gt_ref, g_ref, mixed_ref, lse_ref, k_ref, v_ref, kt_ref, gq_ref, gk_ref, gv_ref, gq_s,
    *, key_block, per_chunk,
):
    tile = qt_ref.shape[1]
    chunks = GROUP // per_chunk
    columns = per_chunk * tile
    first = places[pl.program_id(0)]

    @pl.when(pl.program_id(0) == 0)
    def _():
        gk_ref[...] = jnp.zeros(gk_ref.shape, wide)
        gv_ref[...] = jnp.zeros(gv_ref.shape, wide)

    queries = [head_columns(qt_ref, c, per_chunk) for c in range(chunks)]
    grads = [head_columns(gt_ref, c, per_chunk) for c in range(chunks)]
    inner = [
        jnp.sum(grads[c].astype(wide) * head_columns(mixed_ref, c, per_chunk), axis=0, keepdims=True)
        for c in range(chunks)
    ]
    lse = [
        jnp.concatenate([lse_ref[0, c * per_chunk + i : c * per_chunk + i + 1, :] for i in range(per_chunk)], axis=1)
        for c in range(chunks)
    ]
    gq_s[...] = jnp.zeros(gq_s.shape, wide)

    def step(index, masked):
        offset = pl.multiple_of(index * key_block, key_block)
        keys = k_ref[pl.ds(offset, key_block), :]
        values = v_ref[pl.ds(offset, key_block), :]
        keys_t = kt_ref[:, pl.ds(offset, key_block)]
        if masked:
            keep = causal(offset, first, key_block, tile, per_chunk)
        grad_k = grad_v = None
        for c in range(chunks):
            scores = jnp.dot(keys, queries[c], preferred_element_type=wide)
            if masked:
                scores = jnp.where(keep, scores, -1e30)
            probs = jnp.exp(scores - lse[c])
            grad_probs = jnp.dot(values, grads[c], preferred_element_type=wide)
            grad_scores = (probs * (grad_probs - inner[c])).astype(low)
            rows = slice(c * columns, (c + 1) * columns)
            more_k = jnp.dot(grad_scores, q_ref[0, rows, :], preferred_element_type=wide)
            more_v = jnp.dot(probs.astype(low), g_ref[0, rows, :], preferred_element_type=wide)
            gq_s[c] += jnp.dot(keys_t, grad_scores, preferred_element_type=wide)
            grad_k = more_k if grad_k is None else grad_k + more_k
            grad_v = more_v if grad_v is None else grad_v + more_v
        gk_ref[pl.ds(offset, key_block), :] += grad_k
        gv_ref[pl.ds(offset, key_block), :] += grad_v

    full = first // key_block
    lax.fori_loop(0, full, lambda i, _: (step(i, False), 0)[1], 0)
    step(full, True)
    for c in range(chunks):
        grad_q = gq_s[c] * HDIM**-0.5
        for i in range(per_chunk):
            h = c * per_chunk + i
            gq_ref[h * HDIM : (h + 1) * HDIM, :] = grad_q[:, i * tile : (i + 1) * tile]


def attend_back(places, queries_t, queries, grads_t, grads, mixed, lse, keys, values, keys_t, tile, key_block=512, per_chunk=2):
    features, tokens = queries_t.shape
    tiles = tokens // tile
    chunks = GROUP // per_chunk
    pairs = GROUP * tokens * keys.shape[0] // 2
    by_tile = pl.BlockSpec((features, tile), lambda i, p: (0, i))
    rows = pl.BlockSpec((1, GROUP * tile, HDIM), lambda i, p: (i, 0, 0))

    def whole(value):
        return pl.BlockSpec(value.shape, lambda i, p: (0, 0))

    return pl.pallas_call(
        functools.partial(attend_back_kernel, key_block=key_block, per_chunk=per_chunk),
        grid_spec=pltpu.PrefetchScalarGridSpec(
            num_scalar_prefetch=1,
            grid=(tiles,),
            in_specs=[
                by_tile,
                rows,
                by_tile,
                rows,
                by_tile,
                pl.BlockSpec((1, GROUP, tile), lambda i, p: (i, 0, 0)),
                whole(keys),
                whole(values),
                whole(keys_t),
            ],
            out_specs=[by_tile, whole(keys), whole(values)],
            scratch_shapes=[pltpu.VMEM((chunks, HDIM, per_chunk * tile), wide)],
        ),
        out_shape=[
            jax.ShapeDtypeStruct((features, tokens), wide),
            jax.ShapeDtypeStruct(keys.shape, wide),
            jax.ShapeDtypeStruct(values.shape, wide),
        ],
        compiler_params=pltpu.CompilerParams(vmem_limit_bytes=48 << 20),
        cost_estimate=pl.CostEstimate(
            flops=pairs * HDIM * 40, bytes_accessed=24 << 20, transcendentals=pairs
        ),
        name="attend_back",
    )(places, queries_t, queries, grads_t, grads, mixed, lse, keys, values, keys_t)


def from_core(value):
    return lax.ppermute(value, "seq", [(i, i ^ 1) for i in range(lax.axis_size("seq"))])


def from_chip(value):
    return lax.ppermute(value, "seq", [(i, i ^ 2) for i in range(lax.axis_size("seq"))])


def seq_gather(value):
    pair = jnp.stack([value, from_chip(value)])
    other = from_core(pair)
    return jnp.stack([pair[0], other[0], pair[1], other[1]])


def seq_sum(parts):
    sent = jnp.stack([parts[1], parts[3]]).astype(low)
    came = from_core(sent).astype(wide)
    far = (parts[2] + came[1]).astype(low)
    return parts[0] + came[0] + from_chip(far).astype(wide)


def slots_by_index(value, axis):
    own = lax.axis_index("seq")
    shape = value.shape
    split = value.reshape(shape[:axis] + (2, 2) + shape[axis + 1 :])
    split = jnp.where(own % 2 == 1, jnp.flip(split, axis + 1), split)
    split = jnp.where(own // 2 == 1, jnp.flip(split, axis), split)
    return split.reshape(shape)


def turn(vectors, cosine, sine):
    half = HDIM // 2
    first, second = vectors[:, :half], vectors[:, half:]
    return jnp.concatenate([first * cosine - second * sine, second * cosine + first * sine], axis=1)


def norm_back(grad_hat, normal, inverse):
    return inverse * (grad_hat - normal * jnp.mean(grad_hat * normal, axis=-1, keepdims=True))


def inverse_rms(values):
    return lax.rsqrt(jnp.mean(values * values, axis=-1, keepdims=True) + epsilon)


def local(tokens, gain_attn, w_qkv, w_out, gain_mlp, w_gate_up, w_down, cotangent):
    width = tokens.shape[-1]
    seq_parts = lax.axis_size("seq")
    blocks = lax.axis_size("fsdp")
    assert seq_parts == KVH == 4
    own_tokens = tokens.reshape(-1, width)
    rows = own_tokens.shape[0]
    tile = rows // 2
    slab = rows * seq_parts
    span = SEQ_LEN // slab
    seq_index = lax.axis_index("seq")
    position = lax.axis_index("fsdp") % span
    mirrored = span - 1 - position
    sequences = [list(range(i, i + span)) for i in range(0, blocks, span)]
    groups = None if span == blocks else sequences
    width_q = H * HDIM
    width_kv = KVH * HDIM
    q_part = GROUP * HDIM
    ff_part = FF // seq_parts

    def mirror(half):
        pairs = [(g[i], g[span - 1 - i]) for g in sequences for i in range(span)]
        return lax.ppermute(half, "fsdp", pairs)

    def balance(value):
        return jnp.concatenate([value[:tile], mirror(value[tile:])], axis=0)

    def part(weight, start, size):
        return lax.dynamic_slice_in_dim(weight, start + seq_index * size, size, 1)

    def fsdp_gather(value):
        return lax.all_gather(value, "fsdp", axis=0, tiled=True)

    def fsdp_sum(value):
        return lax.psum_scatter(value.astype(low), "fsdp", scatter_dimension=0, tiled=True)

    def by_rows(value):
        return value.reshape(slab, -1)

    def slots(value):
        return value.reshape(seq_parts, rows, -1)

    inputs_low = balance(own_tokens)
    grad_feed_low = balance(cotangent.reshape(-1, width))
    gains = fsdp_gather(jnp.stack([gain_attn, gain_mlp], axis=1))
    qkv_part = fsdp_gather(
        jnp.concatenate(
            [
                part(w_qkv, 0, q_part),
                part(w_qkv, width_q, HDIM),
                part(w_qkv, width_q + width_kv, HDIM),
            ],
            axis=1,
        )
    )
    out_columns = fsdp_gather(part(w_out, 0, width // seq_parts))
    out_part = lax.all_to_all(out_columns, "seq", split_axis=0, concat_axis=1, tiled=True)
    gate_up_part = fsdp_gather(
        jnp.concatenate([part(w_gate_up, 0, ff_part), part(w_gate_up, FF, ff_part)], axis=1)
    )
    down_part = fsdp_gather(part(w_down, 0, ff_part))
    gain_one = gains[:, 0].astype(wide)
    gain_two = gains[:, 1].astype(wide)

    all_inputs = by_rows(seq_gather(inputs_low)).astype(wide)
    normed_one = (all_inputs * inverse_rms(all_inputs) * gain_one).astype(low)
    projected = dot(qkv_part, normed_one, 0, 1)
    frequency = 1.0 / 10000.0 ** (jnp.arange(HDIM // 2, dtype=wide) * (2.0 / HDIM))
    row = jnp.arange(slab, dtype=jnp.int32)
    within = (row // rows ^ seq_index) * rows + row % rows
    row_places = jnp.where(row % rows < tile, position, mirrored) * slab + within
    angles = frequency[:, None] * row_places.astype(wide)[None, :]
    cosine, sine = jnp.cos(angles), jnp.sin(angles)
    places = row_places[::tile]
    queries = turn(projected[:q_part].reshape(GROUP, HDIM, slab), cosine, sine) * HDIM**-0.5
    queries = queries.reshape(q_part, slab).astype(low)
    keys_own = turn(projected[q_part : q_part + HDIM].reshape(1, HDIM, slab), cosine, sine)[0]
    kv_own = jnp.concatenate([keys_own, projected[q_part + HDIM :]], axis=0).astype(low)
    kv_own = slots_by_index(kv_own.reshape(2 * HDIM, seq_parts, 2, tile), 1)
    kv_all = lax.all_gather(kv_own, "fsdp", axis_index_groups=groups)
    kv_all = jnp.stack([kv_all[:, :, :, 0], kv_all[::-1, :, :, 1]], axis=3)
    kv_all = kv_all.transpose(1, 0, 2, 3, 4).reshape(2 * HDIM, SEQ_LEN)
    keys_t, values_t = kv_all[:HDIM], kv_all[HDIM:]
    keys, values = keys_t.T, values_t.T
    values_ones = jnp.concatenate([values_t, jnp.ones((8, SEQ_LEN), low)], axis=0)
    mixed_wide, lse = attend(places, queries, keys, values_ones, tile)
    mixed = mixed_wide.astype(low)

    inputs = inputs_low.astype(wide)
    middle = inputs + seq_sum(slots(dot(mixed, out_part, 0, 0)))
    inverse_two = inverse_rms(middle)
    hat_two = middle * inverse_two
    normed_two = by_rows(seq_gather((hat_two * gain_two).astype(low)))

    gate_up = jnp.dot(normed_two, gate_up_part, preferred_element_type=wide)
    gate, up = gate_up[:, :ff_part], gate_up[:, ff_part:]
    sigmoid = jax.nn.sigmoid(gate)
    silu = gate * sigmoid
    hidden = (silu * up).astype(low)
    feed = seq_sum(slots(dot(hidden, down_part, 1, 1)))
    layer_out = balance((middle + feed).astype(low))

    grad_feed = by_rows(seq_gather(grad_feed_low))
    grad_hidden = jnp.dot(grad_feed, down_part, preferred_element_type=wide)
    grad_gate = grad_hidden * up * sigmoid * (1.0 + gate * (1.0 - sigmoid))
    grad_pre = jnp.concatenate([grad_gate, grad_hidden * silu], axis=1).astype(low)
    grad_down = fsdp_sum(dot(grad_feed, hidden, 0, 0))
    grad_gate_up = fsdp_sum(dot(normed_two, grad_pre, 0, 0))
    grad_normed_two = seq_sum(slots(dot(grad_pre, gate_up_part, 1, 1)))
    grad_middle = grad_feed_low.astype(wide) + norm_back(
        grad_normed_two * gain_two, hat_two, inverse_two
    )
    grad_branch = by_rows(seq_gather(grad_middle.astype(low)))
    grad_out_rows = dot(mixed, grad_branch, 1, 0).astype(low)
    grad_out = fsdp_sum(lax.all_to_all(grad_out_rows, "seq", split_axis=1, concat_axis=0, tiled=True))

    grad_mixed = dot(out_part, grad_branch, 1, 1).astype(low)

    def head_rows(value):
        by_head = value.reshape(GROUP, HDIM, slab // tile, tile).transpose(2, 0, 3, 1)
        return by_head.reshape(slab // tile, GROUP * tile, HDIM)

    grad_q, grad_k, grad_v = attend_back(
        places, queries, head_rows(queries), grad_mixed, head_rows(grad_mixed),
        mixed_wide, lse, keys, values, keys_t, tile,
    )
    grad_kv = jnp.concatenate([grad_k, grad_v], axis=1).astype(low)
    grad_kv = grad_kv.reshape(span, seq_parts, 2, tile, 2 * HDIM)
    grad_kv = jnp.stack([grad_kv[:, :, 0], grad_kv[::-1, :, 1]], axis=2)
    grad_kv = lax.psum_scatter(grad_kv, "fsdp", scatter_dimension=0, axis_index_groups=groups)
    grad_kv = slots_by_index(grad_kv, 0).reshape(slab, 2 * HDIM).T.astype(wide)
    grad_q = grad_q.astype(low).astype(wide)
    grad_projected = jnp.concatenate(
        [
            turn(grad_q.reshape(GROUP, HDIM, slab), cosine, -sine).reshape(q_part, slab),
            turn(grad_kv[:HDIM].reshape(1, HDIM, slab), cosine, -sine)[0],
            grad_kv[HDIM:],
        ],
        axis=0,
    ).astype(low)
    grad_normed_one = seq_sum(slots(dot(grad_projected, qkv_part, 0, 1)))
    grad_qkv = fsdp_sum(dot(normed_one, grad_projected, 0, 1))
    inverse_one = inverse_rms(inputs)
    grad_inputs = grad_middle + norm_back(
        grad_normed_one * gain_one, inputs * inverse_one, inverse_one
    )
    grad_inputs = balance(grad_inputs)

    def columns_of(value):
        return lax.all_gather(value, "seq").astype(wide)

    def side_by_side(value, start, size):
        return value[:, :, start : start + size].transpose(1, 0, 2).reshape(value.shape[1], -1)

    down = columns_of(grad_down)
    gate_up_all = columns_of(grad_gate_up)
    out_all = columns_of(grad_out)
    qkv_all = columns_of(grad_qkv)
    weight_grad_down = side_by_side(down, 0, ff_part)
    weight_grad_gate_up = jnp.concatenate(
        [side_by_side(gate_up_all, 0, ff_part), side_by_side(gate_up_all, ff_part, ff_part)], axis=1
    )
    weight_grad_out = side_by_side(out_all, 0, width // seq_parts)
    weight_grad_qkv = jnp.concatenate(
        [
            side_by_side(qkv_all, 0, q_part),
            side_by_side(qkv_all, q_part, HDIM),
            side_by_side(qkv_all, q_part + HDIM, HDIM),
        ],
        axis=1,
    )
    grad_gain_one = jnp.sum(w_qkv.astype(wide) * weight_grad_qkv, axis=1) / gain_attn.astype(wide)
    grad_gain_two = jnp.sum(w_gate_up.astype(wide) * weight_grad_gate_up, axis=1) / gain_mlp.astype(wide)
    return (
        layer_out.reshape(tokens.shape),
        grad_inputs.reshape(tokens.shape),
        weight_grad_qkv,
        weight_grad_out,
        weight_grad_gate_up,
        weight_grad_down,
        grad_gain_one,
        grad_gain_two,
    )


def solution(mesh):
    by_token = P("fsdp", "seq", None)
    by_row = P("fsdp", None)
    return jax.shard_map(
        local,
        mesh=mesh,
        in_specs=(by_token, P("fsdp"), by_row, by_row, P("fsdp"), by_row, by_row, by_token),
        out_specs=(by_token, by_token, by_row, by_row, by_row, by_row, P("fsdp"), P("fsdp")),
        check_vma=False,
    )
```

time: 4570 us -> 1410 us (0.31)
  waiting for transfers between devices: 3320 us -> 792 us
  blocking collectives: 365 us -> 63.6 us
  Pallas kernels: 0 us -> 186 us
  matrix products: 298 us -> 127 us
  loops' own time: 149 us -> 0 us
  local copies, waits for them, and re-layouts: 197 us -> 110 us
  starting transfers between devices: 91.2 us -> 27.7 us
    unnamed x7 -> x14, waiting for transfers between devices: 1360 us -> 0.23 us
    all_gather x4 -> x9, waiting for transfers between devices: 894 us -> 105 us  [the longest x4 57.5 us: fsdp_gather(): return lax.all_gather(value, 'fsdp', axis=0, tiled=True)]
    ppermute x14 -> x20, waiting for transfers between devices: 883 us -> 230 us  [the longest x8 156 us: from_chip(): lax.ppermute(value, 'seq', [(i, i ^ 2) for i in range(lax.axis_size('seq'...]
    reduce_scatter x0 -> x5, waiting for transfers between devices: none -> 435 us  [the longest x4 417 us: fsdp_sum(): lax.psum_scatter(value.astype(low), 'fsdp', scatter_dimension=0, tiled=True)]
    all_gather x2 -> x1, blocking collectives: 365 us -> 34.7 us  [fsdp_gather(): return lax.all_gather(value, 'fsdp', axis=0, tiled=True)]
    pallas_call x0 -> x2, Pallas kernels: none -> 186 us  [the longest x1 112 us: attend_back(): pl.pallas_call(functools.partial(attend_back_kernel, key_block=key_block,...]
    psum x1 -> x0, waiting for transfers between devices: 173 us -> none  [local(): summed = lax.psum(owned_grads, 'seq').astype(jnp.float32)]
    dot_general x156 -> x12, matrix products: 298 us -> 127 us  [the longest x10 92.2 us: dot(): lax.dot_general(left, right, (((left_dim,), (right_dim,)), ((), ())), pre...]
  transfers between devices with their start and end apart: 28 -> 35, of which waited for: 20 -> 25; matrix products, arithmetic and copies ran while one was open for 6% -> 15% of each run, Pallas kernels for 0% -> 5%
where the time goes in v1:
time: 1410 us; the launch traced here: 1400 us
  waiting for transfers between devices  792 us (56%)
  Pallas kernels  186 us (13%)
  matrix products  127 us (9%)
  local copies, waits for them, and re-layouts  110 us (8%)
  other arithmetic  81.7 us (6%)
  blocking collectives  63.6 us (5%)
  starting transfers between devices  27.7 us (2%)
  between operations  15.3 us (1%)
    reduce_scatter x4, waiting for transfers between devices, fsdp_sum(): lax.psum_scatter(value.astype(low), 'fsdp', scatter_dimension=0, tiled=True)  417 us
    ppermute x8, waiting for transfers between devices, from_chip(): lax.ppermute(value, 'seq', [(i, i ^ 2) for i in range(lax.axis_size('seq'...  156 us
    pallas_call x1, Pallas kernels, attend_back(): pl.pallas_call(functools.partial(attend_back_kernel, key_block=key_block,...  112 us
    dot_general x10, matrix products, dot(): lax.dot_general(left, right, (((left_dim,), (right_dim,)), ((), ())), pre...  92.2 us
    pallas_call x1, Pallas kernels, attend(): pl.pallas_call(functools.partial(attend_kernel, key_block=key_block, per_...  73.5 us
    ppermute x4, waiting for transfers between devices, mirror(): return lax.ppermute(half, 'fsdp', pairs)  61.4 us
    all_gather x4, waiting for transfers between devices, fsdp_gather(): return lax.all_gather(value, 'fsdp', axis=0, tiled=True)  57.5 us
    all_gather x1, blocking collectives, fsdp_gather(): return lax.all_gather(value, 'fsdp', axis=0, tiled=True)  34.7 us
  transfers between devices with their start and end apart: 35, of which 25 were waited for; matrix products, arithmetic and copies ran while one was open for 15% of the time, Pallas kernels for 5%

profile of v1, /device:TPU:0, one launch (start us, length us, event | category | flops | bytes accessed | tf_op | source)
XLA Modules:
  0.0 1403.2 jit_solution(13740758296463436290)
XLA Ops:
  11.5 6.0 collective-permute-start
  17.6 16.1 %collective-permute-done = bf16[128,2048]{1,0:T(8,128)(2,1)S(1)} collective-permute-done((bf16[128,2048]{1,0:T(8,128)(2,1)S(1)}, bf16[128,2048]{1,0:T(8,128)(2,1)S(1)}, u32[]{:S(2)}, u32[]{:S(2)}) %collective-permute-start) | collective-permute-done | bytes 524320 | tf_op jit(solution)/shard_map/ppermute | solution.py:286
  35.4 21.7 %collective-permute-done.1 = bf16[256,2048]{1,0:T(8,128)(2,1)S(1)} collective-permute-done((bf16[256,2048]{1,0:T(8,128)(2,1)S(1)}, bf16[256,2048]{1,0:T(8,128)(2,1)S(1)}, u32[]{:S(2)}, u32[]{:S(2)}) %collective-permute-start.1) | collective-permute-done | bytes 1048608 | tf_op jit(solution)/shard_map/ppermute | solution.py:225
  60.6 34.7 %all_gather.43 = bf16[2048,2]{0,1:T(2,128)(2,1)S(1)} all-gather(bf16[256,2]{0,1:T(2,128)(2,1)S(1)} %pad_maximum_fusion.26), channel_id=1, replica_groups=mesh['seq'=4,'fsdp'=8] {'fsdp'}, dimensions={0}, use_global_device_ids=true | all-gather | bytes 9216 | tf_op jit(solution)/shard_map/all_gather | solution.py:295
  101.6 5.5 fusion.87
  120.9 8.1 all-gather.18.cloned.1.call-done
  128.9 4.5 all-to-all-start
  136.9 22.3 %all-to-all-done = bf16[4,512,512]{2,1,0:T(8,128)(2,1)} async-done(((bf16[4,512,512]{2,1,0:T(8,128)(2,1)}), bf16[4,512,512]{2,1,0:T(8,128)(2,1)}, u32[]{:S(2)}, u32[]{:S(2)}) %all-to-all-start) | async-done | bytes 2097184 | tf_op jit(solution)/shard_map/all_to_all | solution.py:320
  159.1 4.3 copy.49
  163.4 17.4 %all-gather.16.cloned.1.call-done = bf16[8,128,4,2,128]{4,3,2,0,1:T(2,128)(2,1)} async-done(((bf16[1,128,4,2,128]{4,3,2,0,1:T(2,128)(2,1)}), bf16[8,128,4,2,128]{4,3,2,0,1:T(2,128)(2,1)}) %all-gather.16.cloned.1.call-update) | async-done | bytes 2097168 | tf_op jit(solution)/shard_map/all_gather | solution.py:343
  180.8 7.5 fusion.79
  188.3 5.4 rev.24
  193.7 6.0 maximum_bitcast_fusion
  202.6 4.0 copy.46
  218.8 73.5 %attend.1 = (f32[512,1024]{1,0:T(8,128)S(1)}, f32[8,8,128]{2,1,0:T(8,128)S(1)}) custom-call(s32[8]{0:T(128)S(1)} %slice.272.places, bf16[512,1024]{1,0:T(8,128)(2,1)S(1)} %bitcast.224, bf16[8192,64]{1,0:T(8,128)(2,1)S(1)} %copy-done.7, bf16[72,8192]{1,0:T(8,128)(2,1)S(1)} %concatenate.75.clone.v_ref), custom_call_target="tpu_custom_call" | custom-call | flops 34359738368 | bytes 16777216 | tf_op jit(solution)/shard_map/attend/pallas_call | solution.py:86
  292.3 5.8 fusion.83
  311.2 27.0 %collective-permute-done.10 = bf16[128,2048]{1,0:T(8,128)(2,1)S(1)} collective-permute-done((bf16[128,2048]{1,0:T(8,128)(2,1)S(1)}, bf16[128,2048]{1,0:T(8,128)(2,1)S(1)}, u32[]{:S(2)}, u32[]{:S(2)}) %collective-permute-start.10) | collective-permute-done | bytes 524320 | tf_op jit(solution)/shard_map/ppermute | solution.py:286
  343.7 20.9 %collective-permute-done.11 = bf16[256,2048]{1,0:T(8,128)(2,1)S(1)} collective-permute-done((bf16[256,2048]{1,0:T(8,128)(2,1)S(1)}, bf16[256,2048]{1,0:T(8,128)(2,1)S(1)}, u32[]{:S(2)}, u32[]{:S(2)}) %collective-permute-start.11) | collective-permute-done | bytes 1048608 | tf_op jit(solution)/shard_map/ppermute | solution.py:225
  365.1 19.6 %collective-permute-done.5 = bf16[256,2048]{1,0:T(8,128)(2,1)S(1)} collective-permute-done((bf16[256,2048]{1,0:T(8,128)(2,1)S(1)}, bf16[256,2048]{1,0:T(8,128)(2,1)S(1)}, u32[]{:S(2)}, u32[]{:S(2)}) %collective-permute-start.5) | collective-permute-done | bytes 1048608 | tf_op jit(solution)/shard_map/ppermute | solution.py:225
  391.7 18.7 %fusion.88 = f32[1024,2816]{1,0:T(8,128)} fusion(bf16[1024,2048]{1,0:T(8,128)(2,1)} %bitcast.257, bf16[2048,2816]{1,0:T(8,128)(2,1)} %all-gather.20.cloned.1.call-done), kind=kOutput, calls=%fused_computation.207 | convolution fusion | flops 11811160064 | bytes 27262976 | tf_op jit(solution)/shard_map/dot_general | solution.py:358
  410.4 49.5 %all-gather.22.cloned.1.call-done = bf16[2048,1408]{1,0:T(8,128)(2,1)} async-done(((bf16[256,1408]{1,0:T(8,128)(2,1)}), bf16[2048,1408]{1,0:T(8,128)(2,1)}) %all-gather.22.cloned.1.call-update) | async-done | bytes 5767184 | tf_op jit(solution)/shard_map/all_gather | solution.py:295
  459.9 16.0 %multiply_convert_fusion.1 = (bf16[1024,1408]{1,0:T(8,128)(2,1)S(1)}, bf16[1024,1408]{1,0:T(8,128)(2,1)}, bf16[1024,1408]{1,0:T(8,128)(2,1)}) fusion(f32[1024,2816]{1,0:T(8,128)} %fusion.88, bf16[1024,2048]{1,0:T(8,128)(2,1)} %bitcast.259, bf16[2048,1408]{1,0:T(8,128)(2,1)} %all-gather.22.cloned.1.call-done), kind=kOutput, calls=%fused_computation.12 | convolution fusion | flops 5927206912 | bytes 30146560 | tf_op jit(solution)/shard_map/dot_general | solution.py:367
  475.9 19.6 %fusion.84 = (bf16[1024,2048]{1,0:T(8,128)(2,1)}, f32[1024,2048]{1,0:T(8,128)}) fusion(bf16[2048,2816]{1,0:T(8,128)(2,1)} %all-gather.20.cloned.1.call-done, bf16[1024,1408]{1,0:T(8,128)(2,1)} %get-tuple-element.33, bf16[1024,1408]{1,0:T(8,128)(2,1)S(1)} %get-tuple-element.32), kind=kOutput, calls=%fused_computation.203 | convolution fusion | flops 11824791552 | bytes 29884416 | tf_op jit(solution)/shard_map/dot_general | solution.py:23
  497.4 10.4 fusion.85
  514.8 20.6 %collective-permute-done.14 = bf16[256,2048]{1,0:T(8,128)(2,1)S(1)} collective-permute-done((bf16[256,2048]{1,0:T(8,128)(2,1)S(1)}, bf16[256,2048]{1,0:T(8,128)(2,1)S(1)}, u32[]{:S(2)}, u32[]{:S(2)}) %collective-permute-start.14) | collective-permute-done | bytes 1048608 | tf_op jit(solution)/shard_map/ppermute | solution.py:225
  536.2 21.1 %collective-permute-done.8 = bf16[256,2048]{1,0:T(8,128)(2,1)S(1)} collective-permute-done((bf16[256,2048]{1,0:T(8,128)(2,1)S(1)}, bf16[256,2048]{1,0:T(8,128)(2,1)S(1)}, u32[]{:S(2)}, u32[]{:S(2)}) %collective-permute-start.8) | collective-permute-done | bytes 1048608 | tf_op jit(solution)/shard_map/ppermute | solution.py:225
  562.1 23.0 %collective-permute-done.15 = bf16[256,2048]{1,0:T(8,128)(2,1)S(1)} collective-permute-done((bf16[256,2048]{1,0:T(8,128)(2,1)S(1)}, bf16[256,2048]{1,0:T(8,128)(2,1)S(1)}, u32[]{:S(2)}, u32[]{:S(2)}) %collective-permute-start.15) | collective-permute-done | bytes 1048608 | tf_op jit(solution)/shard_map/ppermute | solution.py:225
  602.3 112.4 %attend_back.1 = (f32[512,1024]{1,0:T(8,128)S(1)}, f32[8192,64]{1,0:T(8,128)}, f32[8192,64]{1,0:T(8,128)}) custom-call(s32[8]{0:T(128)S(1)} %slice.272.places, bf16[512,1024]{1,0:T(8,128)(2,1)S(1)} %bitcast.226, bf16[8,1024,64]{2,1,0:T(8,128)(2,1)} %bitcast.271, bf16[512,1024]{1,0:T(8,128)(2,1)S(1)} %convolution_convert_fusion.4.gt_ref, ...), custom_call_target="tpu_custom_call" | custom-call | flops 85899345920 | bytes 25165824 | tf_op jit(solution)/shard_map/attend_back/pallas_call | solution.py:188
  727.2 4.5 convolution_convert_fusion.3
  731.9 28.9 %all_to_all.38 = bf16[512,4,512]{2,0,1:T(8,128)(2,1)} all-to-all(bf16[512,4,512]{2,0,1:T(8,128)(2,1)S(1)} %bitcast.247), channel_id=1, replica_groups=mesh['seq'=4,'fsdp'=8] {'seq'}, dimensions={1} | all-to-all | bytes 4194304 | tf_op jit(solution)/shard_map/all_to_all | solution.py:378
  760.9 11.0 convolution_convert_fusion.1
  774.9 18.4 %reduce-scatter.6.cloned.1.call-done = bf16[1,4,2,128,128]{4,3,2,1,0:T(8,128)(2,1)} async-done(((bf16[8,4,2,128,128]{4,3,2,1,0:T(8,128)(2,1)}), bf16[1,4,2,128,128]{4,3,2,1,0:T(8,128)(2,1)}) %reduce-scatter.6.cloned.1.call-update) | async-done | bytes 262160 | tf_op jit(solution)/shard_map/reduce_scatter | solution.py:393
  795.8 7.2 convolution_convert_fusion.2
  803.4 18.3 %convolution_convert_fusion = bf16[2048,2816]{1,0:T(8,128)(2,1)} fusion(bf16[1024,2048]{1,0:T(8,128)(2,1)} %bitcast.258, bf16[1024,1408]{1,0:T(8,128)(2,1)} %get-tuple-element.33, bf16[1024,1408]{1,0:T(8,128)(2,1)} %copy-done.53), kind=kOutput, calls=%fused_computation.1 | convolution fusion | flops 11828461568 | bytes 21495808 | tf_op jit(solution)/shard_map/dot_general | solution.py:23
  821.8 41.7 %reduce-scatter.10.cloned.1.call-done = bf16[256,512]{1,0:T(8,128)(2,1)} async-done(((bf16[2048,512]{1,0:T(8,128)(2,1)}), bf16[256,512]{1,0:T(8,128)(2,1)}) %reduce-scatter.10.cloned.1.call-update) | async-done | bytes 262160 | tf_op jit(solution)/shard_map/reduce_scatter | solution.py:298
  863.6 113.3 %reduce-scatter.14.cloned.1.call-done = bf16[256,1408]{1,0:T(8,128)(2,1)} async-done(((bf16[2048,1408]{1,0:T(8,128)(2,1)}), bf16[256,1408]{1,0:T(8,128)(2,1)}) %reduce-scatter.14.cloned.1.call-update) | async-done | bytes 720912 | tf_op jit(solution)/shard_map/reduce_scatter | solution.py:298
  976.9 74.2 %reduce-scatter.8.cloned.1.call-done = bf16[256,640]{1,0:T(8,128)(2,1)} async-done(((bf16[2048,640]{1,0:T(8,128)(2,1)}), bf16[256,640]{1,0:T(8,128)(2,1)}) %reduce-scatter.8.cloned.1.call-update) | async-done | bytes 327696 | tf_op jit(solution)/shard_map/reduce_scatter | solution.py:298
  1051.7 7.5 fusion.86
  1059.3 187.5 %reduce-scatter.12.cloned.1.call-done = bf16[256,2816]{1,0:T(8,128)(2,1)} async-done(((bf16[2048,2816]{1,0:T(8,128)(2,1)}), bf16[256,2816]{1,0:T(8,128)(2,1)}) %reduce-scatter.12.cloned.1.call-update) | async-done | bytes 1441808 | tf_op jit(solution)/shard_map/reduce_scatter | solution.py:298
  1247.2 4.1 collective-permute-done.17
  1256.3 29.3 %collective-permute-done.18 = bf16[256,2048]{1,0:T(8,128)(2,1)S(1)} collective-permute-done((bf16[256,2048]{1,0:T(8,128)(2,1)S(1)}, bf16[256,2048]{1,0:T(8,128)(2,1)S(1)}, u32[]{:S(2)}, u32[]{:S(2)}) %collective-permute-start.18) | collective-permute-done | bytes 1048608 | tf_op jit(solution)/shard_map/ppermute | solution.py:225
  1296.3 18.4 %collective-permute-done.19 = f32[128,2048]{1,0:T(8,128)} collective-permute-done((f32[128,2048]{1,0:T(8,128)}, f32[128,2048]{1,0:T(8,128)}, u32[]{:S(2)}, u32[]{:S(2)}) %collective-permute-start.19) | collective-permute-done | bytes 1048608 | tf_op jit(solution)/shard_map/ppermute | solution.py:286
  1334.3 29.6 %all-gather.28.cloned.1.call-done = bf16[1024,2816]{1,0:T(8,128)(2,1)} async-done(((bf16[256,2816]{1,0:T(8,128)(2,1)}), bf16[1024,2816]{1,0:T(8,128)(2,1)}) %all-gather.28.cloned.1.call-update) | async-done | bytes 5767184 | tf_op jit(solution)/shard_map/all_gather | solution.py:413
  1363.9 8.0 convert.107
  1371.9 7.6 slice_bitcast_fusion
  1379.5 3.4 copy.72
  1383.7 3.3 constant_dynamic-update-slice_fusion.3
  1389.9 5.9 multiply_reduce_fusion
  (305 shorter events, 164.1 us)
Async XLA Ops:
  7.2 292.5 %copy-start = (bf16[256,5632]{1,0:T(8,128)(2,1)S(1)}, bf16[256,5632]{1,0:T(8,128)(2,1)}, u32[]{:S(2)}) copy-start(bf16[256,5632]{1,0:T(8,128)(2,1)} %param.14) | copy-start | bytes 8650756
  7.2 94.5 %all-gather.14.cloned.1.call-start = ((), (), s32[]{:S(2)}) async-start(), calls=%async_computation.7 | async-start | bytes 2949120 | tf_op jit(solution)/shard_map/all_gather | solution.py:295
  10.2 118.7 %all-gather.18.cloned.1.call-start = ((), (), s32[]{:S(2)}) async-start(), calls=%async_computation.9 | async-start | bytes 2359296 | tf_op jit(solution)/shard_map/all_gather | solution.py:295
  11.5 327.5 %copy-start.12 = (bf16[128,2048]{1,0:T(8,128)(2,1)}, bf16[128,2048]{1,0:T(8,128)(2,1)S(1)}, u32[]{:S(2)}) copy-start(bf16[128,2048]{1,0:T(8,128)(2,1)S(1)} %get-tuple-element.81) | copy-start | bytes 1572868
  11.5 22.1 %collective-permute-start = (bf16[128,2048]{1,0:T(8,128)(2,1)S(1)}, bf16[128,2048]{1,0:T(8,128)(2,1)S(1)}, u32[]{:S(2)}, u32[]{:S(2)}) collective-permute-start(bf16[128,2048]{1,0:T(8,128)(2,1)S(1)} %get-tuple-element.82), channel_id=1, source_target_pairs={{0,7},{1,6},{2,5},{3,4},{4,3},{5,2},{6,1},{7,0},{8,15},{9,14},{10,... | collective-permute-start | bytes 1572872 | tf_op jit(solution)/shard_map/ppermute | solution.py:286
  33.8 23.3 %collective-permute-start.1 = (bf16[256,2048]{1,0:T(8,128)(2,1)S(1)}, bf16[256,2048]{1,0:T(8,128)(2,1)S(1)}, u32[]{:S(2)}, u32[]{:S(2)}) collective-permute-start(bf16[256,2048]{1,0:T(8,128)(2,1)S(1)} %get-tuple-element.80), channel_id=1, source_target_pairs={{0,16},{8,24},{16,0},{24,8},{1,17},{9,25},{17,1},{25,9},{2,18},{10... | collective-permute-start | bytes 3145736 | tf_op jit(solution)/shard_map/ppermute | solution.py:225
  58.7 36.6 %collective-permute-start.2 = (bf16[2,256,2048]{2,1,0:T(8,128)(2,1)}, bf16[2,256,2048]{2,1,0:T(8,128)(2,1)}, u32[]{:S(2)}, u32[]{:S(2)}) collective-permute-start(bf16[2,256,2048]{2,1,0:T(8,128)(2,1)} %pad_maximum_fusion.7), channel_id=1, source_target_pairs={{0,8},{8,0},{16,24},{24,16},{1,9},{9,1},{17,25},{25,17},{2,10},{10... | collective-permute-start | bytes 6291464 | tf_op jit(solution)/shard_map/ppermute | solution.py:221
  60.4 120.4 %all-gather.16.cloned.1.call-start = ((), (), s32[]{:S(2)}) async-start(), calls=%async_computation.8 | async-start | bytes 2359296 | tf_op jit(solution)/shard_map/all_gather | solution.py:343
  60.5 36.6 %copy-start.11 = (bf16[1,256,2048]{2,1,0:T(8,128)(2,1)S(1)}, bf16[1,256,2048]{2,1,0:T(8,128)(2,1)}, u32[]{:S(2)}) copy-start(bf16[1,256,2048]{2,1,0:T(8,128)(2,1)} %copy-done.10) | copy-start | bytes 3145732
  60.5 36.6 %copy-start.15 = (bf16[256,2048]{1,0:T(8,128)(2,1)S(1)}, bf16[256,2048]{1,0:T(8,128)(2,1)}, u32[]{:S(2)}) copy-start(bf16[256,2048]{1,0:T(8,128)(2,1)} %copy-done.14) | copy-start | bytes 3145732
  95.3 38.2 %copy-start.46 = (f32[32]{0:T(128)}, f32[32]{0:T(128)S(1)}, u32[]{:S(2)}) copy-start(f32[32]{0:T(128)S(1)} %negate_power_fusion) | copy-start | bytes 388
  95.3 38.2 %copy-start.44 = (f32[1024]{0:T(1024)}, f32[1024]{0:T(1024)S(1)}, u32[]{:S(2)}) copy-start(f32[1024]{0:T(1024)S(1)} %fusion.66) | copy-start | bytes 12292
  118.1 273.6 %all-gather.20.cloned.1.call-start = ((), (), s32[]{:S(2)}) async-start(), calls=%async_computation.10 | async-start | bytes 12976128 | tf_op jit(solution)/shard_map/all_gather | solution.py:295
  128.9 30.2 %all-to-all-start = ((bf16[4,512,512]{2,1,0:T(8,128)(2,1)}), bf16[4,512,512]{2,1,0:T(8,128)(2,1)}, u32[]{:S(2)}, u32[]{:S(2)}) async-start(bf16[4,512,512]{2,1,0:T(8,128)(2,1)} %bitcast.273), calls=%async_computation | async-start | bytes 4194304 | tf_op jit(solution)/shard_map/all_to_all | solution.py:320
  133.4 326.5 %all-gather.22.cloned.1.call-start = ((), (), s32[]{:S(2)}) async-start(), calls=%async_computation.11 | async-start | bytes 6488064 | tf_op jit(solution)/shard_map/all_gather | solution.py:295
  218.8 73.5 %copy-start.19 = (bf16[512,4,512]{0,2,1:T(8,128)(2,1)S(1)}, bf16[512,4,512]{0,2,1:T(8,128)(2,1)}, u32[]{:S(2)}) copy-start(bf16[512,4,512]{0,2,1:T(8,128)(2,1)} %copy.49) | copy-start | bytes 6291460
  299.7 4.5 collective-permute-start.3
  300.7 492.6 %reduce-scatter.6.cloned.1.call-start = ((), (), s32[]{:S(2)}) async-start(), calls=%async_computation.12 | async-start | bytes 2359296 | tf_op jit(solution)/shard_map/reduce_scatter | solution.py:393
  308.3 30.7 %collective-permute-start.4 = (bf16[256,2048]{1,0:T(8,128)(2,1)S(1)}, bf16[256,2048]{1,0:T(8,128)(2,1)S(1)}, u32[]{:S(2)}, u32[]{:S(2)}) collective-permute-start(bf16[256,2048]{1,0:T(8,128)(2,1)S(1)} %fusion.28), channel_id=1, source_target_pairs={{0,16},{8,24},{16,0},{24,8},{1,17},{9,25},{17,1},{25,9},{2,18},{10... | collective-permute-start | bytes 3145736 | tf_op jit(solution)/shard_map/ppermute | solution.py:225
  309.9 28.2 %collective-permute-start.10 = (bf16[128,2048]{1,0:T(8,128)(2,1)S(1)}, bf16[128,2048]{1,0:T(8,128)(2,1)S(1)}, u32[]{:S(2)}, u32[]{:S(2)}) collective-permute-start(bf16[128,2048]{1,0:T(8,128)(2,1)S(1)} %get-tuple-element.76), channel_id=1, source_target_pairs={{0,7},{1,6},{2,5},{3,4},{4,3},{5,2},{6,1},{7,0},{8,15},{9,14},{10,... | collective-permute-start | bytes 1572872 | tf_op jit(solution)/shard_map/ppermute | solution.py:286
  338.4 26.2 %collective-permute-start.11 = (bf16[256,2048]{1,0:T(8,128)(2,1)S(1)}, bf16[256,2048]{1,0:T(8,128)(2,1)S(1)}, u32[]{:S(2)}, u32[]{:S(2)}) collective-permute-start(bf16[256,2048]{1,0:T(8,128)(2,1)S(1)} %get-tuple-element.74), channel_id=1, source_target_pairs={{0,16},{8,24},{16,0},{24,8},{1,17},{9,25},{17,1},{25,9},{2,18},{10... | collective-permute-start | bytes 3145736 | tf_op jit(solution)/shard_map/ppermute | solution.py:225
  342.1 42.6 %collective-permute-start.5 = (bf16[256,2048]{1,0:T(8,128)(2,1)S(1)}, bf16[256,2048]{1,0:T(8,128)(2,1)S(1)}, u32[]{:S(2)}, u32[]{:S(2)}) collective-permute-start(bf16[256,2048]{1,0:T(8,128)(2,1)S(1)} %multiply_convert_fusion.3), channel_id=1, source_target_pairs={{0,16},{8,24},{16,0},{24,8},{1,17},{9,25},{17,1},{25,9},{2,18},{10... | collective-permute-start | bytes 3145736 | tf_op jit(solution)/shard_map/ppermute | solution.py:225
  364.8 20.2 %collective-permute-start.12 = (bf16[2,256,2048]{2,1,0:T(8,128)(2,1)S(1)}, bf16[2,256,2048]{2,1,0:T(8,128)(2,1)S(1)}, u32[]{:S(2)}, u32[]{:S(2)}) collective-permute-start(bf16[2,256,2048]{2,1,0:T(8,128)(2,1)S(1)} %pad_maximum_fusion.11), channel_id=1, source_target_pairs={{0,8},{8,0},{16,24},{24,16},{1,9},{9,1},{17,25},{25,17},{2,10},{10... | collective-permute-start | bytes 6291464 | tf_op jit(solution)/shard_map/ppermute | solution.py:221
  384.9 4.2 collective-permute-start.6
  497.3 11.2 collective-permute-start.13
  508.2 4.2 collective-permute-start.7
  509.4 26.1 %collective-permute-start.14 = (bf16[256,2048]{1,0:T(8,128)(2,1)S(1)}, bf16[256,2048]{1,0:T(8,128)(2,1)S(1)}, u32[]{:S(2)}, u32[]{:S(2)}) collective-permute-start(bf16[256,2048]{1,0:T(8,128)(2,1)S(1)} %fusion.17), channel_id=1, source_target_pairs={{0,16},{8,24},{16,0},{24,8},{1,17},{9,25},{17,1},{25,9},{2,18},{10... | collective-permute-start | bytes 3145736 | tf_op jit(solution)/shard_map/ppermute | solution.py:225
  513.3 44.0 %copy-start.27 = (bf16[128,2048]{1,0:T(8,128)(2,1)S(1)}, bf16[128,2048]{1,0:T(8,128)(2,1)}, u32[]{:S(2)}) copy-start(bf16[128,2048]{1,0:T(8,128)(2,1)} %copy-done.26) | copy-start | bytes 1572868
  513.3 44.0 %copy-start.37 = (bf16[128,2048]{1,0:T(8,128)(2,1)S(1)}, bf16[128,2048]{1,0:T(8,128)(2,1)}, u32[]{:S(2)}) copy-start(bf16[128,2048]{1,0:T(8,128)(2,1)} %copy-done.36) | copy-start | bytes 1572868
  513.3 44.0 %collective-permute-start.8 = (bf16[256,2048]{1,0:T(8,128)(2,1)S(1)}, bf16[256,2048]{1,0:T(8,128)(2,1)S(1)}, u32[]{:S(2)}, u32[]{:S(2)}) collective-permute-start(bf16[256,2048]{1,0:T(8,128)(2,1)S(1)} %fusion.22), channel_id=1, source_target_pairs={{0,16},{8,24},{16,0},{24,8},{1,17},{9,25},{17,1},{25,9},{2,18},{10... | collective-permute-start | bytes 3145736 | tf_op jit(solution)/shard_map/ppermute | solution.py:225
  560.6 24.5 %collective-permute-start.15 = (bf16[256,2048]{1,0:T(8,128)(2,1)S(1)}, bf16[256,2048]{1,0:T(8,128)(2,1)S(1)}, u32[]{:S(2)}, u32[]{:S(2)}) collective-permute-start(bf16[256,2048]{1,0:T(8,128)(2,1)S(1)} %get-tuple-element.28), channel_id=1, source_target_pairs={{0,16},{8,24},{16,0},{24,8},{1,17},{9,25},{17,1},{25,9},{2,18},{10... | collective-permute-start | bytes 3145736 | tf_op jit(solution)/shard_map/ppermute | solution.py:225
  586.7 4.5 collective-permute-start.16
  727.1 136.4 %reduce-scatter.10.cloned.1.call-start = ((), (), s32[]{:S(2)}) async-start(), calls=%async_computation.14 | async-start | bytes 2359296 | tf_op jit(solution)/shard_map/reduce_scatter | solution.py:298
  760.9 216.0 %reduce-scatter.14.cloned.1.call-start = ((), (), s32[]{:S(2)}) async-start(), calls=%async_computation.16 | async-start | bytes 6488064 | tf_op jit(solution)/shard_map/reduce_scatter | solution.py:298
  771.9 279.2 %reduce-scatter.8.cloned.1.call-start = ((), (), s32[]{:S(2)}) async-start(), calls=%async_computation.13 | async-start | bytes 2949120 | tf_op jit(solution)/shard_map/reduce_scatter | solution.py:298
  803.1 443.8 %reduce-scatter.12.cloned.1.call-start = ((), (), s32[]{:S(2)}) async-start(), calls=%async_computation.15 | async-start | bytes 12976128 | tf_op jit(solution)/shard_map/reduce_scatter | solution.py:298
  821.7 468.2 %all-gather.26.cloned.1.call-start = ((), (), s32[]{:S(2)}) async-start(), calls=%async_computation.18 | async-start | bytes 1310720 | tf_op jit(solution)/shard_map/all_gather | solution.py:413
  863.5 454.0 %all-gather.30.cloned.1.call-start = ((), (), s32[]{:S(2)}) async-start(), calls=%async_computation.20 | async-start | bytes 3604480 | tf_op jit(solution)/shard_map/all_gather | solution.py:413
  976.9 346.1 %all-gather.24.cloned.1.call-start = ((), (), s32[]{:S(2)}) async-start(), calls=%async_computation.17 | async-start | bytes 1638400 | tf_op jit(solution)/shard_map/all_gather | solution.py:413
  1051.2 312.7 %all-gather.28.cloned.1.call-start = ((), (), s32[]{:S(2)}) async-start(), calls=%async_computation.19 | async-start | bytes 7208960 | tf_op jit(solution)/shard_map/all_gather | solution.py:413
  1247.1 4.2 collective-permute-start.17
  1251.9 33.7 %copy-start.13 = (bf16[128,2048]{1,0:T(8,128)(2,1)S(1)}, bf16[128,2048]{1,0:T(8,128)(2,1)}, u32[]{:S(2)}) copy-start(bf16[128,2048]{1,0:T(8,128)(2,1)} %copy-done.12) | copy-start | bytes 1572868
  1251.9 33.7 %copy-start.23 = (bf16[128,2048]{1,0:T(8,128)(2,1)S(1)}, bf16[128,2048]{1,0:T(8,128)(2,1)}, u32[]{:S(2)}) copy-start(bf16[128,2048]{1,0:T(8,128)(2,1)} %copy-done.21) | copy-start | bytes 1572868
  1251.9 33.7 %copy-start.43 = (f32[2048,1]{0,1:T(1,128)S(1)}, f32[2048,1]{0,1:T(1,128)}, u32[]{:S(2)}) copy-start(f32[2048,1]{0,1:T(1,128)} %copy-done.42) | copy-start | bytes 24580
  1252.3 33.3 %collective-permute-start.18 = (bf16[256,2048]{1,0:T(8,128)(2,1)S(1)}, bf16[256,2048]{1,0:T(8,128)(2,1)S(1)}, u32[]{:S(2)}, u32[]{:S(2)}) collective-permute-start(bf16[256,2048]{1,0:T(8,128)(2,1)S(1)} %fusion.12), channel_id=1, source_target_pairs={{0,16},{8,24},{16,0},{24,8},{1,17},{9,25},{17,1},{25,9},{2,18},{10... | collective-permute-start | bytes 3145736 | tf_op jit(solution)/shard_map/ppermute | solution.py:225
  1253.9 32.4 %copy-start.18 = (f32[256,2048]{1,0:T(8,128)S(1)}, f32[256,2048]{1,0:T(8,128)}, u32[]{:S(2)}) copy-start(f32[256,2048]{1,0:T(8,128)} %get-tuple-element.29) | copy-start | bytes 6291460
  1253.9 34.9 %collective-permute-start.9 = (bf16[128,2048]{1,0:T(8,128)(2,1)S(1)}, bf16[128,2048]{1,0:T(8,128)(2,1)S(1)}, u32[]{:S(2)}, u32[]{:S(2)}) collective-permute-start(bf16[128,2048]{1,0:T(8,128)(2,1)S(1)} %get-tuple-element.78), channel_id=1, source_target_pairs={{0,7},{1,6},{2,5},{3,4},{4,3},{5,2},{6,1},{7,0},{8,15},{9,14},{10,... | collective-permute-start | bytes 1572872 | tf_op jit(solution)/shard_map/ppermute | solution.py:286
  1288.8 25.9 %collective-permute-start.19 = (f32[128,2048]{1,0:T(8,128)}, f32[128,2048]{1,0:T(8,128)}, u32[]{:S(2)}, u32[]{:S(2)}) collective-permute-start(f32[128,2048]{1,0:T(8,128)} %get-tuple-element.54), channel_id=1, source_target_pairs={{0,7},{1,6},{2,5},{3,4},{4,3},{5,2},{6,1},{7,0},{8,15},{9,14},{10,... | collective-permute-start | bytes 3145736 | tf_op jit(solution)/shard_map/ppermute | solution.py:286
  (46 other events, 409.4 us)
Sparse Core Ops, SparseCore 0:
  10.8 67.4 all-gather.13
  81.0 47.8 all-gather.17
  131.5 49.2 all-gather.15
  182.9 183.1 all-gather.19
  368.1 91.7 all-gather.21
  727.3 65.9 reduce-scatter.5
  796.8 66.6 reduce-scatter.9
  867.7 109.0 reduce-scatter.13
  980.9 70.1 reduce-scatter.7
  1055.2 191.6 reduce-scatter.11
  1248.4 21.4 all-gather.25
  1271.4 28.7 all-gather.29
  1301.7 17.2 all-gather.23
  1320.4 43.3 all-gather.27

commit v2 on v1

v2 whole, which is shorter than its diff:
```python
import functools

import jax
import jax.numpy as jnp
from jax import lax
from jax.experimental import pallas as pl
from jax.experimental.pallas import tpu as pltpu
from jax.sharding import PartitionSpec as P

H = 32
KVH = 4
HDIM = 64
FF = 5632
SEQ_LEN = 8192
GROUP = H // KVH

epsilon = 1e-05
low = jnp.bfloat16
wide = jnp.float32


def dot(left, right, left_dim, right_dim):
    return lax.dot_general(
        left, right, (((left_dim,), (right_dim,)), ((), ())), preferred_element_type=wide
    )


def head_columns(ref, chunk, per_chunk):
    return jnp.concatenate(
        [ref[h * HDIM : (h + 1) * HDIM, :] for h in range(chunk * per_chunk, (chunk + 1) * per_chunk)],
        axis=1,
    )


def causal(offset, first, key_block, tile, copies):
    key_places = offset + lax.broadcasted_iota(jnp.int32, (key_block, tile), 0)
    query_places = first + lax.broadcasted_iota(jnp.int32, (key_block, tile), 1)
    return jnp.concatenate([key_places <= query_places] * copies, axis=1)


def each_piece(places, span, tiles, tile, visit):
    own = places[tiles]

    def one(n, _):
        block, rest = n // tiles, n % tiles
        index, half = rest // 2, rest % 2
        sender = jnp.where(half == 0, block, span - 1 - block)
        visit(
            sender,
            pl.multiple_of(((index ^ own) * 2 + half) * tile, tile),
            pl.multiple_of(n * tile, tile),
        )
        return 0

    lax.fori_loop(0, span * tiles, one, 0, unroll=8)


def unpack_kernel(places, kv_ref, keys_ref, values_ref, kt_ref, ones_ref, *, tile, tiles):
    ones_ref[HDIM:, :] = jnp.ones((8, ones_ref.shape[1]), low)

    def visit(sender, start, place):
        piece = kv_ref[sender, :, pl.ds(start, tile)]
        kt_ref[:, pl.ds(place, tile)] = piece[:HDIM]
        ones_ref[:HDIM, pl.ds(place, tile)] = piece[HDIM:]
        turned = piece.astype(wide).T.astype(low)
        keys_ref[pl.ds(place, tile), :] = turned[:, :HDIM]
        values_ref[pl.ds(place, tile), :] = turned[:, HDIM:]

    each_piece(places, kv_ref.shape[0], tiles, tile, visit)


def whole_block(shape):
    return pl.BlockSpec(shape, lambda i, p: (0,) * len(shape))


def unpack(places, kv, tile):
    span, _, slab = kv.shape
    length = span * slab
    shapes = [(length, HDIM), (length, HDIM), (HDIM, length), (HDIM + 8, length)]
    return pl.pallas_call(
        functools.partial(unpack_kernel, tile=tile, tiles=slab // tile),
        grid_spec=pltpu.PrefetchScalarGridSpec(
            num_scalar_prefetch=1,
            grid=(1,),
            in_specs=[whole_block(kv.shape)],
            out_specs=[whole_block(shape) for shape in shapes],
        ),
        out_shape=[jax.ShapeDtypeStruct(shape, low) for shape in shapes],
        compiler_params=pltpu.CompilerParams(vmem_limit_bytes=32 << 20),
        name="unpack",
    )(places, kv)


def attend_kernel(places, q_ref, keys_ref, values_ref, mixed_ref, lse_ref, max_s, sum_s, *, key_block, per_chunk, base):
    tile = q_ref.shape[1]
    chunks = GROUP // per_chunk
    first = places[pl.program_id(0) + base]
    queries = [head_columns(q_ref, c, per_chunk) for c in range(chunks)]
    max_s[...] = jnp.full(max_s.shape, -1e30, wide)
    sum_s[...] = jnp.zeros(sum_s.shape, wide)

    def step(index, masked):
        offset = pl.multiple_of(index * key_block, key_block)
        keys = keys_ref[pl.ds(offset, key_block), :]
        values = values_ref[:, pl.ds(offset, key_block)]
        if masked:
            keep = causal(offset, first, key_block, tile, per_chunk)
        for c in range(chunks):
            scores = jnp.dot(keys, queries[c], preferred_element_type=wide)
            if masked:
                scores = jnp.where(keep, scores, -1e30)
            old = max_s[c]
            new = jnp.maximum(old, jnp.max(scores, axis=0, keepdims=True))
            probs = jnp.exp(scores - new).astype(low)
            max_s[c] = new
            sum_s[c] = sum_s[c] * jnp.exp(old - new) + jnp.dot(
                values, probs, preferred_element_type=wide
            )

    full = first // key_block
    lax.fori_loop(0, full, lambda i, _: (step(i, False), 0)[1], 0)
    step(full, True)
    for c in range(chunks):
        sums = sum_s[c]
        total = sums[HDIM : HDIM + 1, :]
        mixed = sums[:HDIM, :] * (1.0 / total)
        lse = max_s[c] + jnp.log(total)
        for i in range(per_chunk):
            h = c * per_chunk + i
            mixed_ref[h * HDIM : (h + 1) * HDIM, :] = mixed[:, i * tile : (i + 1) * tile]
            lse_ref[0, h : h + 1, :] = lse[:, i * tile : (i + 1) * tile]


def attend(places, queries, keys, values_ones, tile, base, tiles, key_block=512, per_chunk=8):
    features, _ = queries.shape
    length = keys.shape[0]
    chunks = GROUP // per_chunk
    pairs = GROUP * tiles * tile * length // 2
    return pl.pallas_call(
        functools.partial(attend_kernel, key_block=key_block, per_chunk=per_chunk, base=base),
        grid_spec=pltpu.PrefetchScalarGridSpec(
            num_scalar_prefetch=1,
            grid=(tiles,),
            in_specs=[
                pl.BlockSpec((features, tile), lambda i, p: (0, i + base)),
                whole_block(keys.shape),
                whole_block(values_ones.shape),
            ],
            out_specs=[
                pl.BlockSpec((features, tile), lambda i, p: (0, i)),
                pl.BlockSpec((1, GROUP, tile), lambda i, p: (i, 0, 0)),
            ],
            scratch_shapes=[
                pltpu.VMEM((chunks, 1, per_chunk * tile), wide),
                pltpu.VMEM((chunks, HDIM + 8, per_chunk * tile), wide),
            ],
        ),
        out_shape=[
            jax.ShapeDtypeStruct((features, tiles * tile), wide),
            jax.ShapeDtypeStruct((tiles, GROUP, tile), wide),
        ],
        compiler_params=pltpu.CompilerParams(vmem_limit_bytes=40 << 20),
        cost_estimate=pl.CostEstimate(
            flops=pairs * HDIM * 16, bytes_accessed=8 << 20, transcendentals=pairs
        ),
        name="attend",
    )(places, queries, keys, values_ones)


def attend_back_kernel(places, *refs, key_block, per_chunk, base, tiles, slab, last):
    q_ref, g_ref, mixed_ref, lse_ref, keys_ref, values_ref, kt_ref = refs[:7]
    if last:
        k_before, v_before, gq_ref, gkv_ref, gq_s, gk_s, gv_s = refs[7:]
    else:
        gq_ref, gk_s, gv_s, gq_s = refs[7:]
    tile = q_ref.shape[1]
    chunks = GROUP // per_chunk
    first = places[pl.program_id(0) + base]

    @pl.when(pl.program_id(0) == 0)
    def _():
        gk_s[...] = k_before[...] if last else jnp.zeros(gk_s.shape, wide)
        gv_s[...] = v_before[...] if last else jnp.zeros(gv_s.shape, wide)

    queries = [head_columns(q_ref, c, per_chunk) for c in range(chunks)]
    grads = [head_columns(g_ref, c, per_chunk) for c in range(chunks)]
    inner = [
        jnp.sum(grads[c].astype(wide) * head_columns(mixed_ref, c, per_chunk), axis=0, keepdims=True)
        for c in range(chunks)
    ]
    lse = [
        jnp.concatenate([lse_ref[0, c * per_chunk + i : c * per_chunk + i + 1, :] for i in range(per_chunk)], axis=1)
        for c in range(chunks)
    ]
    gq_s[...] = jnp.zeros(gq_s.shape, wide)

    def step(index, masked):
        offset = pl.multiple_of(index * key_block, key_block)
        keys = keys_ref[pl.ds(offset, key_block), :]
        values = values_ref[pl.ds(offset, key_block), :]
        keys_t = kt_ref[:, pl.ds(offset, key_block)]
        if masked:
            keep = causal(offset, first, key_block, tile, per_chunk)
        grad_k = grad_v = None
        for c in range(chunks):
            scores = jnp.dot(keys, queries[c], preferred_element_type=wide)
            if masked:
                scores = jnp.where(keep, scores, -1e30)
            probs = jnp.exp(scores - lse[c])
            grad_probs = jnp.dot(values, grads[c], preferred_element_type=wide)
            grad_scores = (probs * (grad_probs - inner[c])).astype(low)
            more_k = dot(grad_scores, queries[c], 1, 1)
            more_v = dot(probs.astype(low), grads[c], 1, 1)
            gq_s[c] += jnp.dot(keys_t, grad_scores, preferred_element_type=wide)
            grad_k = more_k if grad_k is None else grad_k + more_k
            grad_v = more_v if grad_v is None else grad_v + more_v
        gk_s[pl.ds(offset, key_block), :] += grad_k
        gv_s[pl.ds(offset, key_block), :] += grad_v

    full = first // key_block
    lax.fori_loop(0, full, lambda i, _: (step(i, False), 0)[1], 0)
    step(full, True)
    for c in range(chunks):
        grad_q = gq_s[c] * HDIM**-0.5
        for i in range(per_chunk):
            h = c * per_chunk + i
            gq_ref[h * HDIM : (h + 1) * HDIM, :] = grad_q[:, i * tile : (i + 1) * tile]

    if last:

        @pl.when(pl.program_id(0) == tiles - 1)
        def _():
            def visit(sender, start, place):
                both = jnp.concatenate([gk_s[pl.ds(place, tile), :], gv_s[pl.ds(place, tile), :]], axis=1)
                gkv_ref[sender, :, pl.ds(start, tile)] = both.T.astype(low)

            each_piece(places, gkv_ref.shape[0], slab // tile, tile, visit)


def attend_back(
    places, queries, grads, mixed, lse, keys, values, keys_t, tile, base, tiles, slab, before=None,
    key_block=512, per_chunk=8,
):
    features, _ = queries.shape
    length = keys.shape[0]
    span = length // slab
    chunks = GROUP // per_chunk
    pairs = GROUP * tiles * tile * length // 2
    last = before is not None
    by_tile = pl.BlockSpec((features, tile), lambda i, p: (0, i))
    packed = (span, 2 * HDIM, slab)
    sums = [pltpu.VMEM((length, HDIM), wide)] * 2
    return pl.pallas_call(
        functools.partial(
            attend_back_kernel,
            key_block=key_block, per_chunk=per_chunk, base=base, tiles=tiles, slab=slab, last=last,
        ),
        grid_spec=pltpu.PrefetchScalarGridSpec(
            num_scalar_prefetch=1,
            grid=(tiles,),
            in_specs=[
                pl.BlockSpec((features, tile), lambda i, p: (0, i + base)),
                by_tile,
                by_tile,
                pl.BlockSpec((1, GROUP, tile), lambda i, p: (i, 0, 0)),
                whole_block(keys.shape),
                whole_block(values.shape),
                whole_block(keys_t.shape),
            ]
            + [whole_block(keys.shape)] * (2 * last),
            out_specs=[by_tile] + ([whole_block(packed)] if last else [whole_block(keys.shape)] * 2),
            scratch_shapes=[pltpu.VMEM((chunks, HDIM, per_chunk * tile), wide)] + sums * last,
        ),
        out_shape=[jax.ShapeDtypeStruct((features, tiles * tile), wide)]
        + ([jax.ShapeDtypeStruct(packed, low)] if last else [jax.ShapeDtypeStruct(keys.shape, wide)] * 2),
        compiler_params=pltpu.CompilerParams(vmem_limit_bytes=56 << 20),
        cost_estimate=pl.CostEstimate(
            flops=pairs * HDIM * 40, bytes_accessed=16 << 20, transcendentals=pairs
        ),
        name="attend_back",
    )(places, queries, grads, mixed, lse, keys, values, keys_t, *(before or ()))


def widen_kernel(own, *refs):
    out_ref = refs[-1]
    for i, ref in enumerate(refs[:-1]):

        @pl.when(pl.program_id(0) == i)
        def _(ref=ref):
            out_ref[...] = ref[...].astype(wide)


def widen(own, pieces, at=0, columns=None):
    parts = len(pieces)
    rows = pieces[0].shape[0]
    columns = columns or pieces[0].shape[1]
    return pl.pallas_call(
        widen_kernel,
        grid_spec=pltpu.PrefetchScalarGridSpec(
            num_scalar_prefetch=1,
            grid=(parts,),
            in_specs=[pl.BlockSpec((rows, columns), lambda i, own: (0, at))] * parts,
            out_specs=pl.BlockSpec((rows, columns), lambda i, own: (0, i ^ own[0])),
        ),
        out_shape=jax.ShapeDtypeStruct((rows, parts * columns), wide),
        compiler_params=pltpu.CompilerParams(vmem_limit_bytes=24 << 20),
        name="widen",
    )(own, *pieces)


def widen_pair_kernel(own, *refs):
    weight_ref, out_ref, total_ref = refs[-3:]
    step = pl.program_id(0)
    for i, ref in enumerate(refs[:-3]):

        @pl.when(step == i)
        def _(ref=ref):
            value = ref[...].astype(wide)
            out_ref[...] = value
            more = jnp.sum(value * weight_ref[...].astype(wide), axis=1, keepdims=True)
            total_ref[...] = jnp.where(step == 0, more, total_ref[...] + more)


def widen_pair(own, left, right, weight):
    parts = len(left)
    rows, columns = left[0].shape

    def place(i, own):
        return (0, i // parts * parts + (i % parts ^ own[0]))

    return pl.pallas_call(
        widen_pair_kernel,
        grid_spec=pltpu.PrefetchScalarGridSpec(
            num_scalar_prefetch=1,
            grid=(2 * parts,),
            in_specs=[pl.BlockSpec((rows, columns), lambda i, own: (0, 0))] * (2 * parts)
            + [pl.BlockSpec((rows, columns), place)],
            out_specs=[
                pl.BlockSpec((rows, columns), place),
                pl.BlockSpec((rows, 1), lambda i, own: (0, 0)),
            ],
        ),
        out_shape=[
            jax.ShapeDtypeStruct((rows, 2 * parts * columns), wide),
            jax.ShapeDtypeStruct((rows, 1), wide),
        ],
        compiler_params=pltpu.CompilerParams(vmem_limit_bytes=32 << 20),
        name="widen_pair",
    )(own, *left, *right, weight)


def widen_qkv_kernel(own, *refs, parts):
    weight_ref, out_ref, total_ref = refs[-3:]
    step = pl.program_id(0)

    def write(value):
        out_ref[...] = value
        more = jnp.sum(value * weight_ref[...].astype(wide), axis=1, keepdims=True)
        total_ref[...] = jnp.where(step == 0, more, total_ref[...] + more)

    for i, ref in enumerate(refs[:parts]):

        @pl.when(step == i)
        def _(ref=ref):
            write(ref[...].astype(wide))

    @pl.when(step == parts)
    def _():
        pieces = [ref[...].astype(wide) for ref in refs[parts : 2 * parts]]
        ordered = []
        for i in range(parts):
            value = pieces[i]
            for j in range(1, parts):
                value = jnp.where(own[0] == j, pieces[i ^ j], value)
            ordered.append(value)
        write(jnp.concatenate([v[:, :HDIM] for v in ordered] + [v[:, HDIM:] for v in ordered], axis=1))


def widen_qkv(own, queries, rest, weight):
    parts = len(queries)
    rows, columns = queries[0].shape[0], parts * 2 * HDIM

    def place(i, own):
        return (0, jnp.where(i < parts, i ^ own[0], parts))

    return pl.pallas_call(
        functools.partial(widen_qkv_kernel, parts=parts),
        grid_spec=pltpu.PrefetchScalarGridSpec(
            num_scalar_prefetch=1,
            grid=(parts + 1,),
            in_specs=[pl.BlockSpec((rows, columns), lambda i, own: (0, 0))] * parts
            + [pl.BlockSpec((rows, 2 * HDIM), lambda i, own: (0, 0))] * parts
            + [pl.BlockSpec((rows, columns), place)],
            out_specs=[
                pl.BlockSpec((rows, columns), place),
                pl.BlockSpec((rows, 1), lambda i, own: (0, 0)),
            ],
        ),
        out_shape=[
            jax.ShapeDtypeStruct((rows, (parts + 1) * columns), wide),
            jax.ShapeDtypeStruct((rows, 1), wide),
        ],
        compiler_params=pltpu.CompilerParams(vmem_limit_bytes=24 << 20),
        name="widen_qkv",
    )(own, *queries, *rest, weight)


def from_core(value):
    return lax.ppermute(value, "seq", [(i, i ^ 1) for i in range(lax.axis_size("seq"))])


def from_chip(value):
    return lax.ppermute(value, "seq", [(i, i ^ 2) for i in range(lax.axis_size("seq"))])


def seq_gather(value):
    far = from_chip(value)
    return [value, from_core(value), far, from_core(far)]


def seq_sum_core(parts):
    far = parts[2].astype(wide) + from_core(parts[3]).astype(wide)
    near = parts[0].astype(wide) + from_core(parts[1]).astype(wide)
    return near, far.astype(low)


def seq_sum(parts):
    near, far = seq_sum_core(parts)
    return near + from_chip(far).astype(wide)


def slots_by_index(value):
    own = lax.axis_index("seq")
    return [
        lax.dynamic_index_in_dim(value, own ^ j, 0, keepdims=False) for j in range(lax.axis_size("seq"))
    ]


def from_turn(value, by):
    size = lax.axis_size("fsdp")
    return lax.ppermute(value, "fsdp", [(i, (i + 2 * by) % size) for i in range(size)])


def from_pair(value):
    return lax.ppermute(value, "fsdp", [(i, i ^ 1) for i in range(lax.axis_size("fsdp"))])


def team_gather(value):
    half = value.shape[0] // 2
    beside, far = from_pair(value), from_chip(value)
    corner = jnp.concatenate([from_chip(beside[:half]), from_pair(far[half:])], axis=0)
    return [each for held in (value, far, beside, corner) for each in (held, from_core(held))]


def team_sum_core(parts):
    return [
        parts[i].astype(wide) + from_core(parts[i + 1]).astype(wide) for i in range(0, len(parts), 2)
    ]


def team_corner_hops(corner):
    half = corner.shape[0] // 2
    return from_chip(corner[:half]), from_pair(corner[half:])


def team_corner_add(sums, top, bottom):
    near, far, beside, _ = sums
    half = near.shape[0] // 2
    beside = jnp.concatenate([beside[:half] + top.astype(wide), beside[half:]], axis=0)
    far = jnp.concatenate([far[:half], far[half:] + bottom.astype(wide)], axis=0)
    return near, far.astype(low), beside.astype(low)


def team_sum(parts):
    sums = team_sum_core(parts)
    near, far, beside = team_corner_add(sums, *team_corner_hops(sums[3].astype(low)))
    return near + from_chip(far).astype(wide) + from_pair(beside).astype(wide)


def seq_swap(value):
    sent = slots_by_index(value)
    corner = from_core(sent[3])
    came = [sent[0], from_core(sent[1]), from_chip(sent[2]), from_chip(corner)]
    return slots_by_index(jnp.stack(came))


def pair_split(value):
    second = lax.axis_index("fsdp") % 2
    axis = value.ndim - 3
    return [lax.dynamic_index_in_dim(value, which, axis, keepdims=False) for which in (second, 1 - second)]


def pair_add(mine, came):
    return (mine.astype(wide) + came.astype(wide)).astype(low)


def turns_sum(pair):
    size = lax.axis_size("fsdp")
    if size != 8:
        teams = [list(range(w, size, 2)) for w in range(2)]
        return lax.psum_scatter(pair, "fsdp", scatter_dimension=0, axis_index_groups=teams)
    index = lax.axis_index("fsdp")

    def part(by):
        return lax.dynamic_index_in_dim(pair, (index // 2 + by) % (size // 2), 0, keepdims=False)

    total = part(0).astype(wide)
    for by in range(1, size // 2):
        total = total + from_turn(part(by), by).astype(wide)
    return total.astype(low)


def turn(vectors, cosine, sine):
    half = HDIM // 2
    first, second = vectors[:, :half], vectors[:, half:]
    return jnp.concatenate([first * cosine - second * sine, second * cosine + first * sine], axis=1)


def norm_back(grad_hat, normal, inverse):
    return inverse * (grad_hat - normal * jnp.mean(grad_hat * normal, axis=-1, keepdims=True))


def inverse_rms(values):
    return lax.rsqrt(jnp.mean(values * values, axis=-1, keepdims=True) + epsilon)


def local(tokens, gain_attn, w_qkv, w_out, gain_mlp, w_gate_up, w_down, cotangent):
    width = tokens.shape[-1]
    seq_parts = lax.axis_size("seq")
    blocks = lax.axis_size("fsdp")
    assert seq_parts == KVH == 4
    own_tokens = tokens.reshape(-1, width)
    rows = own_tokens.shape[0]
    tile = rows // 2
    slab = rows * seq_parts
    span = SEQ_LEN // slab
    seq_index = lax.axis_index("seq")
    position = lax.axis_index("fsdp") % span
    mirrored = span - 1 - position
    sequences = [list(range(i, i + span)) for i in range(0, blocks, span)]
    groups = None if span == blocks else sequences
    width_q = H * HDIM
    width_kv = KVH * HDIM
    q_part = GROUP * HDIM
    ff_part = FF // seq_parts
    ff_own = -(-ff_part // 256) * 128
    ff_shared = 2 * ff_own - ff_part
    second = lax.axis_index("fsdp") % 2
    teams = [list(range(w, blocks, 2)) for w in range(2)]

    def mirror(half):
        pairs = [(g[i], g[span - 1 - i]) for g in sequences for i in range(span)]
        return lax.ppermute(half, "fsdp", pairs)

    def part(weight, start, step, size=None):
        return lax.dynamic_slice_in_dim(weight, start + seq_index * step, size or step, 1)

    def sc_gather(value):
        return lax.all_gather(value, "fsdp", axis=0, tiled=True)

    def ordered(mine, other, axis):
        first = jnp.where(second == 0, mine, other)
        return jnp.concatenate([first, jnp.where(second == 0, other, mine)], axis=axis)

    def ff_rows(weight, start):
        def columns(which):
            return part(weight, start + which * (ff_own - ff_shared), ff_part, ff_own)

        return ordered(columns(second), from_pair(columns(1 - second)), 0)

    def ff_gather(value):
        return lax.all_gather(value, "fsdp", axis=0, tiled=True, axis_index_groups=teams)

    def ff_sum(value):
        return lax.psum_scatter(value, "fsdp", scatter_dimension=0, tiled=True, axis_index_groups=teams)

    def ff_split(value):
        return pair_split(value.reshape(2, -1, value.shape[1]))

    def ff_columns(mine, other):
        left = jnp.where(second == 0, mine, other)
        right = jnp.where(second == 0, other, mine)
        return jnp.concatenate([left, right[:, ff_shared:]], axis=1)

    def ff_keep(value):
        column = lax.broadcasted_iota(jnp.int32, value.shape, 1)
        return jnp.where(column >= second * ff_shared, value, 0.0).astype(low)

    def gather_halves(halves):
        near, far = (seq_gather(half) for half in halves)
        return jnp.stack([jnp.stack(pair) for pair in zip(near, far, strict=True)]).reshape(slab, width)

    def slots(value):
        return value.astype(low).reshape(-1, rows, value.shape[1])

    kept, sent = own_tokens[:tile], own_tokens[tile:]
    halves = [kept, mirror(sent)]
    inputs_low = jnp.concatenate(halves, axis=0)
    own_feed = cotangent.reshape(-1, width)

    gains = jnp.pad(jnp.stack([gain_attn, gain_mlp], axis=1), ((0, 0), (0, 126)))
    first_part = sc_gather(
        jnp.concatenate(
            [
                part(w_qkv, 0, q_part),
                part(w_qkv, width_q, HDIM),
                part(w_qkv, width_q + width_kv, HDIM),
                gains,
                part(w_out, 0, width // seq_parts),
            ],
            axis=1,
        )
    )
    out_columns = first_part[:, -(width // seq_parts) :]
    qkv_part = first_part[:, : q_part + 2 * HDIM]
    gain_one = first_part[:, q_part + 2 * HDIM].astype(wide)
    gain_two = first_part[:, q_part + 2 * HDIM + 1].astype(wide)

    all_inputs = gather_halves(halves).astype(wide)
    normed_one = lax.optimization_barrier((all_inputs * inverse_rms(all_inputs) * gain_one).astype(low))
    projected = dot(qkv_part, normed_one, 0, 1)
    frequency = 1.0 / 10000.0 ** (jnp.arange(HDIM // 2, dtype=wide) * (2.0 / HDIM))
    row = jnp.arange(slab, dtype=jnp.int32)
    within = (row // rows ^ seq_index) * rows + row % rows
    row_places = jnp.where(row % rows < tile, position, mirrored) * slab + within
    angles = frequency[:, None] * row_places.astype(wide)[None, :]
    cosine, sine = jnp.cos(angles), jnp.sin(angles)
    places = jnp.concatenate([row_places[::tile], seq_index[None].astype(jnp.int32)])
    queries = turn(projected[:q_part].reshape(GROUP, HDIM, slab), cosine, sine) * HDIM**-0.5
    queries = queries.reshape(q_part, slab).astype(low)
    keys_own = turn(projected[q_part : q_part + HDIM].reshape(1, HDIM, slab), cosine, sine)[0]
    kv_own = jnp.concatenate([keys_own, projected[q_part + HDIM :]], axis=0).astype(low)

    kv_own, own_feed, w_gate, w_up, w_down, out_columns = lax.optimization_barrier(
        (kv_own, own_feed, w_gate_up, w_gate_up, w_down, out_columns)
    )
    kv = lax.all_gather(kv_own, "fsdp", axis_index_groups=groups)
    grad_feed_low = jnp.concatenate([own_feed[:tile], mirror(own_feed[tile:])], axis=0)
    out_part = seq_swap(out_columns.reshape(seq_parts, -1, width // seq_parts))
    gate_own, up_own, down_own = ff_rows(w_gate, 0), ff_rows(w_up, FF), ff_rows(w_down, 0)
    gate_own, up_own, down_own, kv, queries, grad_feed_low, out_part = lax.optimization_barrier(
        (gate_own, up_own, down_own, kv, queries, grad_feed_low, out_part)
    )
    out_part = jnp.concatenate(out_part, axis=1)
    gate_part, up_part, down_part = ff_gather(gate_own), ff_gather(up_own), ff_gather(down_own)
    keys, values, keys_t, values_ones = unpack(places, kv, tile)

    tiles = slab // tile // 2
    feed_beside, feed_far = from_pair(grad_feed_low), from_chip(grad_feed_low)
    mixed_far, lse_far = attend(places, queries, keys, values_ones, tile, tiles, tiles)
    mixed_far, feed_beside, feed_far = lax.optimization_barrier((mixed_far, feed_beside, feed_far))
    part_two, part_three = slots(dot(mixed_far.astype(low), out_part, 0, 0))
    branch_far = (part_two.astype(wide) + from_core(part_three).astype(wide)).astype(low)
    branch_far, queries = lax.optimization_barrier((branch_far, queries))
    branch_came = from_chip(branch_far)
    feed_corner = [from_chip(feed_beside[:tile]), from_pair(feed_far[tile:])]
    mixed_near, lse_near = attend(places, queries, keys, values_ones, tile, 0, tiles)
    mixed_near, branch_came, feed_corner = lax.optimization_barrier((mixed_near, branch_came, feed_corner))
    feed_corner = jnp.concatenate(feed_corner, axis=0)
    part_zero, part_one = slots(dot(mixed_near.astype(low), out_part, 0, 0))
    inputs = inputs_low.astype(wide)
    middle = inputs + (
        part_zero.astype(wide) + from_core(part_one).astype(wide) + branch_came.astype(wide)
    )
    inverse_two = inverse_rms(middle)
    hat_two = middle * inverse_two
    normed_two = jnp.concatenate(team_gather((hat_two * gain_two).astype(low)), axis=0)
    grad_feed = jnp.concatenate(
        [each for held in (grad_feed_low, feed_far, feed_beside, feed_corner) for each in (held, from_core(held))],
        axis=0,
    )
    normed_two, grad_feed = lax.optimization_barrier((normed_two, grad_feed))

    gate = jnp.dot(normed_two, gate_part, preferred_element_type=wide)
    up = jnp.dot(normed_two, up_part, preferred_element_type=wide)
    sigmoid = jax.nn.sigmoid(gate)
    silu = gate * sigmoid
    hidden = ff_keep(silu * up)
    grad_hidden = jnp.dot(grad_feed, down_part, preferred_element_type=wide)
    grad_gate = ff_keep(grad_hidden * up * sigmoid * (1.0 + gate * (1.0 - sigmoid)))
    grad_up = ff_keep(grad_hidden * silu)
    product_two = (dot(grad_gate, gate_part, 1, 1) + dot(grad_up, up_part, 1, 1)).astype(low)
    product_two, hidden, grad_gate, grad_up = lax.optimization_barrier(
        (product_two, hidden, grad_gate, grad_up)
    )
    local_down = dot(grad_feed, hidden, 0, 0).astype(low)
    local_gate = dot(normed_two, grad_gate, 0, 0).astype(low)
    local_up = dot(normed_two, grad_up, 0, 0).astype(low)
    feed_sums = team_sum_core(slots(dot(hidden, down_part, 1, 1)))
    grad_normed_two = team_sum(slots(product_two))
    grad_middle = grad_feed_low.astype(wide) + norm_back(
        grad_normed_two * gain_two, hat_two, inverse_two
    )
    sum_down = ff_sum(local_down)
    branch_low, feed_sums, sum_down, local_gate, local_up = lax.optimization_barrier(
        (grad_middle.astype(low), feed_sums, sum_down, local_gate, local_up)
    )
    sum_gate, sum_up = ff_sum(local_gate), ff_sum(local_up)

    back_near = jnp.concatenate([branch_low, from_core(branch_low)], axis=0)
    grads_near = dot(out_part, back_near, 1, 1).astype(low)
    back_come = from_chip(branch_low)
    feed_hops = team_corner_hops(feed_sums[3].astype(low))
    mine_down, theirs = ff_split(sum_down)
    other_down = from_pair(theirs)
    grad_q_near, grad_k, grad_v = attend_back(
        places, queries, grads_near, mixed_near, lse_near, keys, values, keys_t, tile, 0, tiles, slab
    )
    grad_q_near, grad_k, grad_v, back_come, feed_hops, other_down, sum_gate = lax.optimization_barrier(
        (grad_q_near, grad_k, grad_v, back_come, feed_hops, other_down, sum_gate)
    )
    feed_near, feed_far, feed_beside = team_corner_add(feed_sums, *feed_hops)
    own_down = ff_columns(mine_down, other_down)
    mine_gate, theirs_gate = ff_split(sum_gate)
    back_far = jnp.concatenate([back_come, from_core(back_come)], axis=0)
    grads_far = dot(out_part, back_far, 1, 1).astype(low)
    local_out = (
        dot(mixed_near.astype(low), back_near, 1, 0) + dot(mixed_far.astype(low), back_far, 1, 0)
    ).astype(low)
    mine_out, theirs_out = pair_split(local_out.reshape(blocks // 8, 2, -1, width))
    grads_far, theirs_out, feed_far, feed_beside, own_down, theirs_gate = lax.optimization_barrier(
        (grads_far, theirs_out, feed_far, feed_beside, own_down, theirs_gate)
    )
    other_out = from_pair(theirs_out)
    feed_far, feed_beside = from_chip(feed_far), from_pair(feed_beside)
    far_down = from_chip(own_down)
    other_gate = from_pair(theirs_gate)
    grad_q_far, grad_kv = attend_back(
        places, queries, grads_far, mixed_far, lse_far, keys, values, keys_t, tile, tiles, tiles, slab,
        before=(grad_k, grad_v),
    )
    grad_q_far, grad_kv, feed_far, feed_beside, far_down, other_gate, other_out, sum_up = lax.optimization_barrier(
        (grad_q_far, grad_kv, feed_far, feed_beside, far_down, other_gate, other_out, sum_up)
    )
    layer_out = (middle + feed_near + feed_far.astype(wide) + feed_beside.astype(wide)).astype(low)
    out_pair = pair_add(mine_out, other_out).reshape(-1, seq_parts, width // seq_parts)

    grad_kv = lax.psum_scatter(grad_kv, "fsdp", scatter_dimension=0, axis_index_groups=groups)
    grad_q = jnp.concatenate([grad_q_near, grad_q_far], axis=1).astype(low).astype(wide)
    grad_q = turn(grad_q.reshape(GROUP, HDIM, slab), cosine, -sine).reshape(q_part, slab).astype(low)
    mine_q, theirs = pair_split(dot(normed_one, grad_q, 0, 1).astype(low).reshape(blocks // 2, 2, -1, q_part))
    other_q = from_pair(theirs)
    out_swapped = seq_swap(out_pair.transpose(1, 0, 2))
    mirrored_out = mirror(layer_out[tile:])
    down_all = [own_down, from_core(own_down), far_down, from_core(far_down)]
    gate_all = seq_gather(ff_columns(mine_gate, other_gate))
    mine, theirs = ff_split(sum_up)
    up_all = seq_gather(ff_columns(mine, from_pair(theirs)))
    grad_kv, other_q, out_swapped, down_all, gate_all, up_all, mirrored_out = lax.optimization_barrier(
        (grad_kv, other_q, out_swapped, down_all, gate_all, up_all, mirrored_out)
    )
    layer_out = jnp.concatenate([layer_out[:tile], mirrored_out], axis=0)
    grad_q_out_own = ff_sum(
        jnp.concatenate(
            [pair_add(mine_q, other_q).reshape(-1, q_part), jnp.concatenate(out_swapped, axis=0)], axis=1
        )
    )
    grad_k = turn(grad_kv[:HDIM].astype(wide).reshape(1, HDIM, slab), cosine, -sine)[0].astype(low)
    grad_kv = jnp.concatenate([grad_k, grad_kv[HDIM:]], axis=0)
    grad_projected = jnp.concatenate([grad_q, grad_kv], axis=0)
    part_two, part_three = slots(dot(grad_projected[:, slab // 2 :], qkv_part, 0, 1))
    far_one = (part_two.astype(wide) + from_core(part_three).astype(wide)).astype(low)
    far_one, grad_projected, grad_kv = lax.optimization_barrier((far_one, grad_projected, grad_kv))
    came_one = from_chip(far_one)
    part_zero, part_one = slots(dot(grad_projected[:, : slab // 2], qkv_part, 0, 1))
    mine_kv, theirs = pair_split(
        dot(normed_one, grad_kv, 0, 1).astype(low).reshape(blocks // 2, 2, -1, 2 * HDIM)
    )
    other_kv = from_pair(theirs)
    near_one = part_zero.astype(wide) + from_core(part_one).astype(wide)
    near_one, came_one, other_kv = lax.optimization_barrier((near_one, came_one, other_kv))

    grad_normed_one = near_one + came_one.astype(wide)
    inverse_one = inverse_rms(inputs)
    grad_inputs = grad_middle + norm_back(
        grad_normed_one * gain_one, inputs * inverse_one, inverse_one
    )
    grad_inputs, kv_pair = lax.optimization_barrier((grad_inputs, pair_add(mine_kv, other_kv)))
    back = mirror(grad_inputs[tile:].astype(low))
    grad_kv_own = turns_sum(kv_pair)
    own = seq_index[None].astype(jnp.int32)
    weight_grad_gate_up, sums_two = widen_pair(own, gate_all, up_all, w_gate_up)
    weight_grad_down = widen(own, down_all)
    q_out_all = seq_gather(grad_q_out_own)
    back, grad_kv_own, q_out_all, weight_grad_down = lax.optimization_barrier(
        (back, grad_kv_own, q_out_all, weight_grad_down)
    )
    grad_inputs = jnp.concatenate([grad_inputs[:tile], back.astype(wide)], axis=0)

    weight_grad_out = widen(own, q_out_all, 1, width // seq_parts)
    weight_grad_qkv, sums_one = widen_qkv(own, q_out_all, seq_gather(grad_kv_own), w_qkv)
    grad_gain_one = sums_one[:, 0] / gain_attn.astype(wide)
    grad_gain_two = sums_two[:, 0] / gain_mlp.astype(wide)
    return (
        layer_out.reshape(tokens.shape),
        grad_inputs.reshape(tokens.shape),
        weight_grad_qkv,
        weight_grad_out,
        weight_grad_gate_up,
        weight_grad_down,
        grad_gain_one,
        grad_gain_two,
    )


def solution(mesh):
    by_token = P("fsdp", "seq", None)
    by_row = P("fsdp", None)
    return jax.shard_map(
        local,
        mesh=mesh,
        in_specs=(by_token, P("fsdp"), by_row, by_row, P("fsdp"), by_row, by_row, by_token),
        out_specs=(by_token, by_token, by_row, by_row, by_row, by_row, P("fsdp"), P("fsdp")),
        check_vma=False,
    )
```

time: 1410 us -> 889 us (0.63)
  waiting for transfers between devices: 792 us -> 277 us
  blocking collectives: 63.6 us -> 0 us
  starting transfers between devices: 27.7 us -> 72.5 us
  local copies, waits for them, and re-layouts: 110 us -> 87.7 us
  Pallas kernels: 186 us -> 205 us
    reduce_scatter x4, waiting for transfers between devices: 417 us -> 2.88 us  [ff_sum(): lax.psum_scatter(value, 'fsdp', scatter_dimension=0, tiled=True, axis_ind...]
    ppermute x8 -> x22, waiting for transfers between devices: 156 us -> 81 us  [from_chip(): lax.ppermute(value, 'seq', [(i, i ^ 2) for i in range(lax.axis_size('seq'...]
    ppermute x0 -> x20, waiting for transfers between devices: none -> 63.5 us  [the longest x17 61.6 us: from_pair(): lax.ppermute(value, 'fsdp', [(i, i ^ 1) for i in range(lax.axis_size('fsd...]
    ppermute x4, waiting for transfers between devices: 61.4 us -> 26.1 us  [mirror(): return lax.ppermute(half, 'fsdp', pairs)]
    all_gather x1 -> x0, blocking collectives: 34.7 us -> none  [fsdp_gather(): return lax.all_gather(value, 'fsdp', axis=0, tiled=True)]
    all_to_all x1 -> x0, blocking collectives: 28.9 us -> none  [local(): lax.all_to_all(grad_out_rows, 'seq', split_axis=1, concat_axis=0, tiled=T...]
    all_gather x9 -> x5, waiting for transfers between devices: 105 us -> 78 us  [the longest x1 61.3 us: sc_gather(): return lax.all_gather(value, 'fsdp', axis=0, tiled=True)]
    pallas_call x0 -> x5, Pallas kernels: none -> 22.7 us  [the longest x1 7.57 us: widen_pair(): pl.pallas_call(widen_pair_kernel, grid_spec=pltpu.PrefetchScalarGridSpec(...]
  transfers between devices with their start and end apart: 35 -> 96, of which waited for: 25 -> 31; matrix products, arithmetic and copies ran while one was open for 15% -> 22% of each run, Pallas kernels for 5% -> 23%
where the time goes in v2:
time: 889 us; the launch traced here: 879 us
  waiting for transfers between devices  277 us (31%)
  Pallas kernels  205 us (23%)
  matrix products  125 us (14%)
  other arithmetic  95.2 us (11%)
  local copies, waits for them, and re-layouts  87.7 us (10%)
  starting transfers between devices  72.5 us (8%)
  between operations  16.8 us (2%)
    pallas_call x2, Pallas kernels, attend_back(): pl.pallas_call(functools.partial(attend_back_kernel, key_block=key_block,...  114 us
    dot_general x17, matrix products, dot(): lax.dot_general(left, right, (((left_dim,), (right_dim,)), ((), ())), pre...  84.7 us
    ppermute x22, waiting for transfers between devices, from_chip(): lax.ppermute(value, 'seq', [(i, i ^ 2) for i in range(lax.axis_size('seq'...  81 us
    pallas_call x2, Pallas kernels, attend(): pl.pallas_call(functools.partial(attend_kernel, key_block=key_block, per_...  68.5 us
    ppermute x17, waiting for transfers between devices, from_pair(): lax.ppermute(value, 'fsdp', [(i, i ^ 1) for i in range(lax.axis_size('fsd...  61.6 us
    all_gather x1, waiting for transfers between devices, sc_gather(): return lax.all_gather(value, 'fsdp', axis=0, tiled=True)  61.3 us
    unnamed x265, local copies, waits for them, and re-layouts  48.2 us
    ppermute x22, starting transfers between devices, from_chip(): lax.ppermute(value, 'seq', [(i, i ^ 2) for i in range(lax.axis_size('seq'...  32.1 us
  transfers between devices with their start and end apart: 96, of which 31 were waited for; matrix products, arithmetic and copies ran while one was open for 22% of the time, Pallas kernels for 23%

profile of v2, /device:TPU:0, one launch (start us, length us, event | category | flops | bytes accessed | tf_op | source)
XLA Modules:
  0.0 879.3 jit_solution(14318660433681320140)
XLA Ops:
  12.2 6.0 collective-permute-start
  19.7 16.3 %collective-permute-done = bf16[128,2048]{1,0:T(8,128)(2,1)S(1)} collective-permute-done((bf16[128,2048]{1,0:T(8,128)(2,1)S(1)}, bf16[128,2048]{1,0:T(8,128)(2,1)S(1)}, u32[]{:S(2)}, u32[]{:S(2)}) %collective-permute-start) | collective-permute-done | bytes 524320 | tf_op jit(solution)/shard_map/ppermute | solution.py:553
  38.1 8.6 collective-permute-done.4
  49.7 3.8 maximum_convert_fusion
  53.5 61.3 %all-gather.7.cloned.1.call-done = bf16[2048,1280]{1,0:T(8,128)(2,1)} async-done(((bf16[256,1280]{1,0:T(8,128)(2,1)}), bf16[2048,1280]{1,0:T(8,128)(2,1)}) %all-gather.7.cloned.1.call-update) | async-done | bytes 5242896 | tf_op jit(solution)/shard_map/all_gather | solution.py:559
  116.7 4.2 fusion.1
  139.1 12.9 %collective-permute-done.9 = bf16[256,768]{1,0:T(8,128)(2,1)S(1)} collective-permute-done((bf16[256,768]{1,0:T(8,128)(2,1)S(1)}, bf16[256,768]{1,0:T(8,128)(2,1)S(1)}, u32[]{:S(2)}, u32[]{:S(2)}) %collective-permute-start.9) | collective-permute-done | bytes 393248 | tf_op jit(solution)/shard_map/ppermute | solution.py:445
  154.7 7.9 collective-permute-done.8
  163.8 10.3 %collective-permute-done.7 = bf16[256,768]{1,0:T(8,128)(2,1)S(1)} collective-permute-done((bf16[256,768]{1,0:T(8,128)(2,1)S(1)}, bf16[256,768]{1,0:T(8,128)(2,1)S(1)}, u32[]{:S(2)}, u32[]{:S(2)}) %collective-permute-start.7) | collective-permute-done | bytes 393248 | tf_op jit(solution)/shard_map/ppermute | solution.py:445
  193.7 4.0 unpack.1
  200.1 36.2 %attend.2 = (f32[512,512]{1,0:T(8,128)S(1)}, f32[4,8,128]{2,1,0:T(8,128)S(1)}) custom-call(s32[9]{0:T(128)S(1)} %pad_add_fusion.places, bf16[512,1024]{1,0:T(8,128)(2,1)S(1)} %bitcast.171, bf16[8192,64]{1,0:T(8,128)(2,1)S(1)} %get-tuple-element.128.keys_ref.refs_4_, bf16[72,8192]{1,0:T(8,128)(2,1)S(1)} %get-tuple-element.129.values_ref), custom_call_target="tpu_custom_call" | custom-call | flops 17179869184 | bytes 8388608 | tf_op jit(solution)/shard_map/attend/pallas_call | solution.py:139
  246.3 32.3 %attend.3 = (f32[512,512]{1,0:T(8,128)S(1)}, f32[4,8,128]{2,1,0:T(8,128)S(1)}) custom-call(s32[9]{0:T(128)S(1)} %pad_add_fusion.places, bf16[512,1024]{1,0:T(8,128)(2,1)S(1)} %bitcast.172, bf16[8192,64]{1,0:T(8,128)(2,1)S(1)} %get-tuple-element.128.keys_ref.refs_4_, bf16[72,8192]{1,0:T(8,128)(2,1)S(1)} %get-tuple-element.129.values_ref), custom_call_target="tpu_custom_call" | custom-call | flops 17179869184 | bytes 8388608 | tf_op jit(solution)/shard_map/attend/pallas_call | solution.py:139
  291.7 3.8 collective-permute-start.23
  298.2 21.0 %collective-permute-done.23 = bf16[256,2048]{1,0:T(8,128)(2,1)S(1)} collective-permute-done((bf16[256,2048]{1,0:T(8,128)(2,1)S(1)}, bf16[256,2048]{1,0:T(8,128)(2,1)S(1)}, u32[]{:S(2)}, u32[]{:S(2)}) %collective-permute-start.23) | collective-permute-done | bytes 1048608 | tf_op jit(solution)/shard_map/ppermute | solution.py:413
  325.3 9.4 %collective-permute-done.27 = bf16[128,2048]{1,0:T(8,128)(2,1)S(1)} collective-permute-done((bf16[128,2048]{1,0:T(8,128)(2,1)S(1)}, bf16[128,2048]{1,0:T(8,128)(2,1)S(1)}, u32[]{:S(2)}, u32[]{:S(2)}) %collective-permute-start.27) | collective-permute-done | bytes 524320 | tf_op jit(solution)/shard_map/ppermute | solution.py:413
  341.4 12.0 %fusion.66 = f32[2048,768]{1,0:T(8,128)} fusion(bf16[2048,2048]{1,0:T(8,128)(2,1)} %copy-done.92, bf16[2048,768]{1,0:T(8,128)(2,1)} %all-gather.9.cloned.1.call-done), kind=kOutput, calls=%fused_computation.259 | convolution fusion | flops 6442450944 | bytes 17825792 | tf_op jit(solution)/shard_map/dot_general | solution.py:679
  353.4 11.7 %fusion.67 = f32[2048,768]{1,0:T(8,128)} fusion(bf16[2048,2048]{1,0:T(8,128)(2,1)} %constant_dynamic-update-slice_fusion.4, bf16[2048,768]{1,0:T(8,128)(2,1)} %all-gather.13.cloned.1.call-done), kind=kOutput, calls=%fused_computation.260 | convolution fusion | flops 6442450944 | bytes 17825792 | tf_op jit(solution)/shard_map/dot_general | solution.py:674
  365.1 15.8 %all-gather.11.cloned.1.call-done = bf16[2048,768]{1,0:T(8,128)(2,1)} async-done(((bf16[512,768]{1,0:T(8,128)(2,1)}), bf16[2048,768]{1,0:T(8,128)(2,1)}) %all-gather.11.cloned.1.call-update) | async-done | bytes 3145744 | tf_op jit(solution)/shard_map/all_gather | solution.py:572
  380.9 16.6 %select_convert_fusion = (bf16[2048,768]{1,0:T(8,128)(2,1)}, bf16[2048,768]{1,0:T(8,128)(2,1)S(1)}, bf16[2048,768]{1,0:T(8,128)(2,1)}) fusion(pred[768]{0:T(1024)(128)(4,1)S(1)} %iota_compare_fusion, f32[2048,768]{1,0:T(8,128)} %fusion.67, f32[2048,768]{1,0:T(8,128)} %fusion.66, bf16[2048,2048]{1,0:T(8,128)(2,1)} %constant_dynamic-update-slice_fusion.4, ...), kind=kOutput, calls=%fused_computation.6 | convolution fusion | flops 6470762496 | bytes 33555200 | tf_op jit(solution)/shard_map/dot_general | solution.py:675
  397.5 9.6 %fusion.68 = f32[2048,2048]{1,0:T(8,128)} fusion(bf16[2048,768]{1,0:T(8,128)(2,1)S(1)} %get-tuple-element.153, bf16[2048,768]{1,0:T(8,128)(2,1)S(1)} %copy-done.108), kind=kOutput, calls=%fused_computation.261 | convolution fusion | flops 6442450944 | bytes 23068672 | tf_op jit(solution)/shard_map/dot_general | solution.py:23
  407.1 14.1 %add_convert_fusion = bf16[2048,2048]{1,0:T(8,128)(2,1)} fusion(f32[2048,2048]{1,0:T(8,128)} %fusion.68, bf16[2048,768]{1,0:T(8,128)(2,1)} %get-tuple-element.154, bf16[2048,768]{1,0:T(8,128)(2,1)} %all-gather.11.cloned.1.call-done), kind=kOutput, calls=%fused_computation | convolution fusion | flops 6450839552 | bytes 31457280 | tf_op jit(solution)/shard_map/dot_general | solution.py:23
  421.2 8.2 convolution_convert_fusion.3
  429.6 4.1 fusion.60
  435.0 7.4 convolution_convert_fusion
  445.8 10.5 %convolution_convert_fusion.2 = bf16[2048,768]{1,0:T(8,128)(2,1)} fusion(bf16[2048,2048]{1,0:T(8,128)(2,1)} %constant_dynamic-update-slice_fusion.4, bf16[2048,768]{1,0:T(8,128)(2,1)S(1)} %copy-done.110), kind=kOutput, calls=%fused_computation.14 | convolution fusion | flops 6444023808 | bytes 14680064 | tf_op jit(solution)/shard_map/dot_general | solution.py:23
  456.4 4.1 convert_add_fusion.9
  463.6 3.9 convert_add_fusion.4
  468.1 8.1 collective-permute-done.40
  480.6 11.0 %convolution_convert_fusion.1 = bf16[2048,768]{1,0:T(8,128)(2,1)} fusion(bf16[2048,2048]{1,0:T(8,128)(2,1)} %constant_dynamic-update-slice_fusion.4, bf16[2048,768]{1,0:T(8,128)(2,1)S(1)} %copy-done.111), kind=kOutput, calls=%fused_computation.13 | convolution fusion | flops 6444023808 | bytes 14680064 | tf_op jit(solution)/shard_map/dot_general | solution.py:23
  492.6 6.2 convert_add_fusion.5
  498.8 4.4 collective-permute-done.41
  507.9 5.2 fusion.59
  527.5 52.5 %attend_back.2 = (f32[512,512]{1,0:T(8,128)}, f32[8192,64]{1,0:T(8,128)}, f32[8192,64]{1,0:T(8,128)}) custom-call(s32[9]{0:T(128)} %copy-done.21, bf16[512,1024]{1,0:T(8,128)(2,1)} %bitcast.173, bf16[512,512]{1,0:T(8,128)(2,1)} %convolution_convert_fusion.11.refs_1_, f32[512,512]{1,0:T(8,128)} %copy-done.7, f32[4,8,128]{2,1,0:T(8,128)} %copy-done.26, ...), custom_call_target="tpu_custom_call" | custom-call | flops 42949672960 | bytes 16777216 | tf_op jit(solution)/shard_map/attend_back/pallas_call | solution.py:253
  598.2 6.3 collective-permute-start.54
  606.5 61.3 %attend_back.3 = (f32[512,512]{1,0:T(8,128)}, bf16[8,128,1024]{2,1,0:T(8,128)(2,1)}) custom-call(s32[9]{0:T(128)} %copy-done.21, bf16[512,1024]{1,0:T(8,128)(2,1)} %bitcast.174, bf16[512,512]{1,0:T(8,128)(2,1)} %convolution_convert_fusion.10.refs_1_, f32[512,512]{1,0:T(8,128)} %copy-done.5, f32[4,8,128]{2,1,0:T(8,128)} %copy-done.25, ...), custom_call_target="tpu_custom_call" | custom-call | flops 42949672960 | bytes 16777216 | tf_op jit(solution)/shard_map/attend_back/pallas_call | solution.py:253
  696.8 4.2 collective-permute-done.59
  702.5 9.8 %collective-permute-done.71 = bf16[128,2048]{1,0:T(8,128)(2,1)S(1)} collective-permute-done((bf16[128,2048]{1,0:T(8,128)(2,1)S(1)}, bf16[128,2048]{1,0:T(8,128)(2,1)S(1)}, u32[]{:S(2)}, u32[]{:S(2)}) %collective-permute-start.71) | collective-permute-done | bytes 524320 | tf_op jit(solution)/shard_map/ppermute | solution.py:553
  713.3 8.2 collective-permute-done.61
  724.6 14.6 %collective-permute-done.57 = bf16[4,256,512]{2,1,0:T(8,128)(2,1)S(1)} collective-permute-done((bf16[4,256,512]{2,1,0:T(8,128)(2,1)S(1)}, bf16[4,256,512]{2,1,0:T(8,128)(2,1)S(1)}, u32[]{:S(2)}, u32[]{:S(2)}) %collective-permute-start.57) | collective-permute-done | bytes 1048608 | tf_op jit(solution)/shard_map/ppermute | solution.py:445
  742.2 21.7 %reduce-scatter.12.cloned.1.call-done = bf16[1,128,1024]{2,1,0:T(8,128)(2,1)} async-done(((bf16[8,128,1024]{2,1,0:T(8,128)(2,1)}), bf16[1,128,1024]{2,1,0:T(8,128)(2,1)}) %reduce-scatter.12.cloned.1.call-update) | async-done | bytes 262160 | tf_op jit(solution)/shard_map/reduce_scatter | solution.py:738
  766.4 8.8 %maximum_maximum_fusion = bf16[1024,1024]{1,0:T(8,128)(2,1)} fusion(bf16[256,512]{1,0:T(8,128)(2,1)S(1)} %get-tuple-element.208, bf16[256,512]{1,0:T(8,128)(2,1)S(1)} %copy-done.71, bf16[256,512]{1,0:T(8,128)(2,1)S(1)} %copy-done.72, bf16[256,512]{1,0:T(8,128)(2,1)S(1)} %copy-done.73, bf16[1024,512]{1,0:T(8,128)(2,1)S(1)} %bitcast.186), kind=kLoop, calls=%fused_computation.35 | loop fusion | flops 10485760 | bytes 4194304 | tf_op jit(solution)/shard_map/concatenate | solution.py:754
  776.6 3.7 convolution_convert_fusion.8
  796.7 6.0 collective-permute-done.75
  802.6 11.9 %collective-permute-done.74 = bf16[256,2048]{1,0:T(8,128)(2,1)S(1)} collective-permute-done((bf16[256,2048]{1,0:T(8,128)(2,1)}, bf16[256,2048]{1,0:T(8,128)(2,1)S(1)}, u32[]{:S(2)}, u32[]{:S(2)}) %collective-permute-start.74) | collective-permute-done | bytes 1048608 | tf_op jit(solution)/shard_map/ppermute | solution.py:413
  825.6 4.8 collective-permute-start.76
  841.6 7.6 widen_pair.1
  851.5 4.0 widen.2
  867.2 4.1 widen_qkv.1
  (594 shorter events, 241.9 us)
Async XLA Ops:
  7.2 107.6 %all-gather.7.cloned.1.call-start = ((), (), s32[]{:S(2)}) async-start(), calls=%async_computation.5 | async-start | bytes 5898240 | tf_op jit(solution)/shard_map/all_gather | solution.py:559
  11.9 177.6 %all-gather.15.cloned.1.call-start = ((), (), s32[]{:S(2)}) async-start(), calls=%async_computation.14 | async-start | bytes 2359296 | tf_op jit(solution)/shard_map/all_gather | solution.py:637
  12.2 23.9 %collective-permute-start = (bf16[128,2048]{1,0:T(8,128)(2,1)S(1)}, bf16[128,2048]{1,0:T(8,128)(2,1)S(1)}, u32[]{:S(2)}, u32[]{:S(2)}) collective-permute-start(bf16[128,2048]{1,0:T(8,128)(2,1)S(1)} %get-tuple-element.302), channel_id=1, source_target_pairs={{0,7},{1,6},{2,5},{3,4},{4,3},{5,2},{6,1},{7,0},{8,15},{9,14},{10,... | collective-permute-start | bytes 1572872 | tf_op jit(solution)/shard_map/ppermute | solution.py:553
  125.5 215.9 %all-gather.9.cloned.1.call-start = ((), (), s32[]{:S(2)}) async-start(), calls=%async_computation.6 | async-start | bytes 3932160 | tf_op jit(solution)/shard_map/all_gather | solution.py:572
  128.0 23.9 %collective-permute-start.9 = (bf16[256,768]{1,0:T(8,128)(2,1)S(1)}, bf16[256,768]{1,0:T(8,128)(2,1)S(1)}, u32[]{:S(2)}, u32[]{:S(2)}) collective-permute-start(bf16[256,768]{1,0:T(8,128)(2,1)S(1)} %constant_dynamic-slice_fusion.5), channel_id=1, source_target_pairs={{0,1},{1,0},{2,3},{3,2},{4,5},{5,4},{6,7},{7,6},{8,9},{9,8},{10,11... | collective-permute-start | bytes 1179656 | tf_op jit(solution)/shard_map/ppermute | solution.py:445
  129.7 32.9 %collective-permute-start.8 = (bf16[256,768]{1,0:T(8,128)(2,1)S(1)}, bf16[256,768]{1,0:T(8,128)(2,1)S(1)}, u32[]{:S(2)}, u32[]{:S(2)}) collective-permute-start(bf16[256,768]{1,0:T(8,128)(2,1)S(1)} %constant_dynamic-slice_fusion.6), channel_id=1, source_target_pairs={{0,1},{1,0},{2,3},{3,2},{4,5},{5,4},{6,7},{7,6},{8,9},{9,8},{10,11... | collective-permute-start | bytes 1179656 | tf_op jit(solution)/shard_map/ppermute | solution.py:445
  132.3 41.8 %collective-permute-start.7 = (bf16[256,768]{1,0:T(8,128)(2,1)S(1)}, bf16[256,768]{1,0:T(8,128)(2,1)S(1)}, u32[]{:S(2)}, u32[]{:S(2)}) collective-permute-start(bf16[256,768]{1,0:T(8,128)(2,1)S(1)} %constant_dynamic-slice_fusion.7), channel_id=1, source_target_pairs={{0,1},{1,0},{2,3},{3,2},{4,5},{5,4},{6,7},{7,6},{8,9},{9,8},{10,11... | collective-permute-start | bytes 1179656 | tf_op jit(solution)/shard_map/ppermute | solution.py:445
  134.0 47.2 %collective-permute-start.10 = (bf16[128,2048]{1,0:T(8,128)(2,1)}, bf16[128,2048]{1,0:T(8,128)(2,1)}, u32[]{:S(2)}, u32[]{:S(2)}) collective-permute-start(bf16[128,2048]{1,0:T(8,128)(2,1)} %get-tuple-element.299), channel_id=1, source_target_pairs={{0,7},{1,6},{2,5},{3,4},{4,3},{5,2},{6,1},{7,0},{8,15},{9,14},{10,... | collective-permute-start | bytes 1572872 | tf_op jit(solution)/shard_map/ppermute | solution.py:553
  137.5 38.5 %collective-permute-start.13 = (bf16[512,512]{1,0:T(8,128)(2,1)S(1)}, bf16[512,512]{1,0:T(8,128)(2,1)}, u32[]{:S(2)}, u32[]{:S(2)}) collective-permute-start(bf16[512,512]{1,0:T(8,128)(2,1)S(1)} %get-tuple-element.278), channel_id=1, source_target_pairs={{0,8},{8,0},{16,24},{24,16},{1,9},{9,1},{17,25},{25,17},{2,10},{10... | collective-permute-start | bytes 1572872 | tf_op jit(solution)/shard_map/ppermute | solution.py:409
  152.0 30.5 %collective-permute-start.12 = (bf16[512,512]{1,0:T(8,128)(2,1)}, bf16[512,512]{1,0:T(8,128)(2,1)}, u32[]{:S(2)}, u32[]{:S(2)}) collective-permute-start(bf16[512,512]{1,0:T(8,128)(2,1)} %get-tuple-element.279), channel_id=1, source_target_pairs={{0,16},{8,24},{16,0},{24,8},{1,17},{9,25},{17,1},{25,9},{2,18},{10... | collective-permute-start | bytes 1572872 | tf_op jit(solution)/shard_map/ppermute | solution.py:413
  189.5 163.9 %all-gather.13.cloned.1.call-start = ((), (), s32[]{:S(2)}) async-start(), calls=%async_computation.8 | async-start | bytes 3932160 | tf_op jit(solution)/shard_map/all_gather | solution.py:572
  189.8 48.2 %collective-permute-start.16 = (bf16[256,2048]{1,0:T(8,128)(2,1)S(1)}, bf16[256,2048]{1,0:T(8,128)(2,1)}, u32[]{:S(2)}, u32[]{:S(2)}) collective-permute-start(bf16[256,2048]{1,0:T(8,128)(2,1)S(1)} %pad_maximum_fusion.3), channel_id=1, source_target_pairs={{0,16},{8,24},{16,0},{24,8},{1,17},{9,25},{17,1},{25,9},{2,18},{10... | collective-permute-start | bytes 3145736 | tf_op jit(solution)/shard_map/ppermute | solution.py:413
  191.3 46.7 %collective-permute-start.15 = (bf16[256,2048]{1,0:T(8,128)(2,1)S(1)}, bf16[256,2048]{1,0:T(8,128)(2,1)}, u32[]{:S(2)}, u32[]{:S(2)}) collective-permute-start(bf16[256,2048]{1,0:T(8,128)(2,1)S(1)} %pad_maximum_fusion.3), channel_id=1, source_target_pairs={{0,1},{1,0},{2,3},{3,2},{4,5},{5,4},{6,7},{7,6},{8,9},{9,8},{10,11... | collective-permute-start | bytes 3145736 | tf_op jit(solution)/shard_map/ppermute | solution.py:445
  191.8 189.1 %all-gather.11.cloned.1.call-start = ((), (), s32[]{:S(2)}) async-start(), calls=%async_computation.7 | async-start | bytes 3932160 | tf_op jit(solution)/shard_map/all_gather | solution.py:572
  239.5 44.8 %collective-permute-start.30 = (bf16[256,2048]{1,0:T(8,128)(2,1)S(1)}, bf16[256,2048]{1,0:T(8,128)(2,1)}, u32[]{:S(2)}, u32[]{:S(2)}) collective-permute-start(bf16[256,2048]{1,0:T(8,128)(2,1)S(1)} %pad_maximum_fusion.3), channel_id=1, source_target_pairs={{0,8},{8,0},{16,24},{24,16},{1,9},{9,1},{17,25},{25,17},{2,10},{10... | collective-permute-start | bytes 3145736 | tf_op jit(solution)/shard_map/ppermute | solution.py:409
  242.2 36.4 %collective-permute-start.20 = (bf16[128,2048]{1,0:T(8,128)(2,1)S(1)}, bf16[128,2048]{1,0:T(8,128)(2,1)S(1)}, u32[]{:S(2)}, u32[]{:S(2)}) collective-permute-start(bf16[128,2048]{1,0:T(8,128)(2,1)S(1)} %slice.243), channel_id=1, source_target_pairs={{0,1},{1,0},{2,3},{3,2},{4,5},{5,4},{6,7},{7,6},{8,9},{9,8},{10,11... | collective-permute-start | bytes 1572872 | tf_op jit(solution)/shard_map/ppermute | solution.py:445
  243.8 34.8 %collective-permute-start.19 = (bf16[128,2048]{1,0:T(8,128)(2,1)S(1)}, bf16[128,2048]{1,0:T(8,128)(2,1)S(1)}, u32[]{:S(2)}, u32[]{:S(2)}) collective-permute-start(bf16[128,2048]{1,0:T(8,128)(2,1)S(1)} %slice.242), channel_id=1, source_target_pairs={{0,16},{8,24},{16,0},{24,8},{1,17},{9,25},{17,1},{25,9},{2,18},{10... | collective-permute-start | bytes 1572872 | tf_op jit(solution)/shard_map/ppermute | solution.py:413
  244.2 35.7 %collective-permute-start.18 = (bf16[256,2048]{1,0:T(8,128)(2,1)S(1)}, bf16[256,2048]{1,0:T(8,128)(2,1)S(1)}, u32[]{:S(2)}, u32[]{:S(2)}) collective-permute-start(bf16[256,2048]{1,0:T(8,128)(2,1)S(1)} %add_convert_fusion.5), channel_id=1, source_target_pairs={{0,16},{8,24},{16,0},{24,8},{1,17},{9,25},{17,1},{25,9},{2,18},{10... | collective-permute-start | bytes 3145736 | tf_op jit(solution)/shard_map/ppermute | solution.py:413
  283.5 229.6 %reduce-scatter.6.cloned.1.call-start = ((), (), s32[]{:S(2)}) async-start(), calls=%async_computation.9 | async-start | bytes 3932160 | tf_op jit(solution)/shard_map/reduce_scatter | solution.py:575
  291.7 27.5 %collective-permute-start.23 = (bf16[256,2048]{1,0:T(8,128)(2,1)S(1)}, bf16[256,2048]{1,0:T(8,128)(2,1)S(1)}, u32[]{:S(2)}, u32[]{:S(2)}) collective-permute-start(bf16[256,2048]{1,0:T(8,128)(2,1)S(1)} %get-tuple-element.243), channel_id=1, source_target_pairs={{0,16},{8,24},{16,0},{24,8},{1,17},{9,25},{17,1},{25,9},{2,18},{10... | collective-permute-start | bytes 3145736 | tf_op jit(solution)/shard_map/ppermute | solution.py:413
  295.6 26.8 %collective-permute-start.33 = (bf16[256,2048]{1,0:T(8,128)(2,1)S(1)}, bf16[256,2048]{1,0:T(8,128)(2,1)S(1)}, u32[]{:S(2)}, u32[]{:S(2)}) collective-permute-start(bf16[256,2048]{1,0:T(8,128)(2,1)S(1)} %pad_maximum_fusion.5), channel_id=1, source_target_pairs={{0,8},{8,0},{16,24},{24,16},{1,9},{9,1},{17,25},{25,17},{2,10},{10... | collective-permute-start | bytes 3145736 | tf_op jit(solution)/shard_map/ppermute | solution.py:409
  295.8 25.4 %collective-permute-start.25 = (bf16[256,2048]{1,0:T(8,128)(2,1)S(1)}, bf16[256,2048]{1,0:T(8,128)(2,1)S(1)}, u32[]{:S(2)}, u32[]{:S(2)}) collective-permute-start(bf16[256,2048]{1,0:T(8,128)(2,1)S(1)} %get-tuple-element.243), channel_id=1, source_target_pairs={{0,1},{1,0},{2,3},{3,2},{4,5},{5,4},{6,7},{7,6},{8,9},{9,8},{10,11... | collective-permute-start | bytes 3145736 | tf_op jit(solution)/shard_map/ppermute | solution.py:445
  296.5 26.1 %collective-permute-start.22 = (bf16[256,2048]{1,0:T(8,128)(2,1)S(1)}, bf16[256,2048]{1,0:T(8,128)(2,1)S(1)}, u32[]{:S(2)}, u32[]{:S(2)}) collective-permute-start(bf16[256,2048]{1,0:T(8,128)(2,1)S(1)} %get-tuple-element.243), channel_id=1, source_target_pairs={{0,8},{8,0},{16,24},{24,16},{1,9},{9,1},{17,25},{25,17},{2,10},{10... | collective-permute-start | bytes 3145736 | tf_op jit(solution)/shard_map/ppermute | solution.py:409
  429.5 150.5 %reduce-scatter.8.cloned.1.call-start = ((), (), s32[]{:S(2)}) async-start(), calls=%async_computation.10 | async-start | bytes 3932160 | tf_op jit(solution)/shard_map/reduce_scatter | solution.py:575
  433.7 65.1 %collective-permute-start.34 = (bf16[256,2048]{1,0:T(8,128)(2,1)}, bf16[256,2048]{1,0:T(8,128)(2,1)}, u32[]{:S(2)}, u32[]{:S(2)}) collective-permute-start(bf16[256,2048]{1,0:T(8,128)(2,1)} %get-tuple-element.256), channel_id=1, source_target_pairs={{0,8},{8,0},{16,24},{24,16},{1,9},{9,1},{17,25},{25,17},{2,10},{10... | collective-permute-start | bytes 3145736 | tf_op jit(solution)/shard_map/ppermute | solution.py:409
  467.6 24.1 %collective-permute-start.43 = (bf16[256,2048]{1,0:T(8,128)(2,1)}, bf16[256,2048]{1,0:T(8,128)(2,1)S(1)}, u32[]{:S(2)}, u32[]{:S(2)}) collective-permute-start(bf16[256,2048]{1,0:T(8,128)(2,1)} %get-tuple-element.251), channel_id=1, source_target_pairs={{0,8},{8,0},{16,24},{24,16},{1,9},{9,1},{17,25},{25,17},{2,10},{10... | collective-permute-start | bytes 3145736 | tf_op jit(solution)/shard_map/ppermute | solution.py:409
  477.4 25.9 %collective-permute-start.41 = (bf16[256,2048]{1,0:T(8,128)(2,1)}, bf16[256,2048]{1,0:T(8,128)(2,1)}, u32[]{:S(2)}, u32[]{:S(2)}) collective-permute-start(bf16[256,2048]{1,0:T(8,128)(2,1)} %pad_maximum_fusion.7), channel_id=1, source_target_pairs={{0,1},{1,0},{2,3},{3,2},{4,5},{5,4},{6,7},{7,6},{8,9},{9,8},{10,11... | collective-permute-start | bytes 3145736 | tf_op jit(solution)/shard_map/ppermute | solution.py:445
  479.2 25.6 %collective-permute-start.38 = (bf16[256,2048]{1,0:T(8,128)(2,1)}, bf16[256,2048]{1,0:T(8,128)(2,1)}, u32[]{:S(2)}, u32[]{:S(2)}) collective-permute-start(bf16[256,2048]{1,0:T(8,128)(2,1)} %pad_maximum_fusion.6), channel_id=1, source_target_pairs={{0,16},{8,24},{16,0},{24,8},{1,17},{9,25},{17,1},{25,9},{2,18},{10... | collective-permute-start | bytes 3145736 | tf_op jit(solution)/shard_map/ppermute | solution.py:413
  513.2 154.8 %reduce-scatter.10.cloned.1.call-start = ((), (), s32[]{:S(2)}) async-start(), calls=%async_computation.11 | async-start | bytes 3932160 | tf_op jit(solution)/shard_map/reduce_scatter | solution.py:575
  513.3 66.7 %collective-permute-start.47 = (bf16[256,2048]{1,0:T(8,128)(2,1)}, bf16[256,2048]{1,0:T(8,128)(2,1)}, u32[]{:S(2)}, u32[]{:S(2)}) collective-permute-start(bf16[256,2048]{1,0:T(8,128)(2,1)} %get-tuple-element.156), channel_id=1, source_target_pairs={{0,16},{8,24},{16,0},{24,8},{1,17},{9,25},{17,1},{25,9},{2,18},{10... | collective-permute-start | bytes 3145736 | tf_op jit(solution)/shard_map/ppermute | solution.py:413
  516.5 63.4 %collective-permute-start.50 = (bf16[256,768]{1,0:T(8,128)(2,1)}, bf16[256,768]{1,0:T(8,128)(2,1)S(1)}, u32[]{:S(2)}, u32[]{:S(2)}) collective-permute-start(bf16[256,768]{1,0:T(8,128)(2,1)} %dynamic-slice_bitcast_fusion.14), channel_id=1, source_target_pairs={{0,1},{1,0},{2,3},{3,2},{4,5},{5,4},{6,7},{7,6},{8,9},{9,8},{10,11... | collective-permute-start | bytes 1179656 | tf_op jit(solution)/shard_map/ppermute | solution.py:445
  522.0 57.9 %collective-permute-start.49 = (bf16[128,2048]{1,0:T(8,128)(2,1)}, bf16[128,2048]{1,0:T(8,128)(2,1)}, u32[]{:S(2)}, u32[]{:S(2)}) collective-permute-start(bf16[128,2048]{1,0:T(8,128)(2,1)} %get-tuple-element.294), channel_id=1, source_target_pairs={{0,1},{1,0},{2,3},{3,2},{4,5},{5,4},{6,7},{7,6},{8,9},{9,8},{10,11... | collective-permute-start | bytes 1572872 | tf_op jit(solution)/shard_map/ppermute | solution.py:445
  522.8 57.2 %collective-permute-start.48 = (bf16[128,2048]{1,0:T(8,128)(2,1)}, bf16[128,2048]{1,0:T(8,128)(2,1)}, u32[]{:S(2)}, u32[]{:S(2)}) collective-permute-start(bf16[128,2048]{1,0:T(8,128)(2,1)} %get-tuple-element.295), channel_id=1, source_target_pairs={{0,16},{8,24},{16,0},{24,8},{1,17},{9,25},{17,1},{25,9},{2,18},{10... | collective-permute-start | bytes 1572872 | tf_op jit(solution)/shard_map/ppermute | solution.py:413
  523.4 240.4 %reduce-scatter.12.cloned.1.call-start = ((), (), s32[]{:S(2)}) async-start(), calls=%async_computation.12 | async-start | bytes 2359296 | tf_op jit(solution)/shard_map/reduce_scatter | solution.py:738
  596.5 71.3 %collective-permute-start.55 = (bf16[256,768]{1,0:T(8,128)(2,1)S(1)}, bf16[256,768]{1,0:T(8,128)(2,1)S(1)}, u32[]{:S(2)}, u32[]{:S(2)}) collective-permute-start(bf16[256,768]{1,0:T(8,128)(2,1)S(1)} %dynamic-slice_bitcast_fusion.12), channel_id=1, source_target_pairs={{0,1},{1,0},{2,3},{3,2},{4,5},{5,4},{6,7},{7,6},{8,9},{9,8},{10,11... | collective-permute-start | bytes 1179656 | tf_op jit(solution)/shard_map/ppermute | solution.py:445
  598.2 69.8 %collective-permute-start.54 = (bf16[256,1408]{1,0:T(8,128)(2,1)S(1)}, bf16[256,1408]{1,0:T(8,128)(2,1)S(1)}, u32[]{:S(2)}, u32[]{:S(2)}) collective-permute-start(bf16[256,1408]{1,0:T(8,128)(2,1)S(1)} %pad_maximum_fusion.15.refs_0_), channel_id=1, source_target_pairs={{0,16},{8,24},{16,0},{24,8},{1,17},{9,25},{17,1},{25,9},{2,18},{10... | collective-permute-start | bytes 2162696 | tf_op jit(solution)/shard_map/ppermute | solution.py:413
  604.5 63.5 %collective-permute-start.52 = (bf16[256,2048]{1,0:T(8,128)(2,1)}, bf16[256,2048]{1,0:T(8,128)(2,1)}, u32[]{:S(2)}, u32[]{:S(2)}) collective-permute-start(bf16[256,2048]{1,0:T(8,128)(2,1)} %pad_maximum_fusion.8), channel_id=1, source_target_pairs={{0,16},{8,24},{16,0},{24,8},{1,17},{9,25},{17,1},{25,9},{2,18},{10... | collective-permute-start | bytes 3145736 | tf_op jit(solution)/shard_map/ppermute | solution.py:413
  604.5 63.5 %collective-permute-start.53 = (bf16[256,2048]{1,0:T(8,128)(2,1)}, bf16[256,2048]{1,0:T(8,128)(2,1)}, u32[]{:S(2)}, u32[]{:S(2)}) collective-permute-start(bf16[256,2048]{1,0:T(8,128)(2,1)} %pad_maximum_fusion.9), channel_id=1, source_target_pairs={{0,1},{1,0},{2,3},{3,2},{4,5},{5,4},{6,7},{7,6},{8,9},{9,8},{10,11... | collective-permute-start | bytes 3145736 | tf_op jit(solution)/shard_map/ppermute | solution.py:445
  605.3 62.7 %collective-permute-start.56 = (bf16[1,256,2048]{2,1,0:T(8,128)(2,1)}, bf16[1,256,2048]{2,1,0:T(8,128)(2,1)}, u32[]{:S(2)}, u32[]{:S(2)}) collective-permute-start(bf16[1,256,2048]{2,1,0:T(8,128)(2,1)} %dynamic-slice_bitcast_fusion.1), channel_id=1, source_target_pairs={{0,1},{1,0},{2,3},{3,2},{4,5},{5,4},{6,7},{7,6},{8,9},{9,8},{10,11... | collective-permute-start | bytes 3145736 | tf_op jit(solution)/shard_map/ppermute | solution.py:445
  669.4 52.2 %collective-permute-start.65 = (bf16[256,1408]{1,0:T(8,128)(2,1)S(1)}, bf16[256,1408]{1,0:T(8,128)(2,1)}, u32[]{:S(2)}, u32[]{:S(2)}) collective-permute-start(bf16[256,1408]{1,0:T(8,128)(2,1)S(1)} %pad_maximum_fusion.16.refs_0_), channel_id=1, source_target_pairs={{0,16},{8,24},{16,0},{24,8},{1,17},{9,25},{17,1},{25,9},{2,18},{10... | collective-permute-start | bytes 2162696 | tf_op jit(solution)/shard_map/ppermute | solution.py:413
  669.5 52.6 %collective-permute-start.64 = (bf16[256,1408]{1,0:T(8,128)(2,1)S(1)}, bf16[256,1408]{1,0:T(8,128)(2,1)}, u32[]{:S(2)}, u32[]{:S(2)}) collective-permute-start(bf16[256,1408]{1,0:T(8,128)(2,1)S(1)} %pad_maximum_fusion.16.refs_0_), channel_id=1, source_target_pairs={{0,8},{8,0},{16,24},{24,16},{1,9},{9,1},{17,25},{25,17},{2,10},{10... | collective-permute-start | bytes 2162696 | tf_op jit(solution)/shard_map/ppermute | solution.py:409
  675.6 142.8 %reduce-scatter.14.cloned.1.call-start = ((), (), s32[]{:S(2)}) async-start(), calls=%async_computation.13 | async-start | bytes 2621440 | tf_op jit(solution)/shard_map/reduce_scatter | solution.py:575
  693.8 28.4 %collective-permute-start.69 = (bf16[256,1408]{1,0:T(8,128)(2,1)S(1)}, bf16[256,1408]{1,0:T(8,128)(2,1)S(1)}, u32[]{:S(2)}, u32[]{:S(2)}) collective-permute-start(bf16[256,1408]{1,0:T(8,128)(2,1)S(1)} %pad_maximum_fusion.17.refs_4_), channel_id=1, source_target_pairs={{0,16},{8,24},{16,0},{24,8},{1,17},{9,25},{17,1},{25,9},{2,18},{10... | collective-permute-start | bytes 2162696 | tf_op jit(solution)/shard_map/ppermute | solution.py:413
  701.0 38.3 %collective-permute-start.57 = (bf16[4,256,512]{2,1,0:T(8,128)(2,1)S(1)}, bf16[4,256,512]{2,1,0:T(8,128)(2,1)S(1)}, u32[]{:S(2)}, u32[]{:S(2)}) collective-permute-start(bf16[4,256,512]{2,1,0:T(8,128)(2,1)S(1)} %dynamic-slice_bitcast_fusion), channel_id=1, source_target_pairs={{0,1},{1,0},{2,3},{3,2},{4,5},{5,4},{6,7},{7,6},{8,9},{9,8},{10,11... | collective-permute-start | bytes 3145736 | tf_op jit(solution)/shard_map/ppermute | solution.py:445
  788.9 25.6 %collective-permute-start.74 = (bf16[256,2048]{1,0:T(8,128)(2,1)}, bf16[256,2048]{1,0:T(8,128)(2,1)S(1)}, u32[]{:S(2)}, u32[]{:S(2)}) collective-permute-start(bf16[256,2048]{1,0:T(8,128)(2,1)} %add_convert_fusion.2), channel_id=1, source_target_pairs={{0,16},{8,24},{16,0},{24,8},{1,17},{9,25},{17,1},{25,9},{2,18},{10... | collective-permute-start | bytes 3145736 | tf_op jit(solution)/shard_map/ppermute | solution.py:413
  825.6 32.8 %collective-permute-start.76 = (bf16[128,2048]{1,0:T(8,128)(2,1)}, bf16[128,2048]{1,0:T(8,128)(2,1)}, u32[]{:S(2)}, u32[]{:S(2)}) collective-permute-start(bf16[128,2048]{1,0:T(8,128)(2,1)} %slice.399), channel_id=1, source_target_pairs={{0,7},{1,6},{2,5},{3,4},{4,3},{5,2},{6,1},{7,0},{8,15},{9,14},{10,... | collective-permute-start | bytes 1572872 | tf_op jit(solution)/shard_map/ppermute | solution.py:553
  830.3 28.0 %collective-permute-start.80 = (bf16[256,1024]{1,0:T(8,128)(2,1)S(1)}, bf16[256,1024]{1,0:T(8,128)(2,1)}, u32[]{:S(2)}, u32[]{:S(2)}) collective-permute-start(bf16[256,1024]{1,0:T(8,128)(2,1)S(1)} %copy-done.3), channel_id=1, source_target_pairs={{0,8},{8,0},{16,24},{24,16},{1,9},{9,1},{17,25},{25,17},{2,10},{10... | collective-permute-start | bytes 1572872 | tf_op jit(solution)/shard_map/ppermute | solution.py:409
  832.1 26.2 %collective-permute-start.82 = (bf16[256,1024]{1,0:T(8,128)(2,1)S(1)}, bf16[256,1024]{1,0:T(8,128)(2,1)}, u32[]{:S(2)}, u32[]{:S(2)}) collective-permute-start(bf16[256,1024]{1,0:T(8,128)(2,1)S(1)} %collective-permute-done.81.refs_2_), channel_id=1, source_target_pairs={{0,8},{8,0},{16,24},{24,16},{1,9},{9,1},{17,25},{25,17},{2,10},{10... | collective-permute-start | bytes 1572872 | tf_op jit(solution)/shard_map/ppermute | solution.py:409
  (171 other events, 2374.6 us)
Sparse Core Ops, SparseCore 0:
  12.0 102.7 all-gather.6
  125.6 63.8 all-gather.14
  191.7 61.4 all-gather.8
  255.1 62.1 all-gather.12
  318.7 62.1 all-gather.10
  429.6 58.8 reduce-scatter.5
  513.3 58.8 reduce-scatter.7
  574.4 60.2 reduce-scatter.9
  675.7 88.1 reduce-scatter.11
  775.4 42.9 reduce-scatter.13

commit v3 on v2

--- a/solution.py
+++ b/solution.py
@@ -99,12 +99,13 @@
     max_s[...] = jnp.full(max_s.shape, -1e30, wide)
     sum_s[...] = jnp.zeros(sum_s.shape, wide)
 
-    def step(index, masked):
+    def step(index, masked=0):
         offset = pl.multiple_of(index * key_block, key_block)
-        keys = keys_ref[pl.ds(offset, key_block), :]
-        values = values_ref[:, pl.ds(offset, key_block)]
+        size = masked or key_block
+        keys = keys_ref[pl.ds(offset, size), :]
+        values = values_ref[:, pl.ds(offset, size)]
         if masked:
-            keep = causal(offset, first, key_block, tile, per_chunk)
+            keep = causal(offset, first, size, tile, per_chunk)
         for c in range(chunks):
             scores = jnp.dot(keys, queries[c], preferred_element_type=wide)
             if masked:
@@ -118,8 +119,13 @@
             )
 
     full = first // key_block
-    lax.fori_loop(0, full, lambda i, _: (step(i, False), 0)[1], 0)
-    step(full, True)
+    lax.fori_loop(0, full, lambda i, _: (step(i), 0)[1], 0)
+    for size in range(tile, key_block + tile, tile):
+
+        @pl.when(first % key_block == size - tile)
+        def _(size=size):
+            step(full, size)
+
     for c in range(chunks):
         sums = sum_s[c]
         total = sums[HDIM : HDIM + 1, :]
@@ -194,13 +200,14 @@
     ]
     gq_s[...] = jnp.zeros(gq_s.shape, wide)
 
-    def step(index, masked):
+    def step(index, masked=0):
         offset = pl.multiple_of(index * key_block, key_block)
-        keys = keys_ref[pl.ds(offset, key_block), :]
-        values = values_ref[pl.ds(offset, key_block), :]
-        keys_t = kt_ref[:, pl.ds(offset, key_block)]
+        size = masked or key_block
+        keys = keys_ref[pl.ds(offset, size), :]
+        values = values_ref[pl.ds(offset, size), :]
+        keys_t = kt_ref[:, pl.ds(offset, size)]
         if masked:
-            keep = causal(offset, first, key_block, tile, per_chunk)
+            keep = causal(offset, first, size, tile, per_chunk)
         grad_k = grad_v = None
         for c in range(chunks):
             scores = jnp.dot(keys, queries[c], preferred_element_type=wide)
@@ -214,12 +221,17 @@
             gq_s[c] += jnp.dot(keys_t, grad_scores, preferred_element_type=wide)
             grad_k = more_k if grad_k is None else grad_k + more_k
             grad_v = more_v if grad_v is None else grad_v + more_v
-        gk_s[pl.ds(offset, key_block), :] += grad_k
-        gv_s[pl.ds(offset, key_block), :] += grad_v
+        gk_s[pl.ds(offset, size), :] += grad_k
+        gv_s[pl.ds(offset, size), :] += grad_v
 
     full = first // key_block
-    lax.fori_loop(0, full, lambda i, _: (step(i, False), 0)[1], 0)
-    step(full, True)
+    lax.fori_loop(0, full, lambda i, _: (step(i), 0)[1], 0)
+    for size in range(tile, key_block + tile, tile):
+
+        @pl.when(first % key_block == size - tile)
+        def _(size=size):
+            step(full, size)
+
     for c in range(chunks):
         grad_q = gq_s[c] * HDIM**-0.5
         for i in range(per_chunk):
@@ -290,16 +302,15 @@
             out_ref[...] = ref[...].astype(wide)
 
 
-def widen(own, pieces, at=0, columns=None):
+def widen(own, pieces):
     parts = len(pieces)
-    rows = pieces[0].shape[0]
-    columns = columns or pieces[0].shape[1]
+    rows, columns = pieces[0].shape
     return pl.pallas_call(
         widen_kernel,
         grid_spec=pltpu.PrefetchScalarGridSpec(
             num_scalar_prefetch=1,
             grid=(parts,),
-            in_specs=[pl.BlockSpec((rows, columns), lambda i, own: (0, at))] * parts,
+            in_specs=[pl.BlockSpec((rows, columns), lambda i, own: (0, 0))] * parts,
             out_specs=pl.BlockSpec((rows, columns), lambda i, own: (0, i ^ own[0])),
         ),
         out_shape=jax.ShapeDtypeStruct((rows, parts * columns), wide),
@@ -308,10 +319,10 @@
     )(own, *pieces)
 
 
-def widen_pair_kernel(own, *refs):
-    weight_ref, out_ref, total_ref = refs[-3:]
+def widen_half_kernel(own, *refs, parts):
+    weight_ref, (out_ref, total_ref) = refs[parts], refs[-2:]
     step = pl.program_id(0)
-    for i, ref in enumerate(refs[:-3]):
+    for i, ref in enumerate(refs[:parts]):
 
         @pl.when(step == i)
         def _(ref=ref):
@@ -321,20 +332,21 @@
             total_ref[...] = jnp.where(step == 0, more, total_ref[...] + more)
 
 
-def widen_pair(own, left, right, weight):
-    parts = len(left)
-    rows, columns = left[0].shape
+def widen_half(own, pieces, weight, half, before=()):
+    parts = len(pieces)
+    rows, columns = pieces[0].shape
 
     def place(i, own):
-        return (0, i // parts * parts + (i % parts ^ own[0]))
+        return (0, half * parts + (i ^ own[0]))
 
     return pl.pallas_call(
-        widen_pair_kernel,
+        functools.partial(widen_half_kernel, parts=parts),
         grid_spec=pltpu.PrefetchScalarGridSpec(
             num_scalar_prefetch=1,
-            grid=(2 * parts,),
-            in_specs=[pl.BlockSpec((rows, columns), lambda i, own: (0, 0))] * (2 * parts)
-            + [pl.BlockSpec((rows, columns), place)],
+            grid=(parts,),
+            in_specs=[pl.BlockSpec((rows, columns), lambda i, own: (0, 0))] * parts
+            + [pl.BlockSpec((rows, columns), place)]
+            + [pl.BlockSpec(memory_space=pl.ANY)] * len(before),
             out_specs=[
                 pl.BlockSpec((rows, columns), place),
                 pl.BlockSpec((rows, 1), lambda i, own: (0, 0)),
@@ -344,9 +356,10 @@
             jax.ShapeDtypeStruct((rows, 2 * parts * columns), wide),
             jax.ShapeDtypeStruct((rows, 1), wide),
         ],
+        input_output_aliases={parts + 2: 0} if before else {},
         compiler_params=pltpu.CompilerParams(vmem_limit_bytes=32 << 20),
-        name="widen_pair",
-    )(own, *left, *right, weight)
+        name="widen_half",
+    )(own, *pieces, weight, *before)
 
 
 def widen_qkv_kernel(own, *refs, parts):
@@ -477,10 +490,13 @@
     return near + from_chip(far).astype(wide) + from_pair(beside).astype(wide)
 
 
+def from_diagonal(value):
+    return lax.ppermute(value, "seq", [(i, i ^ 3) for i in range(lax.axis_size("seq"))])
+
+
 def seq_swap(value):
     sent = slots_by_index(value)
-    corner = from_core(sent[3])
-    came = [sent[0], from_core(sent[1]), from_chip(sent[2]), from_chip(corner)]
+    came = [sent[0], from_core(sent[1]), from_chip(sent[2]), from_diagonal(sent[3])]
     return slots_by_index(jnp.stack(came))
 
 
@@ -733,36 +749,39 @@
         (grad_q_far, grad_kv, feed_far, feed_beside, far_down, other_gate, other_out, sum_up)
     )
     layer_out = (middle + feed_near + feed_far.astype(wide) + feed_beside.astype(wide)).astype(low)
-    out_pair = pair_add(mine_out, other_out).reshape(-1, seq_parts, width // seq_parts)
 
     grad_kv = lax.psum_scatter(grad_kv, "fsdp", scatter_dimension=0, axis_index_groups=groups)
     grad_q = jnp.concatenate([grad_q_near, grad_q_far], axis=1).astype(low).astype(wide)
     grad_q = turn(grad_q.reshape(GROUP, HDIM, slab), cosine, -sine).reshape(q_part, slab).astype(low)
+    own = seq_index[None].astype(jnp.int32)
     mine_q, theirs = pair_split(dot(normed_one, grad_q, 0, 1).astype(low).reshape(blocks // 2, 2, -1, q_part))
     other_q = from_pair(theirs)
-    out_swapped = seq_swap(out_pair.transpose(1, 0, 2))
-    mirrored_out = mirror(layer_out[tile:])
+    out_pair = pair_add(mine_out, other_out).reshape(-1, seq_parts, width // seq_parts)
+    out_sums = seq_swap(out_pair.transpose(1, 0, 2))
     down_all = [own_down, from_core(own_down), far_down, from_core(far_down)]
     gate_all = seq_gather(ff_columns(mine_gate, other_gate))
     mine, theirs = ff_split(sum_up)
     up_all = seq_gather(ff_columns(mine, from_pair(theirs)))
-    grad_kv, other_q, out_swapped, down_all, gate_all, up_all, mirrored_out = lax.optimization_barrier(
-        (grad_kv, other_q, out_swapped, down_all, gate_all, up_all, mirrored_out)
-    )
-    layer_out = jnp.concatenate([layer_out[:tile], mirrored_out], axis=0)
-    grad_q_out_own = ff_sum(
-        jnp.concatenate(
-            [pair_add(mine_q, other_q).reshape(-1, q_part), jnp.concatenate(out_swapped, axis=0)], axis=1
-        )
+    q_far = dot(grad_q[:, slab // 2 :], qkv_part[:, :q_part], 0, 1)
+    q_near = dot(grad_q[:, : slab // 2], qkv_part[:, :q_part], 0, 1)
+    sent_out = layer_out[tile:]
+    grad_kv, other_q, out_sums, down_all, gate_all, up_all, sent_out, q_far, q_near = lax.optimization_barrier(
+        (grad_kv, other_q, out_sums, down_all, gate_all, up_all, sent_out, q_far, q_near)
     )
     grad_k = turn(grad_kv[:HDIM].astype(wide).reshape(1, HDIM, slab), cosine, -sine)[0].astype(low)
     grad_kv = jnp.concatenate([grad_k, grad_kv[HDIM:]], axis=0)
-    grad_projected = jnp.concatenate([grad_q, grad_kv], axis=0)
-    part_two, part_three = slots(dot(grad_projected[:, slab // 2 :], qkv_part, 0, 1))
+    part_two, part_three = slots(q_far + dot(grad_kv[:, slab // 2 :], qkv_part[:, q_part:], 0, 1))
     far_one = (part_two.astype(wide) + from_core(part_three).astype(wide)).astype(low)
-    far_one, grad_projected, grad_kv = lax.optimization_barrier((far_one, grad_projected, grad_kv))
+    far_one, grad_kv, q_near, mine_q, other_q, out_sums = lax.optimization_barrier(
+        (far_one, grad_kv, q_near, mine_q, other_q, out_sums)
+    )
     came_one = from_chip(far_one)
-    part_zero, part_one = slots(dot(grad_projected[:, : slab // 2], qkv_part, 0, 1))
+    grad_out_own = ff_sum(jnp.concatenate(out_sums, axis=0))
+    grad_q_own = ff_sum(pair_add(mine_q, other_q).reshape(-1, q_part))
+    part_zero, part_one = slots(q_near + dot(grad_kv[:, : slab // 2], qkv_part[:, q_part:], 0, 1))
+    weight_grad_down = widen(own, down_all)
+    weight_grad_gate, sums_gate = widen_half(own, gate_all, w_gate_up, 0)
+    weight_grad_gate_up, sums_up = widen_half(own, up_all, w_gate_up, 1, (weight_grad_gate,))
     mine_kv, theirs = pair_split(
         dot(normed_one, grad_kv, 0, 1).astype(low).reshape(blocks // 2, 2, -1, 2 * HDIM)
     )
@@ -778,19 +797,18 @@
     grad_inputs, kv_pair = lax.optimization_barrier((grad_inputs, pair_add(mine_kv, other_kv)))
     back = mirror(grad_inputs[tile:].astype(low))
     grad_kv_own = turns_sum(kv_pair)
-    own = seq_index[None].astype(jnp.int32)
-    weight_grad_gate_up, sums_two = widen_pair(own, gate_all, up_all, w_gate_up)
-    weight_grad_down = widen(own, down_all)
-    q_out_all = seq_gather(grad_q_out_own)
-    back, grad_kv_own, q_out_all, weight_grad_down = lax.optimization_barrier(
-        (back, grad_kv_own, q_out_all, weight_grad_down)
-    )
+    back, grad_kv_own, grad_q_own, grad_out_own, sent_out, weight_grad_gate_up, weight_grad_down = (
+        lax.optimization_barrier(
+            (back, grad_kv_own, grad_q_own, grad_out_own, sent_out, weight_grad_gate_up, weight_grad_down)
+        )
+    )
+    layer_out = jnp.concatenate([layer_out[:tile], mirror(sent_out)], axis=0)
+    q_all, out_all = seq_gather(grad_q_own), seq_gather(grad_out_own)
     grad_inputs = jnp.concatenate([grad_inputs[:tile], back.astype(wide)], axis=0)
-
-    weight_grad_out = widen(own, q_out_all, 1, width // seq_parts)
-    weight_grad_qkv, sums_one = widen_qkv(own, q_out_all, seq_gather(grad_kv_own), w_qkv)
+    weight_grad_out = widen(own, out_all)
+    weight_grad_qkv, sums_one = widen_qkv(own, q_all, seq_gather(grad_kv_own), w_qkv)
     grad_gain_one = sums_one[:, 0] / gain_attn.astype(wide)
-    grad_gain_two = sums_two[:, 0] / gain_mlp.astype(wide)
+    grad_gain_two = (sums_gate + sums_up)[:, 0] / gain_mlp.astype(wide)
     return (
         layer_out.reshape(tokens.shape),
         grad_inputs.reshape(tokens.shape),

time: 889 us -> 882 us (level)
    ppermute x3, waiting for transfers between devices: 1.9 us -> 18.6 us  [from_turn(): lax.ppermute(value, 'fsdp', [(i, (i + 2 * by) % size) for i in range(size)])]
    ppermute x4, waiting for transfers between devices: 26.1 us -> 16.4 us  [mirror(): return lax.ppermute(half, 'fsdp', pairs)]
    ppermute x17, waiting for transfers between devices: 61.6 us -> 51.9 us  [from_pair(): lax.ppermute(value, 'fsdp', [(i, i ^ 1) for i in range(lax.axis_size('fsd...]
    dot_general x17 -> x19, matrix products: 84.7 us -> 88.6 us  [dot(): lax.dot_general(left, right, (((left_dim,), (right_dim,)), ((), ())), pre...]
    ppermute x22 -> x21, waiting for transfers between devices: 81 us -> 84 us  [from_chip(): lax.ppermute(value, 'seq', [(i, i ^ 2) for i in range(lax.axis_size('seq'...]
    unnamed x265 -> x271, local copies, waits for them, and re-layouts: 48.2 us -> 46.2 us
    ppermute x22 -> x21, starting transfers between devices: 32.1 us -> 30.2 us  [from_chip(): lax.ppermute(value, 'seq', [(i, i ^ 2) for i in range(lax.axis_size('seq'...]
  transfers between devices with their start and end apart: 96 -> 98, of which waited for: 31 -> 28; matrix products, arithmetic and copies ran while one was open for 22% -> 23% of each run, Pallas kernels for 23% -> 23%
where the time goes in v3:
time: 882 us; the launch traced here: 868 us
  waiting for transfers between devices  275 us (31%)
  Pallas kernels  197 us (22%)
  matrix products  129 us (15%)
  other arithmetic  88.9 us (10%)
  local copies, waits for them, and re-layouts  88.6 us (10%)
  starting transfers between devices  72.4 us (8%)
  between operations  16.5 us (2%)
    pallas_call x2, Pallas kernels, attend_back(): pl.pallas_call(functools.partial(attend_back_kernel, key_block=key_block,...  111 us
    dot_general x19, matrix products, dot(): lax.dot_general(left, right, (((left_dim,), (right_dim,)), ((), ())), pre...  88.6 us
    ppermute x21, waiting for transfers between devices, from_chip(): lax.ppermute(value, 'seq', [(i, i ^ 2) for i in range(lax.axis_size('seq'...  84 us
    pallas_call x2, Pallas kernels, attend(): pl.pallas_call(functools.partial(attend_kernel, key_block=key_block, per_...  66.5 us
    all_gather x1, waiting for transfers between devices, sc_gather(): return lax.all_gather(value, 'fsdp', axis=0, tiled=True)  61.3 us
    ppermute x17, waiting for transfers between devices, from_pair(): lax.ppermute(value, 'fsdp', [(i, i ^ 1) for i in range(lax.axis_size('fsd...  51.9 us
    unnamed x271, local copies, waits for them, and re-layouts  46.2 us
    ppermute x21, starting transfers between devices, from_chip(): lax.ppermute(value, 'seq', [(i, i ^ 2) for i in range(lax.axis_size('seq'...  30.2 us
  transfers between devices with their start and end apart: 98, of which 28 were waited for; matrix products, arithmetic and copies ran while one was open for 23% of the time, Pallas kernels for 23%

profile of v3, /device:TPU:0, one launch (start us, length us, event | category | flops | bytes accessed | tf_op | source)
XLA Modules:
  0.0 868.1 jit_solution(6673479921349141778)
XLA Ops:
  12.2 6.0 collective-permute-start
  19.7 16.3 %collective-permute-done = bf16[128,2048]{1,0:T(8,128)(2,1)S(1)} collective-permute-done((bf16[128,2048]{1,0:T(8,128)(2,1)S(1)}, bf16[128,2048]{1,0:T(8,128)(2,1)S(1)}, u32[]{:S(2)}, u32[]{:S(2)}) %collective-permute-start) | collective-permute-done | bytes 524320 | tf_op jit(solution)/shard_map/ppermute | solution.py:569
  38.1 8.6 collective-permute-done.4
  49.7 3.8 maximum_convert_fusion
  53.5 61.3 %all-gather.7.cloned.1.call-done = bf16[2048,1280]{1,0:T(8,128)(2,1)} async-done(((bf16[256,1280]{1,0:T(8,128)(2,1)}), bf16[2048,1280]{1,0:T(8,128)(2,1)}) %all-gather.7.cloned.1.call-update) | async-done | bytes 5242896 | tf_op jit(solution)/shard_map/all_gather | solution.py:575
  116.7 4.2 fusion.1
  139.1 12.8 %collective-permute-done.9 = bf16[256,768]{1,0:T(8,128)(2,1)S(1)} collective-permute-done((bf16[256,768]{1,0:T(8,128)(2,1)S(1)}, bf16[256,768]{1,0:T(8,128)(2,1)S(1)}, u32[]{:S(2)}, u32[]{:S(2)}) %collective-permute-start.9) | collective-permute-done | bytes 393248 | tf_op jit(solution)/shard_map/ppermute | solution.py:458
  154.7 8.0 collective-permute-done.8
  164.7 9.5 %collective-permute-done.7 = bf16[256,768]{1,0:T(8,128)(2,1)} collective-permute-done((bf16[256,768]{1,0:T(8,128)(2,1)S(1)}, bf16[256,768]{1,0:T(8,128)(2,1)}, u32[]{:S(2)}, u32[]{:S(2)}) %collective-permute-start.7) | collective-permute-done | bytes 393248 | tf_op jit(solution)/shard_map/ppermute | solution.py:458
  183.2 6.3 all-gather.15.cloned.1.call-done
  193.7 4.0 unpack.1
  199.2 35.2 %attend.2 = (f32[512,512]{1,0:T(8,128)S(1)}, f32[4,8,128]{2,1,0:T(8,128)S(1)}) custom-call(s32[9]{0:T(128)S(1)} %pad_add_fusion.places, bf16[512,1024]{1,0:T(8,128)(2,1)S(1)} %bitcast.168, bf16[8192,64]{1,0:T(8,128)(2,1)S(1)} %get-tuple-element.138.keys_ref.refs_4_, bf16[72,8192]{1,0:T(8,128)(2,1)S(1)} %get-tuple-element.139.values_ref), custom_call_target="tpu_custom_call" | custom-call | flops 17179869184 | bytes 8388608 | tf_op jit(solution)/shard_map/attend/pallas_call | solution.py:145
  244.3 31.3 %attend.3 = (f32[512,512]{1,0:T(8,128)S(1)}, f32[4,8,128]{2,1,0:T(8,128)S(1)}) custom-call(s32[9]{0:T(128)S(1)} %pad_add_fusion.places, bf16[512,1024]{1,0:T(8,128)(2,1)S(1)} %bitcast.169, bf16[8192,64]{1,0:T(8,128)(2,1)S(1)} %get-tuple-element.138.keys_ref.refs_4_, bf16[72,8192]{1,0:T(8,128)(2,1)S(1)} %get-tuple-element.139.values_ref), custom_call_target="tpu_custom_call" | custom-call | flops 17179869184 | bytes 8388608 | tf_op jit(solution)/shard_map/attend/pallas_call | solution.py:145
  295.2 21.1 %collective-permute-done.22 = bf16[256,2048]{1,0:T(8,128)(2,1)S(1)} collective-permute-done((bf16[256,2048]{1,0:T(8,128)(2,1)S(1)}, bf16[256,2048]{1,0:T(8,128)(2,1)S(1)}, u32[]{:S(2)}, u32[]{:S(2)}) %collective-permute-start.22) | collective-permute-done | bytes 1048608 | tf_op jit(solution)/shard_map/ppermute | solution.py:426
  322.4 9.4 %collective-permute-done.26 = bf16[128,2048]{1,0:T(8,128)(2,1)S(1)} collective-permute-done((bf16[128,2048]{1,0:T(8,128)(2,1)S(1)}, bf16[128,2048]{1,0:T(8,128)(2,1)S(1)}, u32[]{:S(2)}, u32[]{:S(2)}) %collective-permute-start.26) | collective-permute-done | bytes 524320 | tf_op jit(solution)/shard_map/ppermute | solution.py:426
  338.5 12.1 %fusion.75 = f32[2048,768]{1,0:T(8,128)} fusion(bf16[2048,2048]{1,0:T(8,128)(2,1)} %copy-done.95, bf16[2048,768]{1,0:T(8,128)(2,1)} %all-gather.9.cloned.1.call-done), kind=kOutput, calls=%fused_computation.270 | convolution fusion | flops 6442450944 | bytes 17825792 | tf_op jit(solution)/shard_map/dot_general | solution.py:695
  350.6 11.8 %fusion.76 = f32[2048,768]{1,0:T(8,128)} fusion(bf16[2048,2048]{1,0:T(8,128)(2,1)} %constant_dynamic-update-slice_fusion.4, bf16[2048,768]{1,0:T(8,128)(2,1)} %all-gather.13.cloned.1.call-done), kind=kOutput, calls=%fused_computation.271 | convolution fusion | flops 6442450944 | bytes 17825792 | tf_op jit(solution)/shard_map/dot_general | solution.py:690
  362.4 18.5 %all-gather.11.cloned.1.call-done = bf16[2048,768]{1,0:T(8,128)(2,1)} async-done(((bf16[512,768]{1,0:T(8,128)(2,1)}), bf16[2048,768]{1,0:T(8,128)(2,1)}) %all-gather.11.cloned.1.call-update) | async-done | bytes 3145744 | tf_op jit(solution)/shard_map/all_gather | solution.py:588
  380.9 16.6 %select_convert_fusion = (bf16[2048,768]{1,0:T(8,128)(2,1)}, bf16[2048,768]{1,0:T(8,128)(2,1)S(1)}, bf16[2048,768]{1,0:T(8,128)(2,1)}) fusion(pred[768]{0:T(1024)(128)(4,1)S(1)} %iota_compare_fusion, f32[2048,768]{1,0:T(8,128)} %fusion.76, f32[2048,768]{1,0:T(8,128)} %fusion.75, bf16[2048,2048]{1,0:T(8,128)(2,1)} %constant_dynamic-update-slice_fusion.4, ...), kind=kOutput, calls=%fused_computation.6 | convolution fusion | flops 6470762496 | bytes 33555200 | tf_op jit(solution)/shard_map/dot_general | solution.py:691
  397.5 9.6 %fusion.77 = f32[2048,2048]{1,0:T(8,128)} fusion(bf16[2048,768]{1,0:T(8,128)(2,1)S(1)} %get-tuple-element.163, bf16[2048,768]{1,0:T(8,128)(2,1)S(1)} %copy-done.111), kind=kOutput, calls=%fused_computation.272 | convolution fusion | flops 6442450944 | bytes 23068672 | tf_op jit(solution)/shard_map/dot_general | solution.py:23
  407.1 14.1 %add_convert_fusion = bf16[2048,2048]{1,0:T(8,128)(2,1)} fusion(f32[2048,2048]{1,0:T(8,128)} %fusion.77, bf16[2048,768]{1,0:T(8,128)(2,1)} %get-tuple-element.164, bf16[2048,768]{1,0:T(8,128)(2,1)} %all-gather.11.cloned.1.call-done), kind=kOutput, calls=%fused_computation | convolution fusion | flops 6450839552 | bytes 31457280 | tf_op jit(solution)/shard_map/dot_general | solution.py:23
  421.2 8.2 convolution_convert_fusion.3
  429.5 4.1 fusion.68
  434.9 7.4 convolution_convert_fusion
  445.8 10.5 %convolution_convert_fusion.2 = bf16[2048,768]{1,0:T(8,128)(2,1)} fusion(bf16[2048,2048]{1,0:T(8,128)(2,1)} %constant_dynamic-update-slice_fusion.4, bf16[2048,768]{1,0:T(8,128)(2,1)S(1)} %copy-done.113), kind=kOutput, calls=%fused_computation.16 | convolution fusion | flops 6444023808 | bytes 14680064 | tf_op jit(solution)/shard_map/dot_general | solution.py:23
  456.3 4.1 convert_add_fusion.8
  463.6 3.9 convert_add_fusion.3
  468.0 8.1 collective-permute-done.39
  480.6 10.9 %convolution_convert_fusion.1 = bf16[2048,768]{1,0:T(8,128)(2,1)} fusion(bf16[2048,2048]{1,0:T(8,128)(2,1)} %constant_dynamic-update-slice_fusion.4, bf16[2048,768]{1,0:T(8,128)(2,1)S(1)} %copy-done.114), kind=kOutput, calls=%fused_computation.15 | convolution fusion | flops 6444023808 | bytes 14680064 | tf_op jit(solution)/shard_map/dot_general | solution.py:23
  492.6 6.2 convert_add_fusion.4
  498.7 4.5 collective-permute-done.40
  507.9 5.2 fusion.67
  527.6 50.9 %attend_back.2 = (f32[512,512]{1,0:T(8,128)}, f32[8192,64]{1,0:T(8,128)}, f32[8192,64]{1,0:T(8,128)}) custom-call(s32[9]{0:T(128)} %copy-done.23, bf16[512,1024]{1,0:T(8,128)(2,1)} %bitcast.170, bf16[512,512]{1,0:T(8,128)(2,1)} %convolution_convert_fusion.9.refs_1_, f32[512,512]{1,0:T(8,128)} %copy-done.6, f32[4,8,128]{2,1,0:T(8,128)} %copy-done.28, ...), custom_call_target="tpu_custom_call" | custom-call | flops 42949672960 | bytes 16777216 | tf_op jit(solution)/shard_map/attend_back/pallas_call | solution.py:265
  596.8 6.7 collective-permute-start.53
  605.6 59.7 %attend_back.3 = (f32[512,512]{1,0:T(8,128)}, bf16[8,128,1024]{2,1,0:T(8,128)(2,1)}) custom-call(s32[9]{0:T(128)} %copy-done.23, bf16[512,1024]{1,0:T(8,128)(2,1)} %bitcast.171, bf16[512,512]{1,0:T(8,128)(2,1)} %convolution_convert_fusion.8.refs_1_, f32[512,512]{1,0:T(8,128)} %copy-done.4, f32[4,8,128]{2,1,0:T(8,128)} %copy-done.27, ...), custom_call_target="tpu_custom_call" | custom-call | flops 42949672960 | bytes 16777216 | tf_op jit(solution)/shard_map/attend_back/pallas_call | solution.py:265
  691.0 3.3 fusion.14
  697.1 3.3 fusion.16
  700.5 13.0 %collective-permute-done.58 = bf16[256,512]{1,0:T(8,128)(2,1)S(1)} collective-permute-done((bf16[256,512]{1,0:T(8,128)(2,1)S(1)}, bf16[256,512]{1,0:T(8,128)(2,1)S(1)}, u32[]{:S(2)}, u32[]{:S(2)}) %collective-permute-start.58) | collective-permute-done | bytes 262176 | tf_op jit(solution)/shard_map/ppermute | solution.py:426
  717.6 9.1 %collective-permute-done.56 = bf16[4,256,512]{2,1,0:T(8,128)(2,1)S(1)} collective-permute-done((bf16[4,256,512]{2,1,0:T(8,128)(2,1)S(1)}, bf16[4,256,512]{2,1,0:T(8,128)(2,1)S(1)}, u32[]{:S(2)}, u32[]{:S(2)}) %collective-permute-start.56) | collective-permute-done | bytes 1048608 | tf_op jit(solution)/shard_map/ppermute | solution.py:458
  729.7 14.5 %reduce-scatter.13.cloned.1.call-done = bf16[1,128,1024]{2,1,0:T(8,128)(2,1)} async-done(((bf16[8,128,1024]{2,1,0:T(8,128)(2,1)}), bf16[1,128,1024]{2,1,0:T(8,128)(2,1)}) %reduce-scatter.13.cloned.1.call-update) | async-done | bytes 262160 | tf_op jit(solution)/shard_map/reduce_scatter | solution.py:753
  755.0 3.3 add_convert_fusion.1
  767.8 4.7 collective-permute-done.72
  772.5 12.9 %collective-permute-done.71 = bf16[256,2048]{1,0:T(8,128)(2,1)} collective-permute-done((bf16[256,2048]{1,0:T(8,128)(2,1)}, bf16[256,2048]{1,0:T(8,128)(2,1)}, u32[]{:S(2)}, u32[]{:S(2)}) %collective-permute-start.71) | collective-permute-done | bytes 1048608 | tf_op jit(solution)/shard_map/ppermute | solution.py:426
  809.4 4.8 widen_half.2
  814.2 3.4 widen_half.3
  817.7 4.5 collective-permute-done.74
  822.1 14.1 %collective-permute-done.75 = bf16[256,128]{1,0:T(8,128)(2,1)} collective-permute-done((bf16[256,128]{1,0:T(8,128)(2,1)}, bf16[256,128]{1,0:T(8,128)(2,1)}, u32[]{:S(2)}, u32[]{:S(2)}) %collective-permute-start.75) | collective-permute-done | bytes 65568 | tf_op jit(solution)/shard_map/ppermute | solution.py:454
  850.7 3.8 collective-permute-done.85.refs_2_
  (608 shorter events, 245.7 us)
Async XLA Ops:
  7.2 107.6 %all-gather.7.cloned.1.call-start = ((), (), s32[]{:S(2)}) async-start(), calls=%async_computation.6 | async-start | bytes 5898240 | tf_op jit(solution)/shard_map/all_gather | solution.py:575
  11.9 177.6 %all-gather.15.cloned.1.call-start = ((), (), s32[]{:S(2)}) async-start(), calls=%async_computation.16 | async-start | bytes 2359296 | tf_op jit(solution)/shard_map/all_gather | solution.py:653
  125.5 213.0 %all-gather.9.cloned.1.call-start = ((), (), s32[]{:S(2)}) async-start(), calls=%async_computation.7 | async-start | bytes 3932160 | tf_op jit(solution)/shard_map/all_gather | solution.py:588
  129.7 32.9 %collective-permute-start.8 = (bf16[256,768]{1,0:T(8,128)(2,1)S(1)}, bf16[256,768]{1,0:T(8,128)(2,1)S(1)}, u32[]{:S(2)}, u32[]{:S(2)}) collective-permute-start(bf16[256,768]{1,0:T(8,128)(2,1)S(1)} %constant_dynamic-slice_fusion.6), channel_id=1, source_target_pairs={{0,1},{1,0},{2,3},{3,2},{4,5},{5,4},{6,7},{7,6},{8,9},{9,8},{10,11... | collective-permute-start | bytes 1179656 | tf_op jit(solution)/shard_map/ppermute | solution.py:458
  132.3 42.0 %collective-permute-start.7 = (bf16[256,768]{1,0:T(8,128)(2,1)S(1)}, bf16[256,768]{1,0:T(8,128)(2,1)}, u32[]{:S(2)}, u32[]{:S(2)}) collective-permute-start(bf16[256,768]{1,0:T(8,128)(2,1)S(1)} %constant_dynamic-slice_fusion.7), channel_id=1, source_target_pairs={{0,1},{1,0},{2,3},{3,2},{4,5},{5,4},{6,7},{7,6},{8,9},{9,8},{10,11... | collective-permute-start | bytes 1179656 | tf_op jit(solution)/shard_map/ppermute | solution.py:458
  133.9 48.2 %collective-permute-start.10 = (bf16[128,2048]{1,0:T(8,128)(2,1)}, bf16[128,2048]{1,0:T(8,128)(2,1)}, u32[]{:S(2)}, u32[]{:S(2)}) collective-permute-start(bf16[128,2048]{1,0:T(8,128)(2,1)} %get-tuple-element.321), channel_id=1, source_target_pairs={{0,7},{1,6},{2,5},{3,4},{4,3},{5,2},{6,1},{7,0},{8,15},{9,14},{10,... | collective-permute-start | bytes 1572872 | tf_op jit(solution)/shard_map/ppermute | solution.py:569
  137.5 41.7 %collective-permute-start.13 = (bf16[512,512]{1,0:T(8,128)(2,1)}, bf16[512,512]{1,0:T(8,128)(2,1)}, u32[]{:S(2)}, u32[]{:S(2)}) collective-permute-start(bf16[512,512]{1,0:T(8,128)(2,1)} %get-tuple-element.300), channel_id=1, source_target_pairs={{0,24},{8,16},{16,8},{24,0},{1,25},{9,17},{17,9},{25,1},{2,26},{10... | collective-permute-start | bytes 1572872 | tf_op jit(solution)/shard_map/ppermute | solution.py:494
  151.9 27.2 %collective-permute-start.12 = (bf16[512,512]{1,0:T(8,128)(2,1)}, bf16[512,512]{1,0:T(8,128)(2,1)}, u32[]{:S(2)}, u32[]{:S(2)}) collective-permute-start(bf16[512,512]{1,0:T(8,128)(2,1)} %get-tuple-element.301), channel_id=1, source_target_pairs={{0,16},{8,24},{16,0},{24,8},{1,17},{9,25},{17,1},{25,9},{2,18},{10... | collective-permute-start | bytes 1572872 | tf_op jit(solution)/shard_map/ppermute | solution.py:426
  189.6 161.0 %all-gather.13.cloned.1.call-start = ((), (), s32[]{:S(2)}) async-start(), calls=%async_computation.9 | async-start | bytes 3932160 | tf_op jit(solution)/shard_map/all_gather | solution.py:588
  189.8 46.3 %collective-permute-start.15 = (bf16[256,2048]{1,0:T(8,128)(2,1)S(1)}, bf16[256,2048]{1,0:T(8,128)(2,1)}, u32[]{:S(2)}, u32[]{:S(2)}) collective-permute-start(bf16[256,2048]{1,0:T(8,128)(2,1)S(1)} %pad_maximum_fusion.2), channel_id=1, source_target_pairs={{0,16},{8,24},{16,0},{24,8},{1,17},{9,25},{17,1},{25,9},{2,18},{10... | collective-permute-start | bytes 3145736 | tf_op jit(solution)/shard_map/ppermute | solution.py:426
  191.3 44.8 %collective-permute-start.14 = (bf16[256,2048]{1,0:T(8,128)(2,1)S(1)}, bf16[256,2048]{1,0:T(8,128)(2,1)}, u32[]{:S(2)}, u32[]{:S(2)}) collective-permute-start(bf16[256,2048]{1,0:T(8,128)(2,1)S(1)} %pad_maximum_fusion.2), channel_id=1, source_target_pairs={{0,1},{1,0},{2,3},{3,2},{4,5},{5,4},{6,7},{7,6},{8,9},{9,8},{10,11... | collective-permute-start | bytes 3145736 | tf_op jit(solution)/shard_map/ppermute | solution.py:458
  191.9 189.1 %all-gather.11.cloned.1.call-start = ((), (), s32[]{:S(2)}) async-start(), calls=%async_computation.8 | async-start | bytes 3932160 | tf_op jit(solution)/shard_map/all_gather | solution.py:588
  237.6 44.8 %collective-permute-start.29 = (bf16[256,2048]{1,0:T(8,128)(2,1)S(1)}, bf16[256,2048]{1,0:T(8,128)(2,1)}, u32[]{:S(2)}, u32[]{:S(2)}) collective-permute-start(bf16[256,2048]{1,0:T(8,128)(2,1)S(1)} %pad_maximum_fusion.2), channel_id=1, source_target_pairs={{0,8},{8,0},{16,24},{24,16},{1,9},{9,1},{17,25},{25,17},{2,10},{10... | collective-permute-start | bytes 3145736 | tf_op jit(solution)/shard_map/ppermute | solution.py:422
  240.3 35.4 %collective-permute-start.19 = (bf16[128,2048]{1,0:T(8,128)(2,1)S(1)}, bf16[128,2048]{1,0:T(8,128)(2,1)S(1)}, u32[]{:S(2)}, u32[]{:S(2)}) collective-permute-start(bf16[128,2048]{1,0:T(8,128)(2,1)S(1)} %slice.259), channel_id=1, source_target_pairs={{0,1},{1,0},{2,3},{3,2},{4,5},{5,4},{6,7},{7,6},{8,9},{9,8},{10,11... | collective-permute-start | bytes 1572872 | tf_op jit(solution)/shard_map/ppermute | solution.py:458
  241.8 33.9 %collective-permute-start.18 = (bf16[128,2048]{1,0:T(8,128)(2,1)S(1)}, bf16[128,2048]{1,0:T(8,128)(2,1)S(1)}, u32[]{:S(2)}, u32[]{:S(2)}) collective-permute-start(bf16[128,2048]{1,0:T(8,128)(2,1)S(1)} %slice.258), channel_id=1, source_target_pairs={{0,16},{8,24},{16,0},{24,8},{1,17},{9,25},{17,1},{25,9},{2,18},{10... | collective-permute-start | bytes 1572872 | tf_op jit(solution)/shard_map/ppermute | solution.py:426
  242.2 35.7 %collective-permute-start.17 = (bf16[256,2048]{1,0:T(8,128)(2,1)S(1)}, bf16[256,2048]{1,0:T(8,128)(2,1)S(1)}, u32[]{:S(2)}, u32[]{:S(2)}) collective-permute-start(bf16[256,2048]{1,0:T(8,128)(2,1)S(1)} %add_convert_fusion.8), channel_id=1, source_target_pairs={{0,16},{8,24},{16,0},{24,8},{1,17},{9,25},{17,1},{25,9},{2,18},{10... | collective-permute-start | bytes 3145736 | tf_op jit(solution)/shard_map/ppermute | solution.py:426
  281.6 231.6 %reduce-scatter.7.cloned.1.call-start = ((), (), s32[]{:S(2)}) async-start(), calls=%async_computation.10 | async-start | bytes 3932160 | tf_op jit(solution)/shard_map/reduce_scatter | solution.py:591
  289.7 26.6 %collective-permute-start.22 = (bf16[256,2048]{1,0:T(8,128)(2,1)S(1)}, bf16[256,2048]{1,0:T(8,128)(2,1)S(1)}, u32[]{:S(2)}, u32[]{:S(2)}) collective-permute-start(bf16[256,2048]{1,0:T(8,128)(2,1)S(1)} %get-tuple-element.263), channel_id=1, source_target_pairs={{0,16},{8,24},{16,0},{24,8},{1,17},{9,25},{17,1},{25,9},{2,18},{10... | collective-permute-start | bytes 3145736 | tf_op jit(solution)/shard_map/ppermute | solution.py:426
  292.7 26.8 %collective-permute-start.32 = (bf16[256,2048]{1,0:T(8,128)(2,1)S(1)}, bf16[256,2048]{1,0:T(8,128)(2,1)S(1)}, u32[]{:S(2)}, u32[]{:S(2)}) collective-permute-start(bf16[256,2048]{1,0:T(8,128)(2,1)S(1)} %pad_maximum_fusion.4), channel_id=1, source_target_pairs={{0,8},{8,0},{16,24},{24,16},{1,9},{9,1},{17,25},{25,17},{2,10},{10... | collective-permute-start | bytes 3145736 | tf_op jit(solution)/shard_map/ppermute | solution.py:422
  292.9 25.4 %collective-permute-start.24 = (bf16[256,2048]{1,0:T(8,128)(2,1)S(1)}, bf16[256,2048]{1,0:T(8,128)(2,1)S(1)}, u32[]{:S(2)}, u32[]{:S(2)}) collective-permute-start(bf16[256,2048]{1,0:T(8,128)(2,1)S(1)} %get-tuple-element.263), channel_id=1, source_target_pairs={{0,1},{1,0},{2,3},{3,2},{4,5},{5,4},{6,7},{7,6},{8,9},{9,8},{10,11... | collective-permute-start | bytes 3145736 | tf_op jit(solution)/shard_map/ppermute | solution.py:458
  293.6 26.1 %collective-permute-start.21 = (bf16[256,2048]{1,0:T(8,128)(2,1)S(1)}, bf16[256,2048]{1,0:T(8,128)(2,1)S(1)}, u32[]{:S(2)}, u32[]{:S(2)}) collective-permute-start(bf16[256,2048]{1,0:T(8,128)(2,1)S(1)} %get-tuple-element.263), channel_id=1, source_target_pairs={{0,8},{8,0},{16,24},{24,16},{1,9},{9,1},{17,25},{25,17},{2,10},{10... | collective-permute-start | bytes 3145736 | tf_op jit(solution)/shard_map/ppermute | solution.py:422
  429.4 149.2 %reduce-scatter.9.cloned.1.call-start = ((), (), s32[]{:S(2)}) async-start(), calls=%async_computation.11 | async-start | bytes 3932160 | tf_op jit(solution)/shard_map/reduce_scatter | solution.py:591
  433.6 65.1 %collective-permute-start.33 = (bf16[256,2048]{1,0:T(8,128)(2,1)}, bf16[256,2048]{1,0:T(8,128)(2,1)}, u32[]{:S(2)}, u32[]{:S(2)}) collective-permute-start(bf16[256,2048]{1,0:T(8,128)(2,1)} %get-tuple-element.276), channel_id=1, source_target_pairs={{0,8},{8,0},{16,24},{24,16},{1,9},{9,1},{17,25},{25,17},{2,10},{10... | collective-permute-start | bytes 3145736 | tf_op jit(solution)/shard_map/ppermute | solution.py:422
  467.5 24.1 %collective-permute-start.42 = (bf16[256,2048]{1,0:T(8,128)(2,1)}, bf16[256,2048]{1,0:T(8,128)(2,1)S(1)}, u32[]{:S(2)}, u32[]{:S(2)}) collective-permute-start(bf16[256,2048]{1,0:T(8,128)(2,1)} %get-tuple-element.271), channel_id=1, source_target_pairs={{0,8},{8,0},{16,24},{24,16},{1,9},{9,1},{17,25},{25,17},{2,10},{10... | collective-permute-start | bytes 3145736 | tf_op jit(solution)/shard_map/ppermute | solution.py:422
  477.3 25.9 %collective-permute-start.40 = (bf16[256,2048]{1,0:T(8,128)(2,1)}, bf16[256,2048]{1,0:T(8,128)(2,1)}, u32[]{:S(2)}, u32[]{:S(2)}) collective-permute-start(bf16[256,2048]{1,0:T(8,128)(2,1)} %pad_maximum_fusion.6), channel_id=1, source_target_pairs={{0,1},{1,0},{2,3},{3,2},{4,5},{5,4},{6,7},{7,6},{8,9},{9,8},{10,11... | collective-permute-start | bytes 3145736 | tf_op jit(solution)/shard_map/ppermute | solution.py:458
  479.2 25.6 %collective-permute-start.37 = (bf16[256,2048]{1,0:T(8,128)(2,1)}, bf16[256,2048]{1,0:T(8,128)(2,1)}, u32[]{:S(2)}, u32[]{:S(2)}) collective-permute-start(bf16[256,2048]{1,0:T(8,128)(2,1)} %pad_maximum_fusion.5), channel_id=1, source_target_pairs={{0,16},{8,24},{16,0},{24,8},{1,17},{9,25},{17,1},{25,9},{2,18},{10... | collective-permute-start | bytes 3145736 | tf_op jit(solution)/shard_map/ppermute | solution.py:426
  513.2 152.1 %reduce-scatter.11.cloned.1.call-start = ((), (), s32[]{:S(2)}) async-start(), calls=%async_computation.12 | async-start | bytes 3932160 | tf_op jit(solution)/shard_map/reduce_scatter | solution.py:591
  513.3 65.3 %collective-permute-start.46 = (bf16[256,2048]{1,0:T(8,128)(2,1)}, bf16[256,2048]{1,0:T(8,128)(2,1)}, u32[]{:S(2)}, u32[]{:S(2)}) collective-permute-start(bf16[256,2048]{1,0:T(8,128)(2,1)} %get-tuple-element.166), channel_id=1, source_target_pairs={{0,16},{8,24},{16,0},{24,8},{1,17},{9,25},{17,1},{25,9},{2,18},{10... | collective-permute-start | bytes 3145736 | tf_op jit(solution)/shard_map/ppermute | solution.py:426
  516.5 62.0 %collective-permute-start.49 = (bf16[256,768]{1,0:T(8,128)(2,1)}, bf16[256,768]{1,0:T(8,128)(2,1)S(1)}, u32[]{:S(2)}, u32[]{:S(2)}) collective-permute-start(bf16[256,768]{1,0:T(8,128)(2,1)} %dynamic-slice_bitcast_fusion.15), channel_id=1, source_target_pairs={{0,1},{1,0},{2,3},{3,2},{4,5},{5,4},{6,7},{7,6},{8,9},{9,8},{10,11... | collective-permute-start | bytes 1179656 | tf_op jit(solution)/shard_map/ppermute | solution.py:458
  522.1 56.5 %collective-permute-start.48 = (bf16[128,2048]{1,0:T(8,128)(2,1)}, bf16[128,2048]{1,0:T(8,128)(2,1)}, u32[]{:S(2)}, u32[]{:S(2)}) collective-permute-start(bf16[128,2048]{1,0:T(8,128)(2,1)} %get-tuple-element.316), channel_id=1, source_target_pairs={{0,1},{1,0},{2,3},{3,2},{4,5},{5,4},{6,7},{7,6},{8,9},{9,8},{10,11... | collective-permute-start | bytes 1572872 | tf_op jit(solution)/shard_map/ppermute | solution.py:458
  522.8 55.8 %collective-permute-start.47 = (bf16[128,2048]{1,0:T(8,128)(2,1)}, bf16[128,2048]{1,0:T(8,128)(2,1)}, u32[]{:S(2)}, u32[]{:S(2)}) collective-permute-start(bf16[128,2048]{1,0:T(8,128)(2,1)} %get-tuple-element.317), channel_id=1, source_target_pairs={{0,16},{8,24},{16,0},{24,8},{1,17},{9,25},{17,1},{25,9},{2,18},{10... | collective-permute-start | bytes 1572872 | tf_op jit(solution)/shard_map/ppermute | solution.py:426
  523.5 220.7 %reduce-scatter.13.cloned.1.call-start = ((), (), s32[]{:S(2)}) async-start(), calls=%async_computation.13 | async-start | bytes 2359296 | tf_op jit(solution)/shard_map/reduce_scatter | solution.py:753
  595.4 69.8 %collective-permute-start.54 = (bf16[256,768]{1,0:T(8,128)(2,1)S(1)}, bf16[256,768]{1,0:T(8,128)(2,1)S(1)}, u32[]{:S(2)}, u32[]{:S(2)}) collective-permute-start(bf16[256,768]{1,0:T(8,128)(2,1)S(1)} %dynamic-slice_bitcast_fusion.13), channel_id=1, source_target_pairs={{0,1},{1,0},{2,3},{3,2},{4,5},{5,4},{6,7},{7,6},{8,9},{9,8},{10,11... | collective-permute-start | bytes 1179656 | tf_op jit(solution)/shard_map/ppermute | solution.py:458
  596.8 68.6 %collective-permute-start.53 = (bf16[256,1408]{1,0:T(8,128)(2,1)S(1)}, bf16[256,1408]{1,0:T(8,128)(2,1)S(1)}, u32[]{:S(2)}, u32[]{:S(2)}) collective-permute-start(bf16[256,1408]{1,0:T(8,128)(2,1)S(1)} %pad_maximum_fusion.15.refs_0_), channel_id=1, source_target_pairs={{0,16},{8,24},{16,0},{24,8},{1,17},{9,25},{17,1},{25,9},{2,18},{10... | collective-permute-start | bytes 2162696 | tf_op jit(solution)/shard_map/ppermute | solution.py:426
  603.5 61.9 %collective-permute-start.51 = (bf16[256,2048]{1,0:T(8,128)(2,1)}, bf16[256,2048]{1,0:T(8,128)(2,1)}, u32[]{:S(2)}, u32[]{:S(2)}) collective-permute-start(bf16[256,2048]{1,0:T(8,128)(2,1)} %pad_maximum_fusion.7), channel_id=1, source_target_pairs={{0,16},{8,24},{16,0},{24,8},{1,17},{9,25},{17,1},{25,9},{2,18},{10... | collective-permute-start | bytes 3145736 | tf_op jit(solution)/shard_map/ppermute | solution.py:426
  603.5 61.8 %collective-permute-start.52 = (bf16[256,2048]{1,0:T(8,128)(2,1)}, bf16[256,2048]{1,0:T(8,128)(2,1)}, u32[]{:S(2)}, u32[]{:S(2)}) collective-permute-start(bf16[256,2048]{1,0:T(8,128)(2,1)} %pad_maximum_fusion.8), channel_id=1, source_target_pairs={{0,1},{1,0},{2,3},{3,2},{4,5},{5,4},{6,7},{7,6},{8,9},{9,8},{10,11... | collective-permute-start | bytes 3145736 | tf_op jit(solution)/shard_map/ppermute | solution.py:458
  604.3 61.1 %collective-permute-start.55 = (bf16[1,256,2048]{2,1,0:T(8,128)(2,1)}, bf16[1,256,2048]{2,1,0:T(8,128)(2,1)}, u32[]{:S(2)}, u32[]{:S(2)}) collective-permute-start(bf16[1,256,2048]{2,1,0:T(8,128)(2,1)} %dynamic-slice_bitcast_fusion.2), channel_id=1, source_target_pairs={{0,1},{1,0},{2,3},{3,2},{4,5},{5,4},{6,7},{7,6},{8,9},{9,8},{10,11... | collective-permute-start | bytes 3145736 | tf_op jit(solution)/shard_map/ppermute | solution.py:458
  666.8 46.7 %collective-permute-start.63 = (bf16[256,1408]{1,0:T(8,128)(2,1)S(1)}, bf16[256,1408]{1,0:T(8,128)(2,1)}, u32[]{:S(2)}, u32[]{:S(2)}) collective-permute-start(bf16[256,1408]{1,0:T(8,128)(2,1)S(1)} %pad_maximum_fusion.16.refs_0_), channel_id=1, source_target_pairs={{0,16},{8,24},{16,0},{24,8},{1,17},{9,25},{17,1},{25,9},{2,18},{10... | collective-permute-start | bytes 2162696 | tf_op jit(solution)/shard_map/ppermute | solution.py:426
  666.9 47.1 %collective-permute-start.62 = (bf16[256,1408]{1,0:T(8,128)(2,1)S(1)}, bf16[256,1408]{1,0:T(8,128)(2,1)}, u32[]{:S(2)}, u32[]{:S(2)}) collective-permute-start(bf16[256,1408]{1,0:T(8,128)(2,1)S(1)} %pad_maximum_fusion.16.refs_0_), channel_id=1, source_target_pairs={{0,8},{8,0},{16,24},{24,16},{1,9},{9,1},{17,25},{25,17},{2,10},{10... | collective-permute-start | bytes 2162696 | tf_op jit(solution)/shard_map/ppermute | solution.py:422
  672.7 164.5 %reduce-scatter.15.cloned.1.call-start = ((), (), s32[]{:S(2)}) async-start(), calls=%async_computation.14 | async-start | bytes 1310720 | tf_op jit(solution)/shard_map/reduce_scatter | solution.py:591
  689.4 24.8 %collective-permute-start.67 = (bf16[256,1408]{1,0:T(8,128)(2,1)S(1)}, bf16[256,1408]{1,0:T(8,128)(2,1)S(1)}, u32[]{:S(2)}, u32[]{:S(2)}) collective-permute-start(bf16[256,1408]{1,0:T(8,128)(2,1)S(1)} %pad_maximum_fusion.17.refs_0_), channel_id=1, source_target_pairs={{0,16},{8,24},{16,0},{24,8},{1,17},{9,25},{17,1},{25,9},{2,18},{10... | collective-permute-start | bytes 2162696 | tf_op jit(solution)/shard_map/ppermute | solution.py:426
  696.0 30.6 %collective-permute-start.56 = (bf16[4,256,512]{2,1,0:T(8,128)(2,1)S(1)}, bf16[4,256,512]{2,1,0:T(8,128)(2,1)S(1)}, u32[]{:S(2)}, u32[]{:S(2)}) collective-permute-start(bf16[4,256,512]{2,1,0:T(8,128)(2,1)S(1)} %get-tuple-element.294), channel_id=1, source_target_pairs={{0,1},{1,0},{2,3},{3,2},{4,5},{5,4},{6,7},{7,6},{8,9},{9,8},{10,11... | collective-permute-start | bytes 3145736 | tf_op jit(solution)/shard_map/ppermute | solution.py:458
  755.0 82.3 %reduce-scatter.17.cloned.1.call-start = ((), (), s32[]{:S(2)}) async-start(), calls=%async_computation.15 | async-start | bytes 1310720 | tf_op jit(solution)/shard_map/reduce_scatter | solution.py:591
  759.6 25.8 %collective-permute-start.71 = (bf16[256,2048]{1,0:T(8,128)(2,1)}, bf16[256,2048]{1,0:T(8,128)(2,1)}, u32[]{:S(2)}, u32[]{:S(2)}) collective-permute-start(bf16[256,2048]{1,0:T(8,128)(2,1)} %add_convert_fusion.5), channel_id=1, source_target_pairs={{0,16},{8,24},{16,0},{24,8},{1,17},{9,25},{17,1},{25,9},{2,18},{10... | collective-permute-start | bytes 3145736 | tf_op jit(solution)/shard_map/ppermute | solution.py:426
  793.0 44.1 %collective-permute-start.73 = (bf16[128,2048]{1,0:T(8,128)(2,1)}, bf16[128,2048]{1,0:T(8,128)(2,1)}, u32[]{:S(2)}, u32[]{:S(2)}) collective-permute-start(bf16[128,2048]{1,0:T(8,128)(2,1)} %slice.438), channel_id=1, source_target_pairs={{0,7},{1,6},{2,5},{3,4},{4,3},{5,2},{6,1},{7,0},{8,15},{9,14},{10,... | collective-permute-start | bytes 1572872 | tf_op jit(solution)/shard_map/ppermute | solution.py:569
  796.7 25.4 %collective-permute-start.74 = (bf16[256,128]{1,0:T(8,128)(2,1)}, bf16[256,128]{1,0:T(8,128)(2,1)S(1)}, u32[]{:S(2)}, u32[]{:S(2)}) collective-permute-start(bf16[256,128]{1,0:T(8,128)(2,1)} %get-tuple-element.329), channel_id=1, source_target_pairs={{0,2},{1,3},{2,4},{3,5},{4,6},{5,7},{6,0},{7,1},{8,10},{9,11},{10,... | collective-permute-start | bytes 196616 | tf_op jit(solution)/shard_map/ppermute | solution.py:454
  797.6 24.6 %collective-permute-start.76 = (bf16[256,128]{1,0:T(8,128)(2,1)}, bf16[256,128]{1,0:T(8,128)(2,1)S(1)}, u32[]{:S(2)}, u32[]{:S(2)}) collective-permute-start(bf16[256,128]{1,0:T(8,128)(2,1)} %get-tuple-element.330), channel_id=1, source_target_pairs={{0,6},{1,7},{2,0},{3,1},{4,2},{5,3},{6,4},{7,5},{8,14},{9,15},{10,... | collective-permute-start | bytes 196616 | tf_op jit(solution)/shard_map/ppermute | solution.py:454
  800.6 35.7 %collective-permute-start.75 = (bf16[256,128]{1,0:T(8,128)(2,1)}, bf16[256,128]{1,0:T(8,128)(2,1)}, u32[]{:S(2)}, u32[]{:S(2)}) collective-permute-start(bf16[256,128]{1,0:T(8,128)(2,1)} %get-tuple-element.331), channel_id=1, source_target_pairs={{0,4},{1,5},{2,6},{3,7},{4,0},{5,1},{6,2},{7,3},{8,12},{9,13},{10,... | collective-permute-start | bytes 196616 | tf_op jit(solution)/shard_map/ppermute | solution.py:454
  (176 other events, 2402.4 us)
Sparse Core Ops, SparseCore 0:
  12.0 102.7 all-gather.6
  125.6 63.8 all-gather.14
  191.7 61.4 all-gather.8
  255.1 62.2 all-gather.12
  318.8 62.0 all-gather.10
  429.5 58.8 reduce-scatter.6
  513.3 58.7 reduce-scatter.8
  574.4 60.2 reduce-scatter.10
  672.8 71.3 reduce-scatter.12
  755.1 26.0 reduce-scatter.14
  783.6 36.9 reduce-scatter.16

commit v4 on v3

--- a/solution.py
+++ b/solution.py
@@ -137,7 +137,7 @@
             lse_ref[0, h : h + 1, :] = lse[:, i * tile : (i + 1) * tile]
 
 
-def attend(places, queries, keys, values_ones, tile, base, tiles, key_block=512, per_chunk=8):
+def attend(places, queries, keys, values_ones, tile, base, tiles, key_block=1024, per_chunk=8):
     features, _ = queries.shape
     length = keys.shape[0]
     chunks = GROUP // per_chunk
@@ -251,7 +251,7 @@
 
 def attend_back(
     places, queries, grads, mixed, lse, keys, values, keys_t, tile, base, tiles, slab, before=None,
-    key_block=512, per_chunk=8,
+    key_block=1024, per_chunk=8,
 ):
     features, _ = queries.shape
     length = keys.shape[0]

time: 882 us -> 880 us (level)
  Pallas kernels: 197 us -> 188 us
  waiting for transfers between devices: 275 us -> 284 us
  transfers between devices with their start and end apart: 98 -> 98, of which waited for: 28 -> 28; matrix products, arithmetic and copies ran while one was open for 23% -> 23% of each run, Pallas kernels for 23% -> 21%
where the time goes in v4:
time: 880 us; the launch traced here: 866 us
  waiting for transfers between devices  284 us (32%)
  Pallas kernels  188 us (21%)
  matrix products  129 us (15%)
  other arithmetic  89 us (10%)
  local copies, waits for them, and re-layouts  88.6 us (10%)
  starting transfers between devices  71.1 us (8%)
  between operations  16.3 us (2%)
    pallas_call x2, Pallas kernels, attend_back(): pl.pallas_call(functools.partial(attend_back_kernel, key_block=key_block,...  109 us
    dot_general x19, matrix products, dot(): lax.dot_general(left, right, (((left_dim,), (right_dim,)), ((), ())), pre...  88.4 us
    ppermute x21, waiting for transfers between devices, from_chip(): lax.ppermute(value, 'seq', [(i, i ^ 2) for i in range(lax.axis_size('seq'...  87.2 us
    all_gather x1, waiting for transfers between devices, sc_gather(): return lax.all_gather(value, 'fsdp', axis=0, tiled=True)  61.3 us
    pallas_call x2, Pallas kernels, attend(): pl.pallas_call(functools.partial(attend_kernel, key_block=key_block, per_...  59 us
    ppermute x17, waiting for transfers between devices, from_pair(): lax.ppermute(value, 'fsdp', [(i, i ^ 1) for i in range(lax.axis_size('fsd...  51.6 us
    unnamed x271, local copies, waits for them, and re-layouts  46.1 us
    ppermute x21, starting transfers between devices, from_chip(): lax.ppermute(value, 'seq', [(i, i ^ 2) for i in range(lax.axis_size('seq'...  28.9 us
  transfers between devices with their start and end apart: 98, of which 28 were waited for; matrix products, arithmetic and copies ran while one was open for 23% of the time, Pallas kernels for 21%

profile of v4, /device:TPU:0, one launch (start us, length us, event | category | flops | bytes accessed | tf_op | source)
XLA Modules:
  0.0 866.0 jit_solution(7399415180407541719)
XLA Ops:
  12.2 6.0 collective-permute-start
  19.7 16.3 %collective-permute-done = bf16[128,2048]{1,0:T(8,128)(2,1)S(1)} collective-permute-done((bf16[128,2048]{1,0:T(8,128)(2,1)S(1)}, bf16[128,2048]{1,0:T(8,128)(2,1)S(1)}, u32[]{:S(2)}, u32[]{:S(2)}) %collective-permute-start) | collective-permute-done | bytes 524320 | tf_op jit(solution)/shard_map/ppermute | solution.py:569
  38.1 8.6 collective-permute-done.4
  49.7 3.8 maximum_convert_fusion
  53.5 61.3 %all-gather.7.cloned.1.call-done = bf16[2048,1280]{1,0:T(8,128)(2,1)} async-done(((bf16[256,1280]{1,0:T(8,128)(2,1)}), bf16[2048,1280]{1,0:T(8,128)(2,1)}) %all-gather.7.cloned.1.call-update) | async-done | bytes 5242896 | tf_op jit(solution)/shard_map/all_gather | solution.py:575
  116.7 4.2 fusion.1
  139.1 12.9 %collective-permute-done.9 = bf16[256,768]{1,0:T(8,128)(2,1)S(1)} collective-permute-done((bf16[256,768]{1,0:T(8,128)(2,1)S(1)}, bf16[256,768]{1,0:T(8,128)(2,1)S(1)}, u32[]{:S(2)}, u32[]{:S(2)}) %collective-permute-start.9) | collective-permute-done | bytes 393248 | tf_op jit(solution)/shard_map/ppermute | solution.py:458
  154.7 8.0 collective-permute-done.8
  164.7 9.5 %collective-permute-done.7 = bf16[256,768]{1,0:T(8,128)(2,1)} collective-permute-done((bf16[256,768]{1,0:T(8,128)(2,1)S(1)}, bf16[256,768]{1,0:T(8,128)(2,1)}, u32[]{:S(2)}, u32[]{:S(2)}) %collective-permute-start.7) | collective-permute-done | bytes 393248 | tf_op jit(solution)/shard_map/ppermute | solution.py:458
  183.2 6.3 all-gather.15.cloned.1.call-done
  193.7 4.0 unpack.1
  199.1 30.8 %attend.2 = (f32[512,512]{1,0:T(8,128)S(1)}, f32[4,8,128]{2,1,0:T(8,128)S(1)}) custom-call(s32[9]{0:T(128)S(1)} %pad_add_fusion.places, bf16[512,1024]{1,0:T(8,128)(2,1)S(1)} %bitcast.168, bf16[8192,64]{1,0:T(8,128)(2,1)S(1)} %get-tuple-element.138.keys_ref.refs_4_, bf16[72,8192]{1,0:T(8,128)(2,1)S(1)} %get-tuple-element.139.values_ref), custom_call_target="tpu_custom_call" | custom-call | flops 17179869184 | bytes 8388608 | tf_op jit(solution)/shard_map/attend/pallas_call | solution.py:145
  239.8 28.2 %attend.3 = (f32[512,512]{1,0:T(8,128)S(1)}, f32[4,8,128]{2,1,0:T(8,128)S(1)}) custom-call(s32[9]{0:T(128)S(1)} %pad_add_fusion.places, bf16[512,1024]{1,0:T(8,128)(2,1)S(1)} %bitcast.169, bf16[8192,64]{1,0:T(8,128)(2,1)S(1)} %get-tuple-element.138.keys_ref.refs_4_, bf16[72,8192]{1,0:T(8,128)(2,1)S(1)} %get-tuple-element.139.values_ref), custom_call_target="tpu_custom_call" | custom-call | flops 17179869184 | bytes 8388608 | tf_op jit(solution)/shard_map/attend/pallas_call | solution.py:145
  268.1 5.3 collective-permute-done.17
  288.4 22.3 %collective-permute-done.22 = bf16[256,2048]{1,0:T(8,128)(2,1)S(1)} collective-permute-done((bf16[256,2048]{1,0:T(8,128)(2,1)S(1)}, bf16[256,2048]{1,0:T(8,128)(2,1)S(1)}, u32[]{:S(2)}, u32[]{:S(2)}) %collective-permute-start.22) | collective-permute-done | bytes 1048608 | tf_op jit(solution)/shard_map/ppermute | solution.py:426
  316.9 8.3 collective-permute-done.26
  332.6 12.1 %fusion.75 = f32[2048,768]{1,0:T(8,128)} fusion(bf16[2048,2048]{1,0:T(8,128)(2,1)} %copy-done.95, bf16[2048,768]{1,0:T(8,128)(2,1)} %all-gather.9.cloned.1.call-done), kind=kOutput, calls=%fused_computation.270 | convolution fusion | flops 6442450944 | bytes 17825792 | tf_op jit(solution)/shard_map/dot_general | solution.py:695
  344.7 11.7 %fusion.76 = f32[2048,768]{1,0:T(8,128)} fusion(bf16[2048,2048]{1,0:T(8,128)(2,1)} %constant_dynamic-update-slice_fusion.4, bf16[2048,768]{1,0:T(8,128)(2,1)} %all-gather.13.cloned.1.call-done), kind=kOutput, calls=%fused_computation.271 | convolution fusion | flops 6442450944 | bytes 17825792 | tf_op jit(solution)/shard_map/dot_general | solution.py:690
  356.5 24.5 %all-gather.11.cloned.1.call-done = bf16[2048,768]{1,0:T(8,128)(2,1)} async-done(((bf16[512,768]{1,0:T(8,128)(2,1)}), bf16[2048,768]{1,0:T(8,128)(2,1)}) %all-gather.11.cloned.1.call-update) | async-done | bytes 3145744 | tf_op jit(solution)/shard_map/all_gather | solution.py:588
  380.9 16.6 %select_convert_fusion = (bf16[2048,768]{1,0:T(8,128)(2,1)}, bf16[2048,768]{1,0:T(8,128)(2,1)S(1)}, bf16[2048,768]{1,0:T(8,128)(2,1)}) fusion(pred[768]{0:T(1024)(128)(4,1)S(1)} %iota_compare_fusion, f32[2048,768]{1,0:T(8,128)} %fusion.76, f32[2048,768]{1,0:T(8,128)} %fusion.75, bf16[2048,2048]{1,0:T(8,128)(2,1)} %constant_dynamic-update-slice_fusion.4, ...), kind=kOutput, calls=%fused_computation.6 | convolution fusion | flops 6470762496 | bytes 33555200 | tf_op jit(solution)/shard_map/dot_general | solution.py:691
  397.5 9.6 %fusion.77 = f32[2048,2048]{1,0:T(8,128)} fusion(bf16[2048,768]{1,0:T(8,128)(2,1)S(1)} %get-tuple-element.163, bf16[2048,768]{1,0:T(8,128)(2,1)S(1)} %copy-done.111), kind=kOutput, calls=%fused_computation.272 | convolution fusion | flops 6442450944 | bytes 23068672 | tf_op jit(solution)/shard_map/dot_general | solution.py:23
  407.1 14.1 %add_convert_fusion = bf16[2048,2048]{1,0:T(8,128)(2,1)} fusion(f32[2048,2048]{1,0:T(8,128)} %fusion.77, bf16[2048,768]{1,0:T(8,128)(2,1)} %get-tuple-element.164, bf16[2048,768]{1,0:T(8,128)(2,1)} %all-gather.11.cloned.1.call-done), kind=kOutput, calls=%fused_computation | convolution fusion | flops 6450839552 | bytes 31457280 | tf_op jit(solution)/shard_map/dot_general | solution.py:23
  421.2 8.2 convolution_convert_fusion.3
  429.5 4.1 fusion.68
  435.0 7.6 convolution_convert_fusion
  446.0 10.5 %convolution_convert_fusion.2 = bf16[2048,768]{1,0:T(8,128)(2,1)} fusion(bf16[2048,2048]{1,0:T(8,128)(2,1)} %constant_dynamic-update-slice_fusion.4, bf16[2048,768]{1,0:T(8,128)(2,1)S(1)} %copy-done.113), kind=kOutput, calls=%fused_computation.16 | convolution fusion | flops 6444023808 | bytes 14680064 | tf_op jit(solution)/shard_map/dot_general | solution.py:23
  456.5 4.1 convert_add_fusion.8
  463.8 3.9 convert_add_fusion.3
  468.2 8.1 collective-permute-done.39
  480.9 10.6 %convolution_convert_fusion.1 = bf16[2048,768]{1,0:T(8,128)(2,1)} fusion(bf16[2048,2048]{1,0:T(8,128)(2,1)} %constant_dynamic-update-slice_fusion.4, bf16[2048,768]{1,0:T(8,128)(2,1)S(1)} %copy-done.114), kind=kOutput, calls=%fused_computation.15 | convolution fusion | flops 6444023808 | bytes 14680064 | tf_op jit(solution)/shard_map/dot_general | solution.py:23
  492.4 6.2 convert_add_fusion.4
  498.7 4.8 collective-permute-done.40
  508.1 5.2 fusion.67
  527.8 50.3 %attend_back.2 = (f32[512,512]{1,0:T(8,128)}, f32[8192,64]{1,0:T(8,128)}, f32[8192,64]{1,0:T(8,128)}) custom-call(s32[9]{0:T(128)} %copy-done.23, bf16[512,1024]{1,0:T(8,128)(2,1)} %bitcast.170, bf16[512,512]{1,0:T(8,128)(2,1)} %convolution_convert_fusion.9.refs_1_, f32[512,512]{1,0:T(8,128)} %copy-done.6, f32[4,8,128]{2,1,0:T(8,128)} %copy-done.28, ...), custom_call_target="tpu_custom_call" | custom-call | flops 42949672960 | bytes 16777216 | tf_op jit(solution)/shard_map/attend_back/pallas_call | solution.py:265
  596.4 6.7 collective-permute-start.53
  605.1 58.4 %attend_back.3 = (f32[512,512]{1,0:T(8,128)}, bf16[8,128,1024]{2,1,0:T(8,128)(2,1)}) custom-call(s32[9]{0:T(128)} %copy-done.23, bf16[512,1024]{1,0:T(8,128)(2,1)} %bitcast.171, bf16[512,512]{1,0:T(8,128)(2,1)} %convolution_convert_fusion.8.refs_1_, f32[512,512]{1,0:T(8,128)} %copy-done.4, f32[4,8,128]{2,1,0:T(8,128)} %copy-done.27, ...), custom_call_target="tpu_custom_call" | custom-call | flops 42949672960 | bytes 16777216 | tf_op jit(solution)/shard_map/attend_back/pallas_call | solution.py:265
  689.1 3.3 fusion.14
  695.2 3.3 fusion.16
  698.6 13.0 %collective-permute-done.58 = bf16[256,512]{1,0:T(8,128)(2,1)S(1)} collective-permute-done((bf16[256,512]{1,0:T(8,128)(2,1)S(1)}, bf16[256,512]{1,0:T(8,128)(2,1)S(1)}, u32[]{:S(2)}, u32[]{:S(2)}) %collective-permute-start.58) | collective-permute-done | bytes 262176 | tf_op jit(solution)/shard_map/ppermute | solution.py:426
  715.7 9.1 %collective-permute-done.56 = bf16[4,256,512]{2,1,0:T(8,128)(2,1)S(1)} collective-permute-done((bf16[4,256,512]{2,1,0:T(8,128)(2,1)S(1)}, bf16[4,256,512]{2,1,0:T(8,128)(2,1)S(1)}, u32[]{:S(2)}, u32[]{:S(2)}) %collective-permute-start.56) | collective-permute-done | bytes 1048608 | tf_op jit(solution)/shard_map/ppermute | solution.py:458
  727.8 14.5 %reduce-scatter.13.cloned.1.call-done = bf16[1,128,1024]{2,1,0:T(8,128)(2,1)} async-done(((bf16[8,128,1024]{2,1,0:T(8,128)(2,1)}), bf16[1,128,1024]{2,1,0:T(8,128)(2,1)}) %reduce-scatter.13.cloned.1.call-update) | async-done | bytes 262160 | tf_op jit(solution)/shard_map/reduce_scatter | solution.py:753
  765.9 4.6 collective-permute-done.72
  770.5 12.9 %collective-permute-done.71 = bf16[256,2048]{1,0:T(8,128)(2,1)} collective-permute-done((bf16[256,2048]{1,0:T(8,128)(2,1)}, bf16[256,2048]{1,0:T(8,128)(2,1)}, u32[]{:S(2)}, u32[]{:S(2)}) %collective-permute-start.71) | collective-permute-done | bytes 1048608 | tf_op jit(solution)/shard_map/ppermute | solution.py:426
  807.4 4.8 widen_half.2
  812.1 3.4 widen_half.3
  815.6 4.7 collective-permute-done.74
  820.3 14.1 %collective-permute-done.75 = bf16[256,128]{1,0:T(8,128)(2,1)} collective-permute-done((bf16[256,128]{1,0:T(8,128)(2,1)}, bf16[256,128]{1,0:T(8,128)(2,1)}, u32[]{:S(2)}, u32[]{:S(2)}) %collective-permute-start.75) | collective-permute-done | bytes 65568 | tf_op jit(solution)/shard_map/ppermute | solution.py:454
  848.8 3.8 collective-permute-done.85.refs_2_
  (608 shorter events, 245.0 us)
Async XLA Ops:
  7.2 107.6 %all-gather.7.cloned.1.call-start = ((), (), s32[]{:S(2)}) async-start(), calls=%async_computation.6 | async-start | bytes 5898240 | tf_op jit(solution)/shard_map/all_gather | solution.py:575
  11.9 177.7 %all-gather.15.cloned.1.call-start = ((), (), s32[]{:S(2)}) async-start(), calls=%async_computation.16 | async-start | bytes 2359296 | tf_op jit(solution)/shard_map/all_gather | solution.py:653
  12.2 23.9 %collective-permute-start = (bf16[128,2048]{1,0:T(8,128)(2,1)S(1)}, bf16[128,2048]{1,0:T(8,128)(2,1)S(1)}, u32[]{:S(2)}, u32[]{:S(2)}) collective-permute-start(bf16[128,2048]{1,0:T(8,128)(2,1)S(1)} %get-tuple-element.324), channel_id=1, source_target_pairs={{0,7},{1,6},{2,5},{3,4},{4,3},{5,2},{6,1},{7,0},{8,15},{9,14},{10,... | collective-permute-start | bytes 1572872 | tf_op jit(solution)/shard_map/ppermute | solution.py:569
  125.5 207.1 %all-gather.9.cloned.1.call-start = ((), (), s32[]{:S(2)}) async-start(), calls=%async_computation.7 | async-start | bytes 3932160 | tf_op jit(solution)/shard_map/all_gather | solution.py:588
  129.7 32.9 %collective-permute-start.8 = (bf16[256,768]{1,0:T(8,128)(2,1)S(1)}, bf16[256,768]{1,0:T(8,128)(2,1)S(1)}, u32[]{:S(2)}, u32[]{:S(2)}) collective-permute-start(bf16[256,768]{1,0:T(8,128)(2,1)S(1)} %constant_dynamic-slice_fusion.6), channel_id=1, source_target_pairs={{0,1},{1,0},{2,3},{3,2},{4,5},{5,4},{6,7},{7,6},{8,9},{9,8},{10,11... | collective-permute-start | bytes 1179656 | tf_op jit(solution)/shard_map/ppermute | solution.py:458
  132.3 42.0 %collective-permute-start.7 = (bf16[256,768]{1,0:T(8,128)(2,1)S(1)}, bf16[256,768]{1,0:T(8,128)(2,1)}, u32[]{:S(2)}, u32[]{:S(2)}) collective-permute-start(bf16[256,768]{1,0:T(8,128)(2,1)S(1)} %constant_dynamic-slice_fusion.7), channel_id=1, source_target_pairs={{0,1},{1,0},{2,3},{3,2},{4,5},{5,4},{6,7},{7,6},{8,9},{9,8},{10,11... | collective-permute-start | bytes 1179656 | tf_op jit(solution)/shard_map/ppermute | solution.py:458
  133.9 48.2 %collective-permute-start.10 = (bf16[128,2048]{1,0:T(8,128)(2,1)}, bf16[128,2048]{1,0:T(8,128)(2,1)}, u32[]{:S(2)}, u32[]{:S(2)}) collective-permute-start(bf16[128,2048]{1,0:T(8,128)(2,1)} %get-tuple-element.321), channel_id=1, source_target_pairs={{0,7},{1,6},{2,5},{3,4},{4,3},{5,2},{6,1},{7,0},{8,15},{9,14},{10,... | collective-permute-start | bytes 1572872 | tf_op jit(solution)/shard_map/ppermute | solution.py:569
  137.5 41.6 %collective-permute-start.13 = (bf16[512,512]{1,0:T(8,128)(2,1)}, bf16[512,512]{1,0:T(8,128)(2,1)}, u32[]{:S(2)}, u32[]{:S(2)}) collective-permute-start(bf16[512,512]{1,0:T(8,128)(2,1)} %get-tuple-element.300), channel_id=1, source_target_pairs={{0,24},{8,16},{16,8},{24,0},{1,25},{9,17},{17,9},{25,1},{2,26},{10... | collective-permute-start | bytes 1572872 | tf_op jit(solution)/shard_map/ppermute | solution.py:494
  152.0 27.2 %collective-permute-start.12 = (bf16[512,512]{1,0:T(8,128)(2,1)}, bf16[512,512]{1,0:T(8,128)(2,1)}, u32[]{:S(2)}, u32[]{:S(2)}) collective-permute-start(bf16[512,512]{1,0:T(8,128)(2,1)} %get-tuple-element.301), channel_id=1, source_target_pairs={{0,16},{8,24},{16,0},{24,8},{1,17},{9,25},{17,1},{25,9},{2,18},{10... | collective-permute-start | bytes 1572872 | tf_op jit(solution)/shard_map/ppermute | solution.py:426
  189.6 155.1 %all-gather.13.cloned.1.call-start = ((), (), s32[]{:S(2)}) async-start(), calls=%async_computation.9 | async-start | bytes 3932160 | tf_op jit(solution)/shard_map/all_gather | solution.py:588
  189.8 41.8 %collective-permute-start.15 = (bf16[256,2048]{1,0:T(8,128)(2,1)S(1)}, bf16[256,2048]{1,0:T(8,128)(2,1)}, u32[]{:S(2)}, u32[]{:S(2)}) collective-permute-start(bf16[256,2048]{1,0:T(8,128)(2,1)S(1)} %pad_maximum_fusion.2), channel_id=1, source_target_pairs={{0,16},{8,24},{16,0},{24,8},{1,17},{9,25},{17,1},{25,9},{2,18},{10... | collective-permute-start | bytes 3145736 | tf_op jit(solution)/shard_map/ppermute | solution.py:426
  191.3 40.3 %collective-permute-start.14 = (bf16[256,2048]{1,0:T(8,128)(2,1)S(1)}, bf16[256,2048]{1,0:T(8,128)(2,1)}, u32[]{:S(2)}, u32[]{:S(2)}) collective-permute-start(bf16[256,2048]{1,0:T(8,128)(2,1)S(1)} %pad_maximum_fusion.2), channel_id=1, source_target_pairs={{0,1},{1,0},{2,3},{3,2},{4,5},{5,4},{6,7},{7,6},{8,9},{9,8},{10,11... | collective-permute-start | bytes 3145736 | tf_op jit(solution)/shard_map/ppermute | solution.py:458
  191.9 189.0 %all-gather.11.cloned.1.call-start = ((), (), s32[]{:S(2)}) async-start(), calls=%async_computation.8 | async-start | bytes 3932160 | tf_op jit(solution)/shard_map/all_gather | solution.py:588
  233.1 44.8 %collective-permute-start.29 = (bf16[256,2048]{1,0:T(8,128)(2,1)S(1)}, bf16[256,2048]{1,0:T(8,128)(2,1)}, u32[]{:S(2)}, u32[]{:S(2)}) collective-permute-start(bf16[256,2048]{1,0:T(8,128)(2,1)S(1)} %pad_maximum_fusion.2), channel_id=1, source_target_pairs={{0,8},{8,0},{16,24},{24,16},{1,9},{9,1},{17,25},{25,17},{2,10},{10... | collective-permute-start | bytes 3145736 | tf_op jit(solution)/shard_map/ppermute | solution.py:422
  235.8 32.2 %collective-permute-start.19 = (bf16[128,2048]{1,0:T(8,128)(2,1)S(1)}, bf16[128,2048]{1,0:T(8,128)(2,1)S(1)}, u32[]{:S(2)}, u32[]{:S(2)}) collective-permute-start(bf16[128,2048]{1,0:T(8,128)(2,1)S(1)} %slice.259), channel_id=1, source_target_pairs={{0,1},{1,0},{2,3},{3,2},{4,5},{5,4},{6,7},{7,6},{8,9},{9,8},{10,11... | collective-permute-start | bytes 1572872 | tf_op jit(solution)/shard_map/ppermute | solution.py:458
  237.3 30.7 %collective-permute-start.18 = (bf16[128,2048]{1,0:T(8,128)(2,1)S(1)}, bf16[128,2048]{1,0:T(8,128)(2,1)S(1)}, u32[]{:S(2)}, u32[]{:S(2)}) collective-permute-start(bf16[128,2048]{1,0:T(8,128)(2,1)S(1)} %slice.258), channel_id=1, source_target_pairs={{0,16},{8,24},{16,0},{24,8},{1,17},{9,25},{17,1},{25,9},{2,18},{10... | collective-permute-start | bytes 1572872 | tf_op jit(solution)/shard_map/ppermute | solution.py:426
  237.7 35.7 %collective-permute-start.17 = (bf16[256,2048]{1,0:T(8,128)(2,1)S(1)}, bf16[256,2048]{1,0:T(8,128)(2,1)S(1)}, u32[]{:S(2)}, u32[]{:S(2)}) collective-permute-start(bf16[256,2048]{1,0:T(8,128)(2,1)S(1)} %add_convert_fusion.8), channel_id=1, source_target_pairs={{0,16},{8,24},{16,0},{24,8},{1,17},{9,25},{17,1},{25,9},{2,18},{10... | collective-permute-start | bytes 3145736 | tf_op jit(solution)/shard_map/ppermute | solution.py:426
  277.1 236.3 %reduce-scatter.7.cloned.1.call-start = ((), (), s32[]{:S(2)}) async-start(), calls=%async_computation.10 | async-start | bytes 3932160 | tf_op jit(solution)/shard_map/reduce_scatter | solution.py:591
  285.2 25.4 %collective-permute-start.22 = (bf16[256,2048]{1,0:T(8,128)(2,1)S(1)}, bf16[256,2048]{1,0:T(8,128)(2,1)S(1)}, u32[]{:S(2)}, u32[]{:S(2)}) collective-permute-start(bf16[256,2048]{1,0:T(8,128)(2,1)S(1)} %get-tuple-element.263), channel_id=1, source_target_pairs={{0,16},{8,24},{16,0},{24,8},{1,17},{9,25},{17,1},{25,9},{2,18},{10... | collective-permute-start | bytes 3145736 | tf_op jit(solution)/shard_map/ppermute | solution.py:426
  285.7 28.1 %collective-permute-start.32 = (bf16[256,2048]{1,0:T(8,128)(2,1)S(1)}, bf16[256,2048]{1,0:T(8,128)(2,1)S(1)}, u32[]{:S(2)}, u32[]{:S(2)}) collective-permute-start(bf16[256,2048]{1,0:T(8,128)(2,1)S(1)} %pad_maximum_fusion.4), channel_id=1, source_target_pairs={{0,8},{8,0},{16,24},{24,16},{1,9},{9,1},{17,25},{25,17},{2,10},{10... | collective-permute-start | bytes 3145736 | tf_op jit(solution)/shard_map/ppermute | solution.py:422
  286.1 25.2 %collective-permute-start.24 = (bf16[256,2048]{1,0:T(8,128)(2,1)S(1)}, bf16[256,2048]{1,0:T(8,128)(2,1)S(1)}, u32[]{:S(2)}, u32[]{:S(2)}) collective-permute-start(bf16[256,2048]{1,0:T(8,128)(2,1)S(1)} %get-tuple-element.263), channel_id=1, source_target_pairs={{0,1},{1,0},{2,3},{3,2},{4,5},{5,4},{6,7},{7,6},{8,9},{9,8},{10,11... | collective-permute-start | bytes 3145736 | tf_op jit(solution)/shard_map/ppermute | solution.py:458
  286.8 27.2 %collective-permute-start.21 = (bf16[256,2048]{1,0:T(8,128)(2,1)S(1)}, bf16[256,2048]{1,0:T(8,128)(2,1)S(1)}, u32[]{:S(2)}, u32[]{:S(2)}) collective-permute-start(bf16[256,2048]{1,0:T(8,128)(2,1)S(1)} %get-tuple-element.263), channel_id=1, source_target_pairs={{0,8},{8,0},{16,24},{24,16},{1,9},{9,1},{17,25},{25,17},{2,10},{10... | collective-permute-start | bytes 3145736 | tf_op jit(solution)/shard_map/ppermute | solution.py:422
  429.5 148.8 %reduce-scatter.9.cloned.1.call-start = ((), (), s32[]{:S(2)}) async-start(), calls=%async_computation.11 | async-start | bytes 3932160 | tf_op jit(solution)/shard_map/reduce_scatter | solution.py:591
  433.6 65.0 %collective-permute-start.33 = (bf16[256,2048]{1,0:T(8,128)(2,1)}, bf16[256,2048]{1,0:T(8,128)(2,1)}, u32[]{:S(2)}, u32[]{:S(2)}) collective-permute-start(bf16[256,2048]{1,0:T(8,128)(2,1)} %get-tuple-element.276), channel_id=1, source_target_pairs={{0,8},{8,0},{16,24},{24,16},{1,9},{9,1},{17,25},{25,17},{2,10},{10... | collective-permute-start | bytes 3145736 | tf_op jit(solution)/shard_map/ppermute | solution.py:422
  477.5 25.9 %collective-permute-start.40 = (bf16[256,2048]{1,0:T(8,128)(2,1)}, bf16[256,2048]{1,0:T(8,128)(2,1)}, u32[]{:S(2)}, u32[]{:S(2)}) collective-permute-start(bf16[256,2048]{1,0:T(8,128)(2,1)} %pad_maximum_fusion.6), channel_id=1, source_target_pairs={{0,1},{1,0},{2,3},{3,2},{4,5},{5,4},{6,7},{7,6},{8,9},{9,8},{10,11... | collective-permute-start | bytes 3145736 | tf_op jit(solution)/shard_map/ppermute | solution.py:458
  479.4 25.6 %collective-permute-start.37 = (bf16[256,2048]{1,0:T(8,128)(2,1)}, bf16[256,2048]{1,0:T(8,128)(2,1)}, u32[]{:S(2)}, u32[]{:S(2)}) collective-permute-start(bf16[256,2048]{1,0:T(8,128)(2,1)} %pad_maximum_fusion.5), channel_id=1, source_target_pairs={{0,16},{8,24},{16,0},{24,8},{1,17},{9,25},{17,1},{25,9},{2,18},{10... | collective-permute-start | bytes 3145736 | tf_op jit(solution)/shard_map/ppermute | solution.py:426
  513.4 150.2 %reduce-scatter.11.cloned.1.call-start = ((), (), s32[]{:S(2)}) async-start(), calls=%async_computation.12 | async-start | bytes 3932160 | tf_op jit(solution)/shard_map/reduce_scatter | solution.py:591
  513.6 64.7 %collective-permute-start.46 = (bf16[256,2048]{1,0:T(8,128)(2,1)}, bf16[256,2048]{1,0:T(8,128)(2,1)}, u32[]{:S(2)}, u32[]{:S(2)}) collective-permute-start(bf16[256,2048]{1,0:T(8,128)(2,1)} %get-tuple-element.166), channel_id=1, source_target_pairs={{0,16},{8,24},{16,0},{24,8},{1,17},{9,25},{17,1},{25,9},{2,18},{10... | collective-permute-start | bytes 3145736 | tf_op jit(solution)/shard_map/ppermute | solution.py:426
  516.8 61.3 %collective-permute-start.49 = (bf16[256,768]{1,0:T(8,128)(2,1)}, bf16[256,768]{1,0:T(8,128)(2,1)S(1)}, u32[]{:S(2)}, u32[]{:S(2)}) collective-permute-start(bf16[256,768]{1,0:T(8,128)(2,1)} %dynamic-slice_bitcast_fusion.15), channel_id=1, source_target_pairs={{0,1},{1,0},{2,3},{3,2},{4,5},{5,4},{6,7},{7,6},{8,9},{9,8},{10,11... | collective-permute-start | bytes 1179656 | tf_op jit(solution)/shard_map/ppermute | solution.py:458
  522.3 55.9 %collective-permute-start.48 = (bf16[128,2048]{1,0:T(8,128)(2,1)}, bf16[128,2048]{1,0:T(8,128)(2,1)}, u32[]{:S(2)}, u32[]{:S(2)}) collective-permute-start(bf16[128,2048]{1,0:T(8,128)(2,1)} %get-tuple-element.316), channel_id=1, source_target_pairs={{0,1},{1,0},{2,3},{3,2},{4,5},{5,4},{6,7},{7,6},{8,9},{9,8},{10,11... | collective-permute-start | bytes 1572872 | tf_op jit(solution)/shard_map/ppermute | solution.py:458
  523.1 55.1 %collective-permute-start.47 = (bf16[128,2048]{1,0:T(8,128)(2,1)}, bf16[128,2048]{1,0:T(8,128)(2,1)}, u32[]{:S(2)}, u32[]{:S(2)}) collective-permute-start(bf16[128,2048]{1,0:T(8,128)(2,1)} %get-tuple-element.317), channel_id=1, source_target_pairs={{0,16},{8,24},{16,0},{24,8},{1,17},{9,25},{17,1},{25,9},{2,18},{10... | collective-permute-start | bytes 1572872 | tf_op jit(solution)/shard_map/ppermute | solution.py:426
  523.7 218.6 %reduce-scatter.13.cloned.1.call-start = ((), (), s32[]{:S(2)}) async-start(), calls=%async_computation.13 | async-start | bytes 2359296 | tf_op jit(solution)/shard_map/reduce_scatter | solution.py:753
  595.0 68.5 %collective-permute-start.54 = (bf16[256,768]{1,0:T(8,128)(2,1)S(1)}, bf16[256,768]{1,0:T(8,128)(2,1)S(1)}, u32[]{:S(2)}, u32[]{:S(2)}) collective-permute-start(bf16[256,768]{1,0:T(8,128)(2,1)S(1)} %dynamic-slice_bitcast_fusion.13), channel_id=1, source_target_pairs={{0,1},{1,0},{2,3},{3,2},{4,5},{5,4},{6,7},{7,6},{8,9},{9,8},{10,11... | collective-permute-start | bytes 1179656 | tf_op jit(solution)/shard_map/ppermute | solution.py:458
  596.4 67.3 %collective-permute-start.53 = (bf16[256,1408]{1,0:T(8,128)(2,1)S(1)}, bf16[256,1408]{1,0:T(8,128)(2,1)S(1)}, u32[]{:S(2)}, u32[]{:S(2)}) collective-permute-start(bf16[256,1408]{1,0:T(8,128)(2,1)S(1)} %pad_maximum_fusion.15.refs_0_), channel_id=1, source_target_pairs={{0,16},{8,24},{16,0},{24,8},{1,17},{9,25},{17,1},{25,9},{2,18},{10... | collective-permute-start | bytes 2162696 | tf_op jit(solution)/shard_map/ppermute | solution.py:426
  603.0 60.6 %collective-permute-start.51 = (bf16[256,2048]{1,0:T(8,128)(2,1)}, bf16[256,2048]{1,0:T(8,128)(2,1)}, u32[]{:S(2)}, u32[]{:S(2)}) collective-permute-start(bf16[256,2048]{1,0:T(8,128)(2,1)} %pad_maximum_fusion.7), channel_id=1, source_target_pairs={{0,16},{8,24},{16,0},{24,8},{1,17},{9,25},{17,1},{25,9},{2,18},{10... | collective-permute-start | bytes 3145736 | tf_op jit(solution)/shard_map/ppermute | solution.py:426
  603.1 60.6 %collective-permute-start.52 = (bf16[256,2048]{1,0:T(8,128)(2,1)}, bf16[256,2048]{1,0:T(8,128)(2,1)}, u32[]{:S(2)}, u32[]{:S(2)}) collective-permute-start(bf16[256,2048]{1,0:T(8,128)(2,1)} %pad_maximum_fusion.8), channel_id=1, source_target_pairs={{0,1},{1,0},{2,3},{3,2},{4,5},{5,4},{6,7},{7,6},{8,9},{9,8},{10,11... | collective-permute-start | bytes 3145736 | tf_op jit(solution)/shard_map/ppermute | solution.py:458
  603.8 59.8 %collective-permute-start.55 = (bf16[1,256,2048]{2,1,0:T(8,128)(2,1)}, bf16[1,256,2048]{2,1,0:T(8,128)(2,1)}, u32[]{:S(2)}, u32[]{:S(2)}) collective-permute-start(bf16[1,256,2048]{2,1,0:T(8,128)(2,1)} %dynamic-slice_bitcast_fusion.2), channel_id=1, source_target_pairs={{0,1},{1,0},{2,3},{3,2},{4,5},{5,4},{6,7},{7,6},{8,9},{9,8},{10,11... | collective-permute-start | bytes 3145736 | tf_op jit(solution)/shard_map/ppermute | solution.py:458
  665.1 46.5 %collective-permute-start.63 = (bf16[256,1408]{1,0:T(8,128)(2,1)S(1)}, bf16[256,1408]{1,0:T(8,128)(2,1)}, u32[]{:S(2)}, u32[]{:S(2)}) collective-permute-start(bf16[256,1408]{1,0:T(8,128)(2,1)S(1)} %pad_maximum_fusion.16.refs_0_), channel_id=1, source_target_pairs={{0,16},{8,24},{16,0},{24,8},{1,17},{9,25},{17,1},{25,9},{2,18},{10... | collective-permute-start | bytes 2162696 | tf_op jit(solution)/shard_map/ppermute | solution.py:426
  665.2 46.9 %collective-permute-start.62 = (bf16[256,1408]{1,0:T(8,128)(2,1)S(1)}, bf16[256,1408]{1,0:T(8,128)(2,1)}, u32[]{:S(2)}, u32[]{:S(2)}) collective-permute-start(bf16[256,1408]{1,0:T(8,128)(2,1)S(1)} %pad_maximum_fusion.16.refs_0_), channel_id=1, source_target_pairs={{0,8},{8,0},{16,24},{24,16},{1,9},{9,1},{17,25},{25,17},{2,10},{10... | collective-permute-start | bytes 2162696 | tf_op jit(solution)/shard_map/ppermute | solution.py:422
  671.0 164.3 %reduce-scatter.15.cloned.1.call-start = ((), (), s32[]{:S(2)}) async-start(), calls=%async_computation.14 | async-start | bytes 1310720 | tf_op jit(solution)/shard_map/reduce_scatter | solution.py:591
  687.4 24.8 %collective-permute-start.67 = (bf16[256,1408]{1,0:T(8,128)(2,1)S(1)}, bf16[256,1408]{1,0:T(8,128)(2,1)S(1)}, u32[]{:S(2)}, u32[]{:S(2)}) collective-permute-start(bf16[256,1408]{1,0:T(8,128)(2,1)S(1)} %pad_maximum_fusion.17.refs_0_), channel_id=1, source_target_pairs={{0,16},{8,24},{16,0},{24,8},{1,17},{9,25},{17,1},{25,9},{2,18},{10... | collective-permute-start | bytes 2162696 | tf_op jit(solution)/shard_map/ppermute | solution.py:426
  694.1 30.6 %collective-permute-start.56 = (bf16[4,256,512]{2,1,0:T(8,128)(2,1)S(1)}, bf16[4,256,512]{2,1,0:T(8,128)(2,1)S(1)}, u32[]{:S(2)}, u32[]{:S(2)}) collective-permute-start(bf16[4,256,512]{2,1,0:T(8,128)(2,1)S(1)} %get-tuple-element.294), channel_id=1, source_target_pairs={{0,1},{1,0},{2,3},{3,2},{4,5},{5,4},{6,7},{7,6},{8,9},{9,8},{10,11... | collective-permute-start | bytes 3145736 | tf_op jit(solution)/shard_map/ppermute | solution.py:458
  753.0 82.3 %reduce-scatter.17.cloned.1.call-start = ((), (), s32[]{:S(2)}) async-start(), calls=%async_computation.15 | async-start | bytes 1310720 | tf_op jit(solution)/shard_map/reduce_scatter | solution.py:591
  757.6 25.8 %collective-permute-start.71 = (bf16[256,2048]{1,0:T(8,128)(2,1)}, bf16[256,2048]{1,0:T(8,128)(2,1)}, u32[]{:S(2)}, u32[]{:S(2)}) collective-permute-start(bf16[256,2048]{1,0:T(8,128)(2,1)} %add_convert_fusion.5), channel_id=1, source_target_pairs={{0,16},{8,24},{16,0},{24,8},{1,17},{9,25},{17,1},{25,9},{2,18},{10... | collective-permute-start | bytes 3145736 | tf_op jit(solution)/shard_map/ppermute | solution.py:426
  791.1 44.2 %collective-permute-start.73 = (bf16[128,2048]{1,0:T(8,128)(2,1)}, bf16[128,2048]{1,0:T(8,128)(2,1)}, u32[]{:S(2)}, u32[]{:S(2)}) collective-permute-start(bf16[128,2048]{1,0:T(8,128)(2,1)} %slice.438), channel_id=1, source_target_pairs={{0,7},{1,6},{2,5},{3,4},{4,3},{5,2},{6,1},{7,0},{8,15},{9,14},{10,... | collective-permute-start | bytes 1572872 | tf_op jit(solution)/shard_map/ppermute | solution.py:569
  794.7 25.6 %collective-permute-start.74 = (bf16[256,128]{1,0:T(8,128)(2,1)}, bf16[256,128]{1,0:T(8,128)(2,1)S(1)}, u32[]{:S(2)}, u32[]{:S(2)}) collective-permute-start(bf16[256,128]{1,0:T(8,128)(2,1)} %get-tuple-element.329), channel_id=1, source_target_pairs={{0,2},{1,3},{2,4},{3,5},{4,6},{5,7},{6,0},{7,1},{8,10},{9,11},{10,... | collective-permute-start | bytes 196616 | tf_op jit(solution)/shard_map/ppermute | solution.py:454
  795.7 24.6 %collective-permute-start.76 = (bf16[256,128]{1,0:T(8,128)(2,1)}, bf16[256,128]{1,0:T(8,128)(2,1)S(1)}, u32[]{:S(2)}, u32[]{:S(2)}) collective-permute-start(bf16[256,128]{1,0:T(8,128)(2,1)} %get-tuple-element.330), channel_id=1, source_target_pairs={{0,6},{1,7},{2,0},{3,1},{4,2},{5,3},{6,4},{7,5},{8,14},{9,15},{10,... | collective-permute-start | bytes 196616 | tf_op jit(solution)/shard_map/ppermute | solution.py:454
  798.5 35.9 %collective-permute-start.75 = (bf16[256,128]{1,0:T(8,128)(2,1)}, bf16[256,128]{1,0:T(8,128)(2,1)}, u32[]{:S(2)}, u32[]{:S(2)}) collective-permute-start(bf16[256,128]{1,0:T(8,128)(2,1)} %get-tuple-element.331), channel_id=1, source_target_pairs={{0,4},{1,5},{2,6},{3,7},{4,0},{5,1},{6,2},{7,3},{8,12},{9,13},{10,... | collective-permute-start | bytes 196616 | tf_op jit(solution)/shard_map/ppermute | solution.py:454
  (176 other events, 2371.8 us)
Sparse Core Ops, SparseCore 0:
  12.0 102.7 all-gather.6
  125.6 63.8 all-gather.14
  191.7 61.3 all-gather.8
  255.1 62.1 all-gather.12
  318.8 62.1 all-gather.10
  429.6 58.8 reduce-scatter.6
  513.5 58.7 reduce-scatter.8
  574.7 60.2 reduce-scatter.10
  671.1 71.1 reduce-scatter.12
  753.1 26.1 reduce-scatter.14
  781.7 37.0 reduce-scatter.16
